TPU v7x, 128 devices: a whole 4x4x4 slice. The times are simulated.
128 devices in a mesh: space: 16 (over x, y), tm: 8 (over z, core).
Axes of the slice: x: 4, y: 4, z: 4, core: 2. Of those that a mesh axis runs over, the one named last changes fastest.
Arguments:
- fluxes: bfloat16 [32, 1024, 512], P('tm', 'space'), may hold values from -6 to 6
- footprints: bfloat16 [65536, 128, 128], P(('space', 'tm')), may hold values from -0.09375 to 0.09375
- block_coords: int32 [3, 65536], P(None, ('space', 'tm')), may hold values from 0 to 1535, as said below
- block_count: int32 [128], P(('space', 'tm')), may hold values from 128 to 512, as said below
- observed: float32 [196608], P('space'), may hold values from -6 to 6
- obs_weight: float32 [196608], P('space'), may hold values from 0.25 to 4
- time_cov: float32 [32, 32], replicated, as said below
- diffusivity: float32 [1024, 512], P('space'), may hold values from 0.04 to 0.24
Outputs:
- misfit: float32 [196608], P(('space', 'tm'))
- gradient: float32 [32, 1024, 512], P('tm', 'space')
Inputs may be any that keep to these rules, and one draw needn't show every extreme that they name: `block_coords`: row 0 lies in 0 to 3, row 1 in 0 to 255, row 2 in 0 to 1535; each row reaches its largest value. Slots at or past a device's live count still hold coordinates in range. `block_count`: some device has all 512 slots live. `time_cov`: Symmetric.
All inputs are finite; a program needn't handle non-finite values.
Results may differ from a plain program's by a relative error of at most 0.0029.
Values may be sent and summed in bfloat16 or wider, within the bound.
No kernel may reach another device: no remote copies, remote signals or barrier semaphores. Data moves between devices by JAX's collectives and lax.ppermute only.
A program may use at most 128 MiB of HBM per device.

v0:
```python
import jax
import jax.numpy as jnp
from jax import lax
from jax.sharding import PartitionSpec as P

SWEEPS = 4


def with_halo(array, sides, width):
    for axis, dim in sides:
        size, length = (lax.axis_size(axis), array.shape[dim])
        up = [(i, (i + 1) % size) for i in range(size - 1)]
        down = [(j, i) for i, j in up]
        last = lax.slice_in_dim(array, length - width, length, axis=dim)
        initial = lax.slice_in_dim(array, 0, width, axis=dim)
        before = lax.ppermute(last, axis, up)
        after = lax.ppermute(initial, axis, down)
        array = jnp.concatenate([before, array, after], axis=dim)
    return array


def body(
    fluxes, footprints, block_coords, block_count, observed, obs_weight, time_cov, diffusivity
):
    time_dev, tile_rows, width = fluxes.shape
    cell_blocks = tile_rows * width // 128
    slot_total = footprints.shape[0]
    obs_blocks = observed.shape[0] * lax.axis_size("space") // 128
    flux_rows = fluxes.reshape(time_dev * cell_blocks, 128)
    target = block_coords[0] * cell_blocks + block_coords[1]
    slot_live = (jnp.arange(slot_total, dtype=jnp.int32) < block_count[0]).astype(jnp.float32)
    pieces = jnp.take(flux_rows, target, axis=0)
    contrib = (
        jnp.einsum("boc,bc->bo", footprints, pieces, preferred_element_type=jnp.float32)
        * slot_live[:, None]
    )
    partial_sums = jax.ops.segment_sum(contrib, block_coords[2], num_segments=obs_blocks).reshape(
        -1
    )
    own_sums = lax.psum_scatter(partial_sums, ("space", "tm"), scatter_dimension=0, tiled=True)
    share = own_sums.shape[0]
    offset = lax.axis_index("tm") * share
    own_weight = lax.dynamic_slice_in_dim(obs_weight, offset, share)
    own_observed = lax.dynamic_slice_in_dim(observed, offset, share)
    misfit = own_weight * (own_sums - own_observed)
    misfit_full = lax.all_gather(misfit.astype(jnp.bfloat16), ("space", "tm"), axis=0, tiled=True)
    misfit_rows = misfit_full.reshape(obs_blocks, 128)
    chosen = jnp.take(misfit_rows, block_coords[2], axis=0)
    adjoint = (
        jnp.einsum("boc,bo->bc", footprints, chosen, preferred_element_type=jnp.float32)
        * slot_live[:, None]
    )
    grid = jax.ops.segment_sum(adjoint, target, num_segments=time_dev * cell_blocks)
    cov_rows = lax.dynamic_slice_in_dim(time_cov, lax.axis_index("tm") * time_dev, time_dev, 0)
    mixed = jnp.dot(
        cov_rows,
        lax.all_gather(grid.reshape(time_dev, cell_blocks * 128), "tm", axis=0, tiled=True),
        precision=lax.Precision.HIGHEST,
    )
    field = mixed.reshape(time_dev, tile_rows, width)
    for repeat in range(SWEEPS):
        rimmed = with_halo(field, (("space", 1),), 1)
        padded = jnp.pad(rimmed, ((0, 0), (0, 0), (1, 1)))
        laplace = (
            padded[:, 2:, 1:-1]
            + padded[:, :-2, 1:-1]
            + padded[:, 1:-1, 2:]
            + padded[:, 1:-1, :-2]
            - 4.0 * field
        )
        field = field + diffusivity * laplace
    return (misfit, field)


def solution(mesh):
    placed = (
        P("tm", "space", None),
        P(("space", "tm"), None, None),
        P(None, ("space", "tm")),
        P(("space", "tm")),
        P("space"),
        P("space"),
        P(),
        P("space", None),
    )
    return jax.shard_map(
        body,
        mesh=mesh,
        in_specs=placed,
        out_specs=(P(("space", "tm")), P("tm", "space", None)),
        check_vma=False,
    )
```

profile of v0, /device:TPU:3, one launch (start us, length us, event | category | flops | bytes accessed | tf_op | source)
XLA Modules:
  0.0 313.2 jit_solution(15878467352701359072)
XLA Ops:
  7.2 0.7 slice.98
  7.9 0.8 compare_select_fusion.1
  9.4 1.1 reshape.110
  10.6 1.3 gather_fusion
  12.0 12.2 %fusion.21 = f32[512,1,128]{2,1,0:T(1,128)S(1)} fusion(bf16[512,128,128]{2,1,0:T(8,128)(2,1)} %param.9, bf16[512,128,1]{1,0,2:T(8,128)(2,1)S(1)} %select_bitcast_fusion.1), kind=kOutput, calls=%fused_computation.52 | convolution fusion | flops 16777216 | bytes 17170432 | tf_op jit(solution)/shard_map/boc,bc->bo/dot_general | solution.py:34
  24.3 3.3 %scatter_custom_fusion = f32[1536,128]{1,0:T(8,128)} fusion(s32[512]{0:T(512)S(1)} %bitcast.33, f32[]{:T(128)} %constant.24.clone.1, f32[512,128]{1,0:T(8,128)S(1)} %bitcast.30, f32[512]{0:T(512)S(1)} %fusion.32), kind=kCustom, calls=%fused_computation.48 | custom fusion | flops 131072 | bytes 1050628 | tf_op jit(solution)/shard_map/scatter-add | solution.py:37
  27.7 147.8 %all-reduce.7.cloned.1.call-done = f32[196608]{0:T(1024)} async-done(((f32[196608]{0:T(1024)}), f32[196608]{0:T(1024)}) %all-reduce.7.cloned.1.call-update) | async-done | bytes 786448
  175.5 1.4 fusion.34
  176.9 35.2 %all-gather = bf16[128,1,1536]{2,1,0:T(2,128)(2,1)S(1)} all-gather(bf16[1,1,1536]{2,1,0:T(2,128)(2,1)S(1)} %reshape.149), channel_id=1, replica_groups=mesh['space'=16,'tm'=8] {'space','tm'}, dimensions={0}, use_global_device_ids=true | all-gather | bytes 396288 | tf_op jit(solution)/shard_map/all_gather | solution.py:46
  212.1 2.5 reduce
  214.5 0.5 reshape.112
  215.0 1.3 gather_fusion.1
  216.5 8.1 %fusion.19 = f32[512,1,128]{2,1,0:T(1,128)S(1)} fusion(bf16[512,128,128]{2,1,0:T(8,128)(2,1)} %param.9, bf16[512,128,1]{1,0,2:T(8,128)(2,1)S(1)} %select_bitcast_fusion), kind=kOutput, calls=%fused_computation.50 | convolution fusion | flops 16777216 | bytes 17170432 | tf_op jit(solution)/shard_map/boc,bo->bc/dot_general | solution.py:50
  224.6 2.7 scatter_custom_fusion.1
  227.4 1.0 reshape.151
  228.4 31.2 %all-gather.4.cloned.1.call-done = f32[8,4,32768]{2,1,0:T(4,128)} async-done(((f32[1,4,32768]{2,1,0:T(4,128)}), f32[8,4,32768]{2,1,0:T(4,128)}) %all-gather.4.cloned.1.call-update) | async-done | bytes 4194320 | tf_op jit(solution)/shard_map/all_gather | solution.py:57
  259.6 5.3 %reshape.152 = f32[32,32768]{1,0:T(8,128)} reshape(f32[8,4,32768]{2,1,0:T(4,128)} %all-gather.4.cloned.1.call-done) | data formatting | bytes 8388608
  264.9 4.3 %fusion.30 = f32[4,32768]{1,0:T(4,128)S(1)} fusion(f32[32,32768]{1,0:T(8,128)} %reshape.152, f32[32,32]{1,0:T(8,128)S(1)} %copy-done, s32[]{:T(128)S(6)} %select_n.50), kind=kOutput, calls=%fused_computation.70 | convolution fusion | flops 50331648 | bytes 4720644 | tf_op jit(solution)/shard_map/dot_general | solution.py:55
  269.4 3.1 collective-permute-start.1
  272.5 4.3 %collective-permute-start = (f32[4,1,512]{2,1,0:T(1,128)S(1)}, f32[4,1,512]{2,1,0:T(1,128)S(1)}, u32[]{:S(2)}, u32[]{:S(2)}) collective-permute-start(f32[4,1,512]{2,1,0:T(1,128)S(1)} %get-tuple-element.13), channel_id=1, source_target_pairs={{8,0},{16,8},{24,16},{32,24},{40,32},{48,40},{56,48},{64,56},{72,6... | collective-permute-start | bytes 24584 | tf_op jit(solution)/shard_map/ppermute | solution.py:17
  276.8 0.8 collective-permute-done
  277.9 0.3 fusion.15
  278.2 2.5 collective-permute-start.3
  280.7 5.2 %collective-permute-start.2 = (f32[4,1,512]{2,1,0:T(1,128)S(1)}, f32[4,1,512]{2,1,0:T(1,128)S(1)}, u32[]{:S(2)}, u32[]{:S(2)}) collective-permute-start(f32[4,1,512]{2,1,0:T(1,128)S(1)} %get-tuple-element.11), channel_id=1, source_target_pairs={{8,0},{16,8},{24,16},{32,24},{40,32},{48,40},{56,48},{64,56},{72,6... | collective-permute-start | bytes 24584 | tf_op jit(solution)/shard_map/ppermute | solution.py:17
  285.9 0.8 collective-permute-done.2
  287.4 3.0 collective-permute-start.5
  290.4 4.6 %collective-permute-start.4 = (f32[4,1,512]{2,1,0:T(1,128)S(1)}, f32[4,1,512]{2,1,0:T(1,128)S(1)}, u32[]{:S(2)}, u32[]{:S(2)}) collective-permute-start(f32[4,1,512]{2,1,0:T(1,128)S(1)} %get-tuple-element.9), channel_id=1, source_target_pairs={{8,0},{16,8},{24,16},{32,24},{40,32},{48,40},{56,48},{64,56},{72,6... | collective-permute-start | bytes 24584 | tf_op jit(solution)/shard_map/ppermute | solution.py:17
  295.0 0.8 collective-permute-done.4
  296.5 3.0 collective-permute-start.7
  299.5 4.6 %collective-permute-start.6 = (f32[4,1,512]{2,1,0:T(1,128)S(1)}, f32[4,1,512]{2,1,0:T(1,128)S(1)}, u32[]{:S(2)}, u32[]{:S(2)}) collective-permute-start(f32[4,1,512]{2,1,0:T(1,128)S(1)} %get-tuple-element.7), channel_id=1, source_target_pairs={{8,0},{16,8},{24,16},{32,24},{40,32},{48,40},{56,48},{64,56},{72,6... | collective-permute-start | bytes 24584 | tf_op jit(solution)/shard_map/ppermute | solution.py:17
  304.1 0.8 collective-permute-done.6
  305.2 1.1 fusion.3
  (31 shorter events, 2.6 us)
Async XLA Ops:
  7.2 257.7 %copy-start = (f32[32,32]{1,0:T(8,128)S(1)}, f32[32,32]{1,0:T(8,128)}, u32[]{:S(2)}) copy-start(f32[32,32]{1,0:T(8,128)} %param.14) | copy-start | bytes 12292
  7.2 168.3 %all-reduce.7.cloned.1.call-start = ((), (), s32[]{:S(2)}) async-start(), calls=%async_computation.1 | async-start | bytes 1572864
  27.6 232.0 %all-gather.4.cloned.1.call-start = ((), (), s32[]{:S(2)}) async-start(), calls=%async_computation | async-start | bytes 4718592 | tf_op jit(solution)/shard_map/all_gather | solution.py:57
  216.5 61.4 %copy-start.1 = (f32[64,512]{1,0:T(8,128)S(1)}, f32[64,512]{1,0:T(8,128)}, u32[]{:S(2)}) copy-start(f32[64,512]{1,0:T(8,128)} %param.15) | copy-start | bytes 393220
  269.4 7.4 %collective-permute-start.1 = (f32[4,1,512]{2,1,0:T(1,128)S(1)}, f32[4,1,512]{2,1,0:T(1,128)S(1)}, u32[]{:S(2)}, u32[]{:S(2)}) collective-permute-start(f32[4,1,512]{2,1,0:T(1,128)S(1)} %get-tuple-element.12), channel_id=1, source_target_pairs={{0,8},{8,16},{16,24},{24,32},{32,40},{40,48},{48,56},{56,64},{64,7... | collective-permute-start | bytes 24584 | tf_op jit(solution)/shard_map/ppermute | solution.py:16
  272.5 5.1 %collective-permute-start = (f32[4,1,512]{2,1,0:T(1,128)S(1)}, f32[4,1,512]{2,1,0:T(1,128)S(1)}, u32[]{:S(2)}, u32[]{:S(2)}) collective-permute-start(f32[4,1,512]{2,1,0:T(1,128)S(1)} %get-tuple-element.13), channel_id=1, source_target_pairs={{8,0},{16,8},{24,16},{32,24},{40,32},{48,40},{56,48},{64,56},{72,6... | collective-permute-start | bytes 24584 | tf_op jit(solution)/shard_map/ppermute | solution.py:17
  278.2 7.7 %collective-permute-start.3 = (f32[4,1,512]{2,1,0:T(1,128)S(1)}, f32[4,1,512]{2,1,0:T(1,128)S(1)}, u32[]{:S(2)}, u32[]{:S(2)}) collective-permute-start(f32[4,1,512]{2,1,0:T(1,128)S(1)} %get-tuple-element.10), channel_id=1, source_target_pairs={{0,8},{8,16},{16,24},{24,32},{32,40},{40,48},{48,56},{56,64},{64,7... | collective-permute-start | bytes 24584 | tf_op jit(solution)/shard_map/ppermute | solution.py:16
  280.7 6.0 %collective-permute-start.2 = (f32[4,1,512]{2,1,0:T(1,128)S(1)}, f32[4,1,512]{2,1,0:T(1,128)S(1)}, u32[]{:S(2)}, u32[]{:S(2)}) collective-permute-start(f32[4,1,512]{2,1,0:T(1,128)S(1)} %get-tuple-element.11), channel_id=1, source_target_pairs={{8,0},{16,8},{24,16},{32,24},{40,32},{48,40},{56,48},{64,56},{72,6... | collective-permute-start | bytes 24584 | tf_op jit(solution)/shard_map/ppermute | solution.py:17
  287.4 7.7 %collective-permute-start.5 = (f32[4,1,512]{2,1,0:T(1,128)S(1)}, f32[4,1,512]{2,1,0:T(1,128)S(1)}, u32[]{:S(2)}, u32[]{:S(2)}) collective-permute-start(f32[4,1,512]{2,1,0:T(1,128)S(1)} %get-tuple-element.8), channel_id=1, source_target_pairs={{0,8},{8,16},{16,24},{24,32},{32,40},{40,48},{48,56},{56,64},{64,7... | collective-permute-start | bytes 24584 | tf_op jit(solution)/shard_map/ppermute | solution.py:16
  290.4 5.4 %collective-permute-start.4 = (f32[4,1,512]{2,1,0:T(1,128)S(1)}, f32[4,1,512]{2,1,0:T(1,128)S(1)}, u32[]{:S(2)}, u32[]{:S(2)}) collective-permute-start(f32[4,1,512]{2,1,0:T(1,128)S(1)} %get-tuple-element.9), channel_id=1, source_target_pairs={{8,0},{16,8},{24,16},{32,24},{40,32},{48,40},{56,48},{64,56},{72,6... | collective-permute-start | bytes 24584 | tf_op jit(solution)/shard_map/ppermute | solution.py:17
  296.5 7.7 %collective-permute-start.7 = (f32[4,1,512]{2,1,0:T(1,128)S(1)}, f32[4,1,512]{2,1,0:T(1,128)S(1)}, u32[]{:S(2)}, u32[]{:S(2)}) collective-permute-start(f32[4,1,512]{2,1,0:T(1,128)S(1)} %get-tuple-element.6), channel_id=1, source_target_pairs={{0,8},{8,16},{16,24},{24,32},{32,40},{40,48},{48,56},{56,64},{64,7... | collective-permute-start | bytes 24584 | tf_op jit(solution)/shard_map/ppermute | solution.py:16
  299.5 5.4 %collective-permute-start.6 = (f32[4,1,512]{2,1,0:T(1,128)S(1)}, f32[4,1,512]{2,1,0:T(1,128)S(1)}, u32[]{:S(2)}, u32[]{:S(2)}) collective-permute-start(f32[4,1,512]{2,1,0:T(1,128)S(1)} %get-tuple-element.7), channel_id=1, source_target_pairs={{8,0},{16,8},{24,16},{32,24},{40,32},{48,40},{56,48},{64,56},{72,6... | collective-permute-start | bytes 24584 | tf_op jit(solution)/shard_map/ppermute | solution.py:17
Sparse Core Ops, SparseCore 0:
  27.7 147.7 all-reduce.6
  228.5 30.9 all-gather.3
where the time goes:
time: 319 us; the launch traced here: 313 us
  waiting for transfers between devices  182 us (57%)
  blocking collectives  35.2 us (11%)
  starting transfers between devices  30.4 us (10%)
  matrix products  24.6 us (8%)
  between operations  15 us (5%)
  other arithmetic  14.4 us (5%)
  local copies, waits for them, and re-layouts  11.6 us (4%)
    unnamed x3, waiting for transfers between devices  148 us
    all_gather x1, blocking collectives, body(): lax.all_gather(misfit.astype(jnp.bfloat16), ('space', 'tm'), axis=0, tile...  35.2 us
    all_gather x1, waiting for transfers between devices, body(): lax.all_gather(grid.reshape(time_dev, cell_blocks * 128), 'tm', axis=0, t...  31.2 us
    ppermute x4, starting transfers between devices, with_halo(): after = lax.ppermute(initial, axis, down)  18.7 us
    dot_general x1, matrix products, body(): jnp.einsum('boc,bc->bo', footprints, pieces, preferred_element_type=jnp.f...  12.2 us
    ppermute x4, starting transfers between devices, with_halo(): before = lax.ppermute(last, axis, up)  11.6 us
    dot_general x1, matrix products, body(): jnp.einsum('boc,bo->bc', footprints, chosen, preferred_element_type=jnp.f...  8.1 us
    unnamed x8, local copies, waits for them, and re-layouts  6.55 us
  transfers between devices with their start and end apart: 10, of which 6 were waited for; matrix products, arithmetic and copies ran while one was open for 0% of the time, Pallas kernels for 0%

commit v1 on v0

v1 whole, which is shorter than its diff:
```python
import jax
import jax.numpy as jnp
from jax import lax
from jax.experimental import pallas as pl
from jax.experimental.pallas import tpu as pltpu
from jax.sharding import PartitionSpec as P

SWEEPS = 4
LANES = 128
CHUNKS = 8
EDGE = 8
VMEM = 60 * 1024 * 1024

f32 = jnp.float32
bf16 = jnp.bfloat16


def split3(x):
    hi = x.astype(bf16)
    rest = x - hi.astype(f32)
    mid = rest.astype(bf16)
    low = (rest - mid.astype(f32)).astype(bf16)
    return hi, mid, low


def iota(shape, dim):
    return lax.broadcasted_iota(jnp.int32, shape, dim)


def onehot(equal):
    return jnp.where(equal, 1.0, 0.0).astype(bf16)


def dot(a, b, precision=None):
    return lax.dot_general(
        a, b, (((1,), (0,)), ((), ())), preferred_element_type=f32, precision=precision
    )


def column(row):
    wide = jnp.broadcast_to(row.astype(f32), (LANES, LANES))
    return jnp.transpose(wide, (1, 0)).astype(jnp.int32)


def forward_kernel(count_ref, coords_ref, flux_ref, foot_ref, out_ref, keep_ref, rhs, spread, sems):
    slots = foot_ref.shape[0]
    groups = slots // LANES
    per = slots // CHUNKS
    time_dev, tile_rows, width = flux_ref.shape
    across = width // LANES
    steps = time_dev * tile_rows

    def fetch(k):
        part = pl.ds(k * per, per)
        return pltpu.make_async_copy(foot_ref.at[part], keep_ref.at[part], sems.at[k])

    for k in range(CHUNKS):
        fetch(k).start()

    flux = flux_ref[...].reshape(steps, width)
    flux = jnp.concatenate([flux[:, l * LANES : (l + 1) * LANES] for l in range(across)], axis=0)
    lane = iota((LANES, LANES), 1)
    for g in range(groups):
        cut = slice(g * LANES, (g + 1) * LANES)
        cell = coords_ref[1:2, cut]
        code = (cell % across) * steps + coords_ref[0:1, cut] * tile_rows + cell // across
        code = column(code)
        pick = jnp.concatenate(
            [onehot(code == lane + j * LANES) for j in range(across * steps // LANES)], axis=1
        )
        piece = jnp.transpose(dot(pick, flux), (1, 0))
        even = (lane & 1) == 0
        rhs[g, :LANES, :] = jnp.where(even, piece, 0.0).astype(bf16)
        rhs[g, LANES:, :] = jnp.where(even, 0.0, piece).astype(bf16)

    pair_of_lane = lane // 2
    chunks_per_group = CHUNKS // groups
    for g in range(groups):
        total = jnp.zeros((LANES, LANES), f32)
        for part in range(chunks_per_group):
            fetch(g * chunks_per_group + part).wait()

            def step(i, total, part=part, g=g):
                for j in range(4):
                    p = part * (per // 2) + i * 4 + j
                    b = g * LANES + 2 * p
                    both = jnp.concatenate([keep_ref[b], keep_ref[b + 1]], axis=1)
                    total = jnp.where(pair_of_lane == p, dot(both, rhs[g]), total)
                return total

            total = lax.fori_loop(0, per // 8, step, total)
        parts = split3(jnp.transpose(total, (1, 0)))
        for n in range(3):
            spread[g * LANES : (g + 1) * LANES, n * LANES : (n + 1) * LANES] = parts[n]

    slot = iota((1, slots), 1)
    block = jnp.where(slot < count_ref[0], coords_ref[2:3, :], -1)
    rows = out_ref.shape[0] * out_ref.shape[1]
    cols = out_ref.shape[2] // LANES
    for l in range(cols):
        mine = iota((rows, slots), 0) * cols + l
        full = dot(onehot(mine == block), spread[...])
        summed = full[:, :LANES] + full[:, LANES : 2 * LANES] + full[:, 2 * LANES :]
        out_ref[:, :, l * LANES : (l + 1) * LANES] = summed.reshape(
            out_ref.shape[0], out_ref.shape[1], LANES
        )


def forward(count, coords, fluxes, footprints, devices, obs_blocks):
    per = obs_blocks // devices
    slots = footprints.shape[0]
    vmem = pl.BlockSpec(memory_space=pltpu.VMEM)
    return pl.pallas_call(
        forward_kernel,
        out_shape=(
            jax.ShapeDtypeStruct((devices, 4, per * LANES // 4), f32),
            jax.ShapeDtypeStruct(footprints.shape, bf16),
        ),
        in_specs=[pl.BlockSpec(memory_space=pltpu.SMEM), vmem, vmem, pl.BlockSpec(memory_space=pl.ANY)],
        out_specs=(vmem, vmem),
        scratch_shapes=[
            pltpu.VMEM((slots // LANES, 2 * LANES, LANES), bf16),
            pltpu.VMEM((slots, 3 * LANES), bf16),
            pltpu.SemaphoreType.DMA((CHUNKS,)),
        ],
        compiler_params=pltpu.CompilerParams(vmem_limit_bytes=VMEM),
        name="forward",
    )(count, coords, fluxes, footprints)


def misfit_kernel(sums_ref, weight_ref, observed_ref, out_ref, half_ref):
    total = jnp.sum(sums_ref[...], axis=0)
    misfit = weight_ref[...] * (total - observed_ref[...])
    out_ref[...] = misfit
    half_ref[...] = jnp.broadcast_to(misfit[None], half_ref.shape).astype(bf16)


def misfit_of(sums, weight, observed):
    devices = sums.shape[0]
    shape = sums.shape[1:]
    return pl.pallas_call(
        misfit_kernel,
        out_shape=(
            jax.ShapeDtypeStruct(shape, f32),
            jax.ShapeDtypeStruct((devices,) + shape, bf16),
        ),
        name="misfit",
    )(sums, weight.reshape(shape), observed.reshape(shape))


def adjoint_kernel(
    count_ref,
    coords_ref,
    misfit_ref,
    foot_ref,
    before_ref,
    diff_ref,
    after_ref,
    out_ref,
    contrib,
    spread,
    field,
    other,
    rows_ref,
):
    slots = foot_ref.shape[0]
    groups = slots // LANES
    devices, quarter, wide = misfit_ref.shape
    cols = wide // LANES
    rows = devices * quarter
    lane = iota((LANES, LANES), 1)
    rows_ref[...] = misfit_ref[...].astype(f32).reshape(rows, wide).astype(bf16)
    for g in range(groups):
        block = column(coords_ref[2:3, g * LANES : (g + 1) * LANES])
        chosen = jnp.zeros((LANES, LANES), f32)
        for l in range(cols):
            pick = jnp.concatenate(
                [onehot(block == (lane + j * LANES) * cols + l) for j in range(rows // LANES)], axis=1
            )
            chosen = chosen + dot(pick, rows_ref[:, l * LANES : (l + 1) * LANES])
        contrib[g * LANES : (g + 1) * LANES, :] = chosen

    batch = 16
    sub = iota((batch, LANES), 0)

    def step(i, carry):
        for half in range(2):
            at = pl.multiple_of(i * 2 * batch + half * batch, batch)
            some = contrib[pl.ds(at, batch), :]
            left = jnp.concatenate(
                [jnp.where(sub == j, some, 0.0).astype(bf16) for j in range(batch)], axis=1
            )
            blocks = foot_ref[pl.ds(at, batch)].reshape(batch * LANES, LANES)
            for n, part in enumerate(split3(dot(left, blocks))):
                spread[pl.ds(at, batch), n * LANES : (n + 1) * LANES] = part
        return carry

    lax.fori_loop(0, slots // (2 * batch), step, 0)

    time_dev, ext_rows, width = field.shape
    across = width // LANES
    tile_rows = diff_ref.shape[0]
    steps = time_dev * tile_rows
    slot = iota((1, slots), 1)
    cell = coords_ref[1:2, :]
    code = coords_ref[0:1, :] * tile_rows + cell // across
    code = jnp.where(slot < count_ref[0], code, -1)
    up, inner, down = slice(EDGE - 1, ext_rows - EDGE - 1), slice(EDGE, ext_rows - EDGE), slice(EDGE + 1, ext_rows - EDGE + 1)
    for buffer in (field, other):
        for t in range(time_dev):
            buffer[t, : 2 * EDGE, :] = jnp.zeros((2 * EDGE, width), f32)
            buffer[t, ext_rows - 2 * EDGE :, :] = jnp.zeros((2 * EDGE, width), f32)
    for l in range(across):
        pick = onehot(iota((steps, slots), 0) == jnp.where(cell % across == l, code, -1))
        full = dot(pick, spread[...])
        summed = full[:, :LANES] + full[:, LANES : 2 * LANES] + full[:, 2 * LANES :]
        for t in range(time_dev):
            field[t, 2 * EDGE : 2 * EDGE + tile_rows, l * LANES : (l + 1) * LANES] = summed[
                t * tile_rows : (t + 1) * tile_rows
            ]
    diff = jnp.concatenate([before_ref[...], diff_ref[...], after_ref[...]], axis=0)
    column_of = iota(diff.shape, 1)
    source, target = field, other
    for sweep in range(SWEEPS):
        for t in range(time_dev):
            here = source[t, inner, :]
            left = jnp.where(column_of == 0, 0.0, pltpu.roll(here, 1, 1))
            right = jnp.where(column_of == width - 1, 0.0, pltpu.roll(here, width - 1, 1))
            laplace = source[t, down, :] + source[t, up, :] + right + left - 4.0 * here
            target[t, inner, :] = here + diff * laplace
        source, target = target, source
    half = tile_rows // 2
    first = 2 * EDGE
    for h in range(2):
        edge = first - SWEEPS if h == 0 else first + tile_rows
        for l in range(across):
            cut = slice(l * LANES, (l + 1) * LANES)
            rows_out = [
                source[t, first + h * half : first + (h + 1) * half, cut] for t in range(time_dev)
            ] + [source[t, edge : edge + SWEEPS, cut] for t in range(time_dev)]
            out_ref[h * across + l] = jnp.concatenate(rows_out, axis=0).astype(out_ref.dtype)


def adjoint_of(count, coords, misfit_rows, footprints, before, diffusivity, after, time_dev):
    slots = footprints.shape[0]
    tile_rows, width = diffusivity.shape
    devices, quarter, wide = misfit_rows.shape
    parts = 2 * width // LANES
    vmem = pl.BlockSpec(memory_space=pltpu.VMEM)
    field = pltpu.VMEM((time_dev, tile_rows + 4 * EDGE, width), f32)
    return pl.pallas_call(
        adjoint_kernel,
        out_shape=jax.ShapeDtypeStruct((parts, time_dev * (tile_rows // 2 + SWEEPS), LANES), bf16),
        in_specs=[pl.BlockSpec(memory_space=pltpu.SMEM)] + [vmem] * 6,
        out_specs=vmem,
        scratch_shapes=[
            pltpu.VMEM((slots, LANES), f32),
            pltpu.VMEM((slots, 3 * LANES), bf16),
            field,
            field,
            pltpu.VMEM((devices * quarter, wide), bf16),
        ],
        compiler_params=pltpu.CompilerParams(vmem_limit_bytes=VMEM),
        name="adjoint",
    )(count, coords, misfit_rows, footprints, before, diffusivity, after)


def expanded(cov, rows, per_row, cols, per_col, shift):
    times = cov.shape[0]
    tall = onehot(iota((rows, times), 0) // per_row == iota((rows, times), 1)).astype(f32)
    broad = onehot(iota((times, cols), 1) // per_col == iota((times, cols), 0)).astype(f32)
    full = dot(dot(tall, cov, lax.Precision.HIGHEST), broad, lax.Precision.HIGHEST)
    same = iota((rows, cols), 0) % per_row == iota((rows, cols), 1) % per_col + shift
    return jnp.where(same, full, 0.0)


def spill_kernel(half_ref, cov_ref, parts_ref, out_ref):
    senders, rows, _ = parts_ref.shape
    times = cov_ref.shape[0]
    time_dev = times // senders
    main = rows - time_dev * SWEEPS
    edges = jnp.concatenate(
        [parts_ref[n, main:, :].astype(f32) for n in range(senders)], axis=0
    ).astype(bf16)
    shift = jnp.where(half_ref[0] == 0, SWEEPS, 0)
    wide = expanded(cov_ref[...], times * EDGE, EDGE, times * SWEEPS, SWEEPS, shift)
    out_ref[...] = sum(dot(part, edges) for part in split3(wide))


def mix_spill(half, cov, parts):
    vmem = pl.BlockSpec(memory_space=pltpu.VMEM)
    return pl.pallas_call(
        spill_kernel,
        out_shape=jax.ShapeDtypeStruct((cov.shape[0] * EDGE, LANES), f32),
        in_specs=[pl.BlockSpec(memory_space=pltpu.SMEM), vmem, vmem],
        out_specs=vmem,
        name="mix_spill",
    )(half, cov, parts)


def mix_kernel(half_ref, cov_ref, parts_ref, spill_ref, out_ref):
    senders, rows, _ = parts_ref.shape
    times = cov_ref.shape[0]
    time_dev = times // senders
    tall = (rows - time_dev * SWEEPS) // time_dev
    wide = split3(expanded(cov_ref[...], times * EDGE, EDGE, times * EDGE, EDGE, 0))
    strips = []
    for r in range(tall // EDGE):
        strips.append(
            jnp.concatenate(
                [
                    parts_ref[n, u * tall + r * EDGE : u * tall + (r + 1) * EDGE, :].astype(f32)
                    for n in range(senders)
                    for u in range(time_dev)
                ],
                axis=0,
            ).astype(bf16)
        )
    field = jnp.concatenate(strips, axis=1)
    mixed = dot(wide[0], field) + dot(wide[1], field) + dot(wide[2], field)
    strips = [mixed[:, r * LANES : (r + 1) * LANES] for r in range(tall // EDGE)]
    strips[0] = strips[0] + jnp.where(half_ref[0] == 0, spill_ref[...], 0.0)
    strips[-1] = strips[-1] + jnp.where(half_ref[0] == 0, 0.0, spill_ref[...])
    for t in range(times):
        cut = slice(t * EDGE, (t + 1) * EDGE)
        at = (t % time_dev) * tall
        out_ref[t // time_dev, at : at + tall, :] = jnp.concatenate(
            [strip[cut] for strip in strips], axis=0
        ).astype(out_ref.dtype)


def mix(half, cov, parts, spill):
    senders, rows, _ = parts.shape
    time_dev = cov.shape[0] // senders
    vmem = pl.BlockSpec(memory_space=pltpu.VMEM)
    return pl.pallas_call(
        mix_kernel,
        out_shape=jax.ShapeDtypeStruct((senders, rows - time_dev * SWEEPS, LANES), bf16),
        in_specs=[pl.BlockSpec(memory_space=pltpu.SMEM), vmem, vmem, vmem],
        out_specs=vmem,
        name="mix",
    )(half, cov, parts, spill)


def place_kernel(parts_ref, out_ref):
    time_dev, tile_rows, width = out_ref.shape
    across = width // LANES
    half = tile_rows // 2
    for h in range(2):
        for l in range(across):
            for t in range(time_dev):
                out_ref[t, h * half : (h + 1) * half, l * LANES : (l + 1) * LANES] = parts_ref[
                    h * across + l, t * half : (t + 1) * half, :
                ].astype(f32)


def body(
    fluxes, footprints, block_coords, block_count, observed, obs_weight, time_cov, diffusivity
):
    time_dev, tile_rows, width = fluxes.shape
    n_space, n_tm = lax.axis_size("space"), lax.axis_size("tm")
    devices = n_space * n_tm
    obs_blocks = observed.shape[0] * n_space // LANES
    tm = lax.axis_index("tm")
    half = (tm // (n_tm // 2)).astype(jnp.int32).reshape(1)

    down = [(i, i + 1) for i in range(n_space - 1)]
    up = [(i + 1, i) for i in range(n_space - 1)]
    before = lax.ppermute(diffusivity[tile_rows - EDGE :], "space", down)
    after = lax.ppermute(diffusivity[:EDGE], "space", up)

    sums, kept = forward(block_count, block_coords, fluxes, footprints, devices, obs_blocks)
    sums = lax.all_to_all(sums, ("space", "tm"), 0, 0, tiled=True)
    share = observed.shape[0] // n_tm
    weight = lax.dynamic_slice_in_dim(obs_weight, tm * share, share)
    target = lax.dynamic_slice_in_dim(observed, tm * share, share)
    misfit, halves = misfit_of(sums, weight, target)
    halves = lax.all_to_all(halves, ("space", "tm"), 0, 0, tiled=True)
    parts = adjoint_of(
        block_count, block_coords, halves, kept, before, diffusivity, after, time_dev
    )
    parts = lax.all_to_all(parts, "tm", 0, 0, tiled=True)
    spill = mix_spill(half, time_cov, parts)
    across = n_tm // 2
    moves = []
    for s in range(n_space):
        for l in range(across):
            if s + 1 < n_space:
                moves.append((s * n_tm + across + l, (s + 1) * n_tm + l))
                moves.append(((s + 1) * n_tm + l, s * n_tm + across + l))
    spill = lax.ppermute(spill, ("space", "tm"), moves)
    mixed = mix(half, time_cov, parts, spill)
    mixed = lax.all_to_all(mixed, "tm", 0, 0, tiled=True)
    field = pl.pallas_call(
        place_kernel,
        out_shape=jax.ShapeDtypeStruct(fluxes.shape, f32),
        name="place",
    )(mixed)
    return misfit.reshape(share), field


def solution(mesh):
    placed = (
        P("tm", "space", None),
        P(("space", "tm"), None, None),
        P(None, ("space", "tm")),
        P(("space", "tm")),
        P("space"),
        P("space"),
        P(),
        P("space", None),
    )
    return jax.shard_map(
        body,
        mesh=mesh,
        in_specs=placed,
        out_specs=(P(("space", "tm")), P("tm", "space", None)),
        check_vma=False,
    )
```

time: 319 us -> 129 us (0.40); the launches traced: 313 us -> 128 us
  waiting for transfers between devices: 182 us -> 33.1 us
  Pallas kernels: 0 us -> 46.1 us
  blocking collectives: 35.2 us -> 0 us
  matrix products: 24.6 us -> 0 us
  other arithmetic: 14.4 us -> 0 us
  between operations: 15 us -> 1.36 us
  starting transfers between devices: 30.4 us -> 39.8 us
  local copies, waits for them, and re-layouts: 11.6 us -> 7.8 us
    unnamed x3 -> x0, waiting for transfers between devices: 148 us -> none
    pallas_call x0 -> x6, Pallas kernels: none -> 46.1 us  [the longest x1 22.5 us: forward(): pl.pallas_call(forward_kernel, out_shape=(jax.ShapeDtypeStruct((devices,...]
    all_gather x1 -> x0, blocking collectives: 35.2 us -> none  [body(): lax.all_gather(misfit.astype(jnp.bfloat16), ('space', 'tm'), axis=0, tile...]
    all_gather x1 -> x0, waiting for transfers between devices: 31.2 us -> none  [body(): lax.all_gather(grid.reshape(time_dev, cell_blocks * 128), 'tm', axis=0, t...]
    all_to_all x0 -> x4, waiting for transfers between devices: none -> 27.7 us  [the longest x1 12.6 us: body(): sums = lax.all_to_all(sums, ('space', 'tm'), 0, 0, tiled=True)]
    all_to_all x0 -> x4, starting transfers between devices: none -> 26.7 us  [the longest x1 10.8 us: body(): sums = lax.all_to_all(sums, ('space', 'tm'), 0, 0, tiled=True)]
    dot_general x3 -> x0, matrix products: 24.6 us -> none  [the longest x1 12.2 us: body(): jnp.einsum('boc,bc->bo', footprints, pieces, preferred_element_type=jnp.f...]
    ppermute x8 -> x3, starting transfers between devices: 30.3 us -> 13.2 us  [the longest x1 5.77 us: body(): spill = lax.ppermute(spill, ('space', 'tm'), moves)]
  transfers between devices with their start and end apart: 10 -> 7, of which waited for: 6 -> 6; matrix products, arithmetic and copies ran while one was open for 0% -> 3% of each run, Pallas kernels for 0% -> 0%
where the time goes in v1:
time: 129 us; the launch traced here: 128 us
  Pallas kernels  46.1 us (36%)
  starting transfers between devices  39.8 us (31%)
  waiting for transfers between devices  33.1 us (26%)
  local copies, waits for them, and re-layouts  7.8 us (6%)
  between operations  1.36 us (1%)
    pallas_call x1, Pallas kernels, forward(): pl.pallas_call(forward_kernel, out_shape=(jax.ShapeDtypeStruct((devices,...  22.5 us
    pallas_call x1, Pallas kernels, adjoint_of(): pl.pallas_call(adjoint_kernel, out_shape=jax.ShapeDtypeStruct((parts, tim...  14.4 us
    all_to_all x1, waiting for transfers between devices, body(): sums = lax.all_to_all(sums, ('space', 'tm'), 0, 0, tiled=True)  12.6 us
    all_to_all x1, starting transfers between devices, body(): sums = lax.all_to_all(sums, ('space', 'tm'), 0, 0, tiled=True)  10.8 us
    all_to_all x1, waiting for transfers between devices, body(): parts = lax.all_to_all(parts, 'tm', 0, 0, tiled=True)  6.83 us
    all_to_all x1, waiting for transfers between devices, body(): mixed = lax.all_to_all(mixed, 'tm', 0, 0, tiled=True)  5.91 us
    all_to_all x1, starting transfers between devices, body(): halves = lax.all_to_all(halves, ('space', 'tm'), 0, 0, tiled=True)  5.8 us
    ppermute x1, starting transfers between devices, body(): spill = lax.ppermute(spill, ('space', 'tm'), moves)  5.77 us
  transfers between devices with their start and end apart: 7, of which 6 were waited for; matrix products, arithmetic and copies ran while one was open for 3% of the time, Pallas kernels for 0%

profile of v1, /device:TPU:3, one launch (start us, length us, event | category | flops | bytes accessed | tf_op | source)
XLA Modules:
  0.0 128.2 jit_solution(10453451189584566355)
XLA Ops:
  1.3 22.5 %forward.1 = (f32[128,4,384]{2,1,0:T(4,128)}, bf16[512,128,128]{2,1,0:T(8,128)(2,1)}) custom-call(s32[1]{0:T(128)S(6)} %copy.10.count_ref, s32[3,512]{1,0:T(4,128)} %coords_ref.3, bf16[4,64,512]{2,1,0:T(8,128)(2,1)} %flux_ref.1, bf16[512,128,128]{2,1,0:T(8,128)(2,1)} %foot_ref.1), custom_call_target="tpu_custom_call" | custom-call | tf_op jit(solution)/shard_map/forward/pallas_call | solution.py:113
  23.8 10.8 %all-to-all-start = ((f32[128,4,384]{2,1,0:T(4,128)}), f32[128,4,384]{2,1,0:T(4,128)S(1)}, u32[]{:S(2)}, u32[]{:S(2)}) async-start(f32[128,4,384]{2,1,0:T(4,128)} %get-tuple-element.6), calls=%async_computation | async-start | bytes 1572864 | tf_op jit(solution)/shard_map/all_to_all | solution.py:373
  34.6 0.8 dynamic_slice.6
  35.4 0.6 reshape.16.weight_ref
  36.0 0.8 dynamic_slice.7
  36.8 0.6 reshape.17.observed_ref
  37.4 12.6 %all-to-all-done.sums_ref = f32[128,4,384]{2,1,0:T(4,128)S(1)} async-done(((f32[128,4,384]{2,1,0:T(4,128)}), f32[128,4,384]{2,1,0:T(4,128)S(1)}, u32[]{:S(2)}, u32[]{:S(2)}) %all-to-all-start) | async-done | bytes 786464 | tf_op jit(solution)/shard_map/all_to_all | solution.py:373
  50.0 0.9 copy-done
  50.9 2.1 %misfit.1 = (f32[4,384]{1,0:T(4,128)}, bf16[128,4,384]{2,1,0:T(4,128)(2,1)}) custom-call(f32[128,4,384]{2,1,0:T(4,128)} %copy-done, f32[4,384]{1,0:T(4,128)} %reshape.16.weight_ref, f32[4,384]{1,0:T(4,128)} %reshape.17.observed_ref), custom_call_target="tpu_custom_call" | custom-call | tf_op jit(solution)/shard_map/misfit/pallas_call | solution.py:141
  53.0 5.8 %all-to-all-start.1 = ((bf16[128,4,384]{2,1,0:T(4,128)(2,1)}), bf16[128,4,384]{2,1,0:T(4,128)(2,1)S(1)}, u32[]{:S(2)}, u32[]{:S(2)}) async-start(bf16[128,4,384]{2,1,0:T(4,128)(2,1)} %get-tuple-element.8), calls=%async_computation.1 | async-start | bytes 786432 | tf_op jit(solution)/shard_map/all_to_all | solution.py:378
  58.8 0.7 fusion
  59.6 3.1 %collective-permute-start = (f32[8,512]{1,0:T(8,128)S(1)}, f32[8,512]{1,0:T(8,128)S(1)}, u32[]{:S(2)}, u32[]{:S(2)}) collective-permute-start(f32[8,512]{1,0:T(8,128)S(1)} %get-tuple-element.11), channel_id=1, source_target_pairs={{0,8},{8,16},{16,24},{24,32},{32,40},{40,48},{48,56},{56,64},{64,7... | collective-permute-start | bytes 49160 | tf_op jit(solution)/shard_map/ppermute | solution.py:369
  62.7 4.2 %collective-permute-start.1 = (f32[8,512]{1,0:T(8,128)S(1)}, f32[8,512]{1,0:T(8,128)S(1)}, u32[]{:S(2)}, u32[]{:S(2)}) collective-permute-start(f32[8,512]{1,0:T(8,128)S(1)} %get-tuple-element.10), channel_id=1, source_target_pairs={{8,0},{16,8},{24,16},{32,24},{40,32},{48,40},{56,48},{64,56},{72,6... | collective-permute-start | bytes 49160 | tf_op jit(solution)/shard_map/ppermute | solution.py:370
  67.0 0.0 collective-permute-done.before_ref
  67.0 0.8 collective-permute-done.1.after_ref
  67.8 2.3 %all-to-all-done.1.misfit_ref = bf16[128,4,384]{2,1,0:T(4,128)(2,1)S(1)} async-done(((bf16[128,4,384]{2,1,0:T(4,128)(2,1)}), bf16[128,4,384]{2,1,0:T(4,128)(2,1)S(1)}, u32[]{:S(2)}, u32[]{:S(2)}) %all-to-all-start.1) | async-done | bytes 393248 | tf_op jit(solution)/shard_map/all_to_all | solution.py:378
  70.1 0.0 copy-done.6
  70.1 0.7 copy-done.2
  70.9 14.4 %adjoint.1 = bf16[8,144,128]{2,1,0:T(8,128)(2,1)} custom-call(s32[1]{0:T(128)S(6)} %copy.10.count_ref, s32[3,512]{1,0:T(4,128)} %coords_ref.3, bf16[128,4,384]{2,1,0:T(4,128)(2,1)} %copy-done.2, bf16[512,128,128]{2,1,0:T(8,128)(2,1)} %get-tuple-element.9.foot_ref, f32[8,512]{1,0:T(8,128)} %copy-done.5, f32[64,512]{1,0:T(8,128)} %diff_ref.1, f32[8,512]{1,0:T(8,128)} %copy-done.6), custom_call_target="tpu_custom_call" | custom-call | tf_op jit(solution)/shard_map/adjoint/pallas_call | solution.py:251
  85.2 4.5 %all-to-all-start.2 = ((bf16[8,144,128]{2,1,0:T(8,128)(2,1)}), bf16[8,144,128]{2,1,0:T(8,128)(2,1)S(1)}, u32[]{:S(2)}, u32[]{:S(2)}) async-start(bf16[8,144,128]{2,1,0:T(8,128)(2,1)} %adjoint.1), calls=%async_computation.2 | async-start | bytes 589824 | tf_op jit(solution)/shard_map/all_to_all | solution.py:382
  89.7 6.8 %all-to-all-done.2.parts_ref = bf16[8,144,128]{2,1,0:T(8,128)(2,1)S(1)} async-done(((bf16[8,144,128]{2,1,0:T(8,128)(2,1)}), bf16[8,144,128]{2,1,0:T(8,128)(2,1)S(1)}, u32[]{:S(2)}, u32[]{:S(2)}) %all-to-all-start.2) | async-done | bytes 294944 | tf_op jit(solution)/shard_map/all_to_all | solution.py:382
  96.5 0.7 copy-done.1
  97.3 2.4 %mix_spill.1 = f32[256,128]{1,0:T(8,128)} custom-call(s32[1]{0:T(128)} %bitcast.half_ref, f32[32,32]{1,0:T(8,128)} %cov_ref.3, bf16[8,144,128]{2,1,0:T(8,128)(2,1)} %copy-done.1), custom_call_target="tpu_custom_call" | custom-call | tf_op jit(solution)/shard_map/mix_spill/pallas_call | solution.py:292
  99.7 5.8 %collective-permute-start.2 = (f32[256,128]{1,0:T(8,128)}, f32[256,128]{1,0:T(8,128)S(1)}, u32[]{:S(2)}, u32[]{:S(2)}) collective-permute-start(f32[256,128]{1,0:T(8,128)} %mix_spill.1), channel_id=1, source_target_pairs={{4,8},{8,4},{5,9},{9,5},{6,10},{10,6},{7,11},{11,7},{12,16},{16,12... | collective-permute-start | bytes 393224 | tf_op jit(solution)/shard_map/ppermute | solution.py:391
  105.4 4.6 %collective-permute-done.2.spill_ref = f32[256,128]{1,0:T(8,128)S(1)} collective-permute-done((f32[256,128]{1,0:T(8,128)}, f32[256,128]{1,0:T(8,128)S(1)}, u32[]{:S(2)}, u32[]{:S(2)}) %collective-permute-start.2) | collective-permute-done | bytes 131104 | tf_op jit(solution)/shard_map/ppermute | solution.py:391
  110.1 0.6 copy-done.4
  110.7 2.9 %mix.1 = bf16[8,128,128]{2,1,0:T(8,128)(2,1)} custom-call(s32[1]{0:T(128)} %bitcast.half_ref, f32[32,32]{1,0:T(8,128)} %cov_ref.3, bf16[8,144,128]{2,1,0:T(8,128)(2,1)} %copy-done.1, f32[256,128]{1,0:T(8,128)} %copy-done.4), custom_call_target="tpu_custom_call" | custom-call | tf_op jit(solution)/shard_map/mix/pallas_call | solution.py:336
  113.6 5.5 %all-to-all-start.3 = ((bf16[8,128,128]{2,1,0:T(8,128)(2,1)}), bf16[8,128,128]{2,1,0:T(8,128)(2,1)S(1)}, u32[]{:S(2)}, u32[]{:S(2)}) async-start(bf16[8,128,128]{2,1,0:T(8,128)(2,1)} %mix.1), calls=%async_computation.3 | async-start | bytes 524288 | tf_op jit(solution)/shard_map/all_to_all | solution.py:393
  119.2 0.6 reshape.18
  119.8 5.9 %all-to-all-done.3.parts_ref = bf16[8,128,128]{2,1,0:T(8,128)(2,1)S(1)} async-done(((bf16[8,128,128]{2,1,0:T(8,128)(2,1)}), bf16[8,128,128]{2,1,0:T(8,128)(2,1)S(1)}, u32[]{:S(2)}, u32[]{:S(2)}) %all-to-all-start.3) | async-done | bytes 262176 | tf_op jit(solution)/shard_map/all_to_all | solution.py:393
  125.7 0.7 copy-done.3
  126.4 1.8 %place.1 = f32[4,64,512]{2,1,0:T(8,128)} custom-call(bf16[8,128,128]{2,1,0:T(8,128)(2,1)} %copy-done.3), custom_call_target="tpu_custom_call" | custom-call | tf_op jit(solution)/shard_map/place/pallas_call | solution.py:394
  (10 shorter events, 0.0 us)
Async XLA Ops:
  23.8 26.2 %all-to-all-start = ((f32[128,4,384]{2,1,0:T(4,128)}), f32[128,4,384]{2,1,0:T(4,128)S(1)}, u32[]{:S(2)}, u32[]{:S(2)}) async-start(f32[128,4,384]{2,1,0:T(4,128)} %get-tuple-element.6), calls=%async_computation | async-start | bytes 1572864 | tf_op jit(solution)/shard_map/all_to_all | solution.py:373
  50.0 0.9 copy-start
  53.0 66.2 %copy-start.7 = (f32[4,384]{1,0:T(4,128)S(1)}, f32[4,384]{1,0:T(4,128)}, u32[]{:S(2)}) copy-start(f32[4,384]{1,0:T(4,128)} %get-tuple-element.7) | copy-start | bytes 18436
  53.0 17.1 %all-to-all-start.1 = ((bf16[128,4,384]{2,1,0:T(4,128)(2,1)}), bf16[128,4,384]{2,1,0:T(4,128)(2,1)S(1)}, u32[]{:S(2)}, u32[]{:S(2)}) async-start(bf16[128,4,384]{2,1,0:T(4,128)(2,1)} %get-tuple-element.8), calls=%async_computation.1 | async-start | bytes 786432 | tf_op jit(solution)/shard_map/all_to_all | solution.py:378
  59.6 7.4 %collective-permute-start = (f32[8,512]{1,0:T(8,128)S(1)}, f32[8,512]{1,0:T(8,128)S(1)}, u32[]{:S(2)}, u32[]{:S(2)}) collective-permute-start(f32[8,512]{1,0:T(8,128)S(1)} %get-tuple-element.11), channel_id=1, source_target_pairs={{0,8},{8,16},{16,24},{24,32},{32,40},{40,48},{48,56},{56,64},{64,7... | collective-permute-start | bytes 49160 | tf_op jit(solution)/shard_map/ppermute | solution.py:369
  62.7 5.1 %collective-permute-start.1 = (f32[8,512]{1,0:T(8,128)S(1)}, f32[8,512]{1,0:T(8,128)S(1)}, u32[]{:S(2)}, u32[]{:S(2)}) collective-permute-start(f32[8,512]{1,0:T(8,128)S(1)} %get-tuple-element.10), channel_id=1, source_target_pairs={{8,0},{16,8},{24,16},{32,24},{40,32},{48,40},{56,48},{64,56},{72,6... | collective-permute-start | bytes 49160 | tf_op jit(solution)/shard_map/ppermute | solution.py:370
  67.0 3.2 %copy-start.5 = (f32[8,512]{1,0:T(8,128)}, f32[8,512]{1,0:T(8,128)S(1)}, u32[]{:S(2)}) copy-start(f32[8,512]{1,0:T(8,128)S(1)} %collective-permute-done.before_ref) | copy-start | bytes 49156
  67.8 2.3 %copy-start.6 = (f32[8,512]{1,0:T(8,128)}, f32[8,512]{1,0:T(8,128)S(1)}, u32[]{:S(2)}) copy-start(f32[8,512]{1,0:T(8,128)S(1)} %collective-permute-done.1.after_ref) | copy-start | bytes 49156
  70.1 0.7 copy-start.2
  85.2 11.3 %all-to-all-start.2 = ((bf16[8,144,128]{2,1,0:T(8,128)(2,1)}), bf16[8,144,128]{2,1,0:T(8,128)(2,1)S(1)}, u32[]{:S(2)}, u32[]{:S(2)}) async-start(bf16[8,144,128]{2,1,0:T(8,128)(2,1)} %adjoint.1), calls=%async_computation.2 | async-start | bytes 589824 | tf_op jit(solution)/shard_map/all_to_all | solution.py:382
  96.5 0.7 copy-start.1
  99.7 10.4 %collective-permute-start.2 = (f32[256,128]{1,0:T(8,128)}, f32[256,128]{1,0:T(8,128)S(1)}, u32[]{:S(2)}, u32[]{:S(2)}) collective-permute-start(f32[256,128]{1,0:T(8,128)} %mix_spill.1), channel_id=1, source_target_pairs={{4,8},{8,4},{5,9},{9,5},{6,10},{10,6},{7,11},{11,7},{12,16},{16,12... | collective-permute-start | bytes 393224 | tf_op jit(solution)/shard_map/ppermute | solution.py:391
  110.1 0.6 copy-start.4
  113.6 12.1 %all-to-all-start.3 = ((bf16[8,128,128]{2,1,0:T(8,128)(2,1)}), bf16[8,128,128]{2,1,0:T(8,128)(2,1)S(1)}, u32[]{:S(2)}, u32[]{:S(2)}) async-start(bf16[8,128,128]{2,1,0:T(8,128)(2,1)} %mix.1), calls=%async_computation.3 | async-start | bytes 524288 | tf_op jit(solution)/shard_map/all_to_all | solution.py:393
  125.7 0.7 copy-start.3

commit v2 on v0

v2 whole, which is shorter than its diff:
```python
import jax
import jax.numpy as jnp
from jax import lax
from jax.experimental import pallas as pl
from jax.experimental.pallas import tpu as pltpu
from jax.sharding import PartitionSpec as P

SWEEPS = 4
LANES = 128
CHUNKS = 8
EDGE = 8
MIB = 1024 * 1024

f32 = jnp.float32
bf16 = jnp.bfloat16


def split2(x):
    hi = x.astype(bf16)
    return hi, (x - hi.astype(f32)).astype(bf16)


def iota(shape, dim):
    return lax.broadcasted_iota(jnp.int32, shape, dim)


def onehot(equal):
    return jnp.where(equal, 1.0, 0.0).astype(bf16)


def dot(a, b, precision=None):
    return lax.dot_general(
        a, b, (((1,), (0,)), ((), ())), preferred_element_type=f32, precision=precision
    )


def column(row):
    wide = jnp.broadcast_to(row.astype(f32), (LANES, LANES))
    return jnp.transpose(wide, (1, 0)).astype(jnp.int32)


def forward_kernel(tm_ref, count_ref, coords_ref, flux_ref, foot_ref, out_ref, keep_ref, rhs, spread, early, sems):
    slots = foot_ref.shape[0]
    groups = slots // LANES
    per = slots // CHUNKS
    time_dev, tile_rows, width = flux_ref.shape
    across = width // LANES
    steps = time_dev * tile_rows

    def fetch(k):
        part = pl.ds(k * per, per)
        return pltpu.make_async_copy(foot_ref.at[part], keep_ref.at[part], sems.at[k])

    for k in range(CHUNKS):
        fetch(k).start()

    flux = flux_ref[...].reshape(steps, width)
    flux = jnp.concatenate([flux[:, l * LANES : (l + 1) * LANES] for l in range(across)], axis=0)
    lane = iota((LANES, LANES), 1)
    even = (lane & 1) == 0
    for g in range(groups):
        cut = slice(g * LANES, (g + 1) * LANES)
        cell = coords_ref[1:2, cut]
        code = (cell % across) * steps + coords_ref[0:1, cut] * tile_rows + cell // across
        code = column(code)
        pick = jnp.concatenate(
            [onehot(code == lane + j * LANES) for j in range(across * steps // LANES)], axis=1
        )
        piece = jnp.transpose(dot(pick, flux), (1, 0))
        rhs[g, :LANES, :] = jnp.where(even, piece, 0.0).astype(bf16)
        rhs[g, LANES:, :] = jnp.where(even, 0.0, piece).astype(bf16)

    slot = iota((1, slots), 1)
    block = jnp.where(slot < count_ref[0], coords_ref[2:3, :], -1)
    rows = out_ref.shape[0] * out_ref.shape[1]
    cols = out_ref.shape[2] // LANES

    def summed(l, low, high):
        mine = iota((rows, high - low), 0) * cols + l
        full = dot(onehot(mine == block[:, low:high]), spread[low:high, :])
        return full[:, :LANES] + full[:, LANES:]

    pair_of_lane = lane // 2
    chunks_per_group = CHUNKS // groups
    batch = 8
    for g in range(groups):
        total = jnp.zeros((LANES, LANES), f32)
        for part in range(chunks_per_group):
            fetch(g * chunks_per_group + part).wait()
            for i in range(per // (2 * batch)):
                b = g * LANES + part * per + i * 2 * batch
                blocks = keep_ref[b : b + 2 * batch].reshape(batch, 2, LANES, LANES)
                both = jnp.concatenate([blocks[:, 0], blocks[:, 1]], axis=-1)
                result = dot(both.reshape(batch * LANES, 2 * LANES), rhs[g])
                for j in range(batch):
                    p = part * (per // 2) + i * batch + j
                    total = jnp.where(pair_of_lane == p, result[j * LANES : (j + 1) * LANES], total)
        parts = split2(jnp.transpose(total, (1, 0)))
        for n in range(2):
            spread[g * LANES : (g + 1) * LANES, n * LANES : (n + 1) * LANES] = parts[n]
        if g == groups - 2:
            for l in range(cols):
                early[l] = summed(l, 0, slots - LANES)
    for l in range(cols):
        full = early[l] + summed(l, slots - LANES, slots)
        out_ref[:, :, l * LANES : (l + 1) * LANES] = full.reshape(
            out_ref.shape[0], out_ref.shape[1], LANES
        )


def forward(tm, count, coords, fluxes, footprints, devices, obs_blocks):
    per = obs_blocks // devices
    slots = footprints.shape[0]
    cols = per // 4
    vmem = pl.BlockSpec(memory_space=pltpu.VMEM)
    return pl.pallas_call(
        forward_kernel,
        out_shape=(
            jax.ShapeDtypeStruct((devices, 4, cols * LANES), f32),
            pltpu.VMEM(footprints.shape, bf16),
        ),
        in_specs=[
            pl.BlockSpec(memory_space=pltpu.SMEM),
            pl.BlockSpec(memory_space=pltpu.SMEM),
            vmem,
            vmem,
            pl.BlockSpec(memory_space=pltpu.HBM),
        ],
        out_specs=(vmem, vmem),
        scratch_shapes=[
            pltpu.VMEM((slots // LANES, 2 * LANES, LANES), bf16),
            pltpu.VMEM((slots, 2 * LANES), bf16),
            pltpu.VMEM((cols, devices * 4, LANES), f32),
            pltpu.SemaphoreType.DMA((CHUNKS,)),
        ],
        compiler_params=pltpu.CompilerParams(vmem_limit_bytes=38 * MIB),
        name="forward",
    )(tm, count, coords, fluxes, footprints)


def misfit_kernel(tm_ref, sums_ref, weight_ref, observed_ref, out_ref, half_ref):
    devices, quarter, wide = sums_ref.shape
    cols = wide // LANES
    total = jnp.sum(sums_ref[...], axis=0)
    base = tm_ref[0] * (quarter * cols)

    def own(ref):
        return jnp.concatenate(
            [ref[pl.ds(base + l, quarter, stride=cols), :] for l in range(cols)], axis=1
        )

    misfit = own(weight_ref) * (total - own(observed_ref))
    for q in range(quarter):
        for l in range(cols):
            out_ref[q * cols + l : q * cols + l + 1, :] = misfit[
                q : q + 1, l * LANES : (l + 1) * LANES
            ]
    half_ref[...] = jnp.broadcast_to(misfit[None], half_ref.shape).astype(bf16)


def misfit_of(tm, sums, weight, observed):
    devices, quarter, wide = sums.shape
    vmem = pl.BlockSpec(memory_space=pltpu.VMEM)
    return pl.pallas_call(
        misfit_kernel,
        out_shape=(
            jax.ShapeDtypeStruct((quarter * wide // LANES, LANES), f32),
            jax.ShapeDtypeStruct(sums.shape, bf16),
        ),
        in_specs=[pl.BlockSpec(memory_space=pltpu.SMEM), vmem, vmem, vmem],
        out_specs=(vmem, vmem),
        compiler_params=pltpu.CompilerParams(vmem_limit_bytes=4 * MIB),
        name="misfit",
    )(tm, sums, weight.reshape(-1, LANES), observed.reshape(-1, LANES))


def adjoint_kernel(
    count_ref,
    coords_ref,
    misfit_ref,
    foot_ref,
    diff_ref,
    main_ref,
    down_ref,
    up_ref,
    contrib,
    spread,
    rows_ref,
):
    slots = foot_ref.shape[0]
    groups = slots // LANES
    devices, quarter, wide = misfit_ref.shape
    cols = wide // LANES
    rows = devices * quarter
    tile_rows = diff_ref.shape[0]
    lane = iota((LANES, LANES), 1)
    rows_ref[...] = misfit_ref[...].astype(f32).reshape(rows, wide).astype(bf16)
    for g in range(groups):
        block = column(coords_ref[2:3, g * LANES : (g + 1) * LANES])
        chosen = jnp.zeros((LANES, LANES), f32)
        for l in range(cols):
            pick = jnp.concatenate(
                [onehot(block == (lane + j * LANES) * cols + l) for j in range(rows // LANES)], axis=1
            )
            chosen = chosen + dot(pick, rows_ref[:, l * LANES : (l + 1) * LANES])
        contrib[g * LANES : (g + 1) * LANES, :] = chosen

    batch = 16
    sub = iota((batch, LANES), 0)

    def step(i, carry):
        for half in range(2):
            at = pl.multiple_of(i * 2 * batch + half * batch, batch)
            some = contrib[pl.ds(at, batch), :]
            left = jnp.concatenate(
                [jnp.where(sub == j, some, 0.0).astype(bf16) for j in range(batch)], axis=1
            )
            blocks = foot_ref[pl.ds(at, batch)].reshape(batch * LANES, LANES)
            for n, part in enumerate(split2(dot(left, blocks))):
                spread[pl.ds(at, batch), n * LANES : (n + 1) * LANES] = part
        return carry

    lax.fori_loop(0, slots // (2 * batch), step, 0)

    time_dev = main_ref.shape[0] // tile_rows
    width = main_ref.shape[1]
    across = width // LANES
    steps = time_dev * tile_rows
    slot = iota((1, slots), 1)
    cell = coords_ref[1:2, :]
    code = coords_ref[0:1, :] * tile_rows + cell // across
    code = jnp.where(slot < count_ref[0], code, -1)
    for l in range(across):
        cut = slice(l * LANES, (l + 1) * LANES)
        pick = onehot(iota((steps, slots), 0) == jnp.where(cell % across == l, code, -1))
        full = dot(pick, spread[...])
        summed = full[:, :LANES] + full[:, LANES:]
        main_ref[:, cut] = summed.astype(bf16)
        for t in range(time_dev):
            row, at = t * tile_rows, t * SWEEPS
            down_ref[at : at + SWEEPS, cut] = summed[row + tile_rows - SWEEPS : row + tile_rows]
            up_ref[at : at + SWEEPS, cut] = summed[row : row + SWEEPS]
    down_ref[time_dev * SWEEPS :, :] = diff_ref[tile_rows - EDGE :, :]
    up_ref[time_dev * SWEEPS :, :] = diff_ref[:EDGE, :]


def adjoint_of(count, coords, misfit_rows, footprints, diffusivity, time_dev):
    slots = footprints.shape[0]
    tile_rows, width = diffusivity.shape
    devices, quarter, wide = misfit_rows.shape
    vmem = pl.BlockSpec(memory_space=pltpu.VMEM)
    edge = jax.ShapeDtypeStruct((time_dev * SWEEPS + EDGE, width), f32)
    return pl.pallas_call(
        adjoint_kernel,
        out_shape=(jax.ShapeDtypeStruct((time_dev * tile_rows, width), bf16), edge, edge),
        in_specs=[pl.BlockSpec(memory_space=pltpu.SMEM)] + [vmem] * 4,
        out_specs=(vmem, vmem, vmem),
        scratch_shapes=[
            pltpu.VMEM((slots, LANES), f32),
            pltpu.VMEM((slots, 2 * LANES), bf16),
            pltpu.VMEM((devices * quarter, wide), bf16),
        ],
        compiler_params=pltpu.CompilerParams(vmem_limit_bytes=12 * MIB),
        name="adjoint",
    )(count, coords, misfit_rows, footprints, diffusivity)


def mix_kernel(tm_ref, cov_ref, *refs):
    mains, halos, (own_ref, twin_ref) = refs[:4], refs[4:8], refs[8:]
    time_dev, ext_rows, width = own_ref.shape
    tile_rows = ext_rows - EDGE
    times = cov_ref.shape[0]
    depth, core = tm_ref[0] // 2, tm_ref[0] % 2
    block = EDGE * time_dev
    row = iota((2 * block, times), 0)
    core_of = jnp.where(row < block, core, 1 - core)
    tall = (2 * depth + core_of) * time_dev + (row % block) // EDGE == iota((2 * block, times), 1)
    col = iota((times, 4 * block), 1)
    depth_of = (depth + 4 - col // block) % 4
    broad = (2 * depth_of + core) * time_dev + (col % block) // EDGE == iota((times, 4 * block), 0)
    highest = lax.Precision.HIGHEST
    wide = dot(
        dot(onehot(tall).astype(f32), cov_ref[...], highest), onehot(broad).astype(f32), highest
    )
    same = iota(wide.shape, 0) % EDGE == iota(wide.shape, 1) % EDGE
    wide = jnp.concatenate(split2(jnp.where(same, wide, 0.0)), axis=0)

    def mixed(pieces, at):
        full = dot(wide, jnp.concatenate(pieces, axis=0).astype(bf16))
        full = full[: 2 * block] + full[2 * block :]
        for t in range(time_dev):
            own_ref[t, at : at + EDGE, :] = full[t * EDGE : (t + 1) * EDGE]
            twin_ref[t, at : at + EDGE, :] = full[block + t * EDGE : block + (t + 1) * EDGE]

    for r in range(0, tile_rows, EDGE):
        mixed(
            [
                main[u * tile_rows + r : u * tile_rows + r + EDGE, :].astype(f32)
                for main in mains
                for u in range(time_dev)
            ],
            r,
        )
    pieces = []
    for halo in halos:
        edges = halo[...].astype(f32)
        for u in range(time_dev):
            for n in (u, u + time_dev):
                pieces.append(edges[n * SWEEPS : (n + 1) * SWEEPS])
    mixed(pieces, tile_rows)


def mix(tm, cov, mains, halos, shape):
    vmem = pl.BlockSpec(memory_space=pltpu.VMEM)
    whole = jax.ShapeDtypeStruct((shape[0], shape[1] + EDGE, shape[2]), f32)
    return pl.pallas_call(
        mix_kernel,
        out_shape=(whole, whole),
        in_specs=[pl.BlockSpec(memory_space=pltpu.SMEM)] + [vmem] * 9,
        out_specs=(vmem, vmem),
        compiler_params=pltpu.CompilerParams(vmem_limit_bytes=8 * MIB),
        name="mix",
    )(tm, cov, *mains, *halos)


def diffuse_kernel(own_ref, twin_ref, before_ref, diff_ref, after_ref, out_ref, field, other):
    time_dev, tile_rows, width = out_ref.shape
    ext_rows = field.shape[1]
    first, last = 2 * EDGE, 2 * EDGE + tile_rows
    edge = before_ref.shape[0] - EDGE
    diff = jnp.concatenate([before_ref[edge:, :], diff_ref[...], after_ref[edge:, :]], axis=0)
    column_of = iota(diff.shape, 1)
    here = slice(EDGE, ext_rows - EDGE)
    for buffer in (field, other):
        for t in range(time_dev):
            buffer[t, :first, :] = jnp.zeros((first, width), f32)
            buffer[t, last:, :] = jnp.zeros((ext_rows - last, width), f32)
    for t in range(time_dev):
        field[t, first:last, :] = own_ref[t, :tile_rows, :] + twin_ref[t, :tile_rows, :]
        halo = own_ref[t, tile_rows:, :] + twin_ref[t, tile_rows:, :]
        field[t, first - SWEEPS : first, :] = halo[:SWEEPS]
        field[t, last : last + SWEEPS, :] = halo[SWEEPS:]
    source, target = field, other
    for sweep in range(SWEEPS):
        for t in range(time_dev):
            centre = source[t, here, :]
            left = jnp.where(column_of == 0, 0.0, pltpu.roll(centre, 1, 1))
            right = jnp.where(column_of == width - 1, 0.0, pltpu.roll(centre, width - 1, 1))
            above = source[t, EDGE - 1 : ext_rows - EDGE - 1, :]
            below = source[t, EDGE + 1 : ext_rows - EDGE + 1, :]
            moved = centre + diff * (below + above + right + left - 4.0 * centre)
            if sweep + 1 < SWEEPS:
                target[t, here, :] = moved
            else:
                out_ref[t] = moved[EDGE : EDGE + tile_rows]
        source, target = target, source


def diffuse(own, twin, before, diffusivity, after):
    time_dev = own.shape[0]
    tile_rows, width = diffusivity.shape
    field = pltpu.VMEM((time_dev, tile_rows + 4 * EDGE, width), f32)
    vmem = pl.BlockSpec(memory_space=pltpu.VMEM)
    return pl.pallas_call(
        diffuse_kernel,
        out_shape=jax.ShapeDtypeStruct((time_dev, tile_rows, width), f32),
        in_specs=[vmem] * 5,
        out_specs=vmem,
        scratch_shapes=[field, field],
        compiler_params=pltpu.CompilerParams(vmem_limit_bytes=8 * MIB),
        name="diffuse",
    )(own, twin, before, diffusivity, after)


def body(
    fluxes, footprints, block_coords, block_count, observed, obs_weight, time_cov, diffusivity
):
    time_dev, tile_rows, width = fluxes.shape
    n_space, n_tm = lax.axis_size("space"), lax.axis_size("tm")
    devices = n_space * n_tm
    obs_blocks = observed.shape[0] * n_space // LANES
    tm = lax.axis_index("tm").astype(jnp.int32).reshape(1)
    both = ("space", "tm")

    sums, kept = forward(tm, block_count, block_coords, fluxes, footprints, devices, obs_blocks)
    sums = lax.all_to_all(sums, both, 0, 0, tiled=True)
    misfit, halves = misfit_of(tm, sums, obs_weight, observed)
    halves = lax.all_to_all(halves, both, 0, 0, tiled=True)
    main, edge_down, edge_up = adjoint_of(
        block_count, block_coords, halves, kept, diffusivity, time_dev
    )

    def along(array, steps):
        return lax.ppermute(array, "tm", [(i, (i + 2 * steps) % n_tm) for i in range(n_tm)])

    mains = [main] + [along(main, k) for k in (1, 2, 3)]
    before = lax.ppermute(edge_down, "space", [(i, i + 1) for i in range(n_space - 1)])
    after = lax.ppermute(edge_up, "space", [(i + 1, i) for i in range(n_space - 1)])
    field_rows = time_dev * SWEEPS
    halo = jnp.concatenate([before[:field_rows], after[:field_rows]], axis=0).astype(bf16)
    halos = [halo] + [along(halo, k) for k in (1, 2, 3)]
    own, twin = mix(tm, time_cov, mains, halos, fluxes.shape)
    twin = lax.ppermute(twin, "tm", [(i, i ^ 1) for i in range(n_tm)])
    gradient = diffuse(own, twin, before, diffusivity, after)
    return misfit.reshape(-1), gradient


def solution(mesh):
    placed = (
        P("tm", "space", None),
        P(("space", "tm"), None, None),
        P(None, ("space", "tm")),
        P(("space", "tm")),
        P("space"),
        P("space"),
        P(),
        P("space", None),
    )
    return jax.shard_map(
        body,
        mesh=mesh,
        in_specs=placed,
        out_specs=(P(("space", "tm")), P("tm", "space", None)),
        check_vma=False,
    )
```

time: 319 us -> 90.8 us (0.28); the launches traced: 313 us -> 89.1 us
  waiting for transfers between devices: 182 us -> 5.93 us
  matrix products: 24.6 us -> 0 us
  Pallas kernels: 0 us -> 20.4 us
  other arithmetic: 14.4 us -> 0.01 us
  between operations: 15 us -> 1.43 us
  starting transfers between devices: 30.4 us -> 18.5 us
  local copies, waits for them, and re-layouts: 11.6 us -> 0.03 us
  blocking collectives: 35.2 us -> 42.8 us
    unnamed x3 -> x0, waiting for transfers between devices: 148 us -> none
    all_to_all x0 -> x2, blocking collectives: none -> 42.8 us  [the longest x1 26.2 us: body(): sums = lax.all_to_all(sums, both, 0, 0, tiled=True)]
    all_gather x1 -> x0, blocking collectives: 35.2 us -> none  [body(): lax.all_gather(misfit.astype(jnp.bfloat16), ('space', 'tm'), axis=0, tile...]
    all_gather x1 -> x0, waiting for transfers between devices: 31.2 us -> none  [body(): lax.all_gather(grid.reshape(time_dev, cell_blocks * 128), 'tm', axis=0, t...]
    dot_general x3 -> x0, matrix products: 24.6 us -> none  [the longest x1 12.2 us: body(): jnp.einsum('boc,bc->bo', footprints, pieces, preferred_element_type=jnp.f...]
    pallas_call x0 -> x5, Pallas kernels: none -> 20.4 us  [the longest x1 10.7 us: forward(): pl.pallas_call(forward_kernel, out_shape=(jax.ShapeDtypeStruct((devices,...]
    ppermute x8 -> x9, starting transfers between devices: 30.3 us -> 18.5 us  [the longest x6 6.6 us: along(): lax.ppermute(array, 'tm', [(i, (i + 2 * steps) % n_tm) for i in range(n_t...]
    unnamed x8 -> x10, local copies, waits for them, and re-layouts: 6.55 us -> 0.02 us
  transfers between devices with their start and end apart: 10 -> 9, of which waited for: 6 -> 5; matrix products, arithmetic and copies ran while one was open for 0% -> 0% of each run, Pallas kernels for 0% -> 0%
where the time goes in v2:
time: 90.8 us; the launch traced here: 89.1 us
  blocking collectives  42.8 us (47%)
  Pallas kernels  20.4 us (22%)
  starting transfers between devices  18.5 us (20%)
  waiting for transfers between devices  5.93 us (7%)
  between operations  1.43 us (2%)
    all_to_all x1, blocking collectives, body(): sums = lax.all_to_all(sums, both, 0, 0, tiled=True)  26.2 us
    all_to_all x1, blocking collectives, body(): halves = lax.all_to_all(halves, both, 0, 0, tiled=True)  16.6 us
    pallas_call x1, Pallas kernels, forward(): pl.pallas_call(forward_kernel, out_shape=(jax.ShapeDtypeStruct((devices,...  10.7 us
    ppermute x6, starting transfers between devices, along(): lax.ppermute(array, 'tm', [(i, (i + 2 * steps) % n_tm) for i in range(n_t...  6.6 us
    pallas_call x1, Pallas kernels, adjoint_of(): pl.pallas_call(adjoint_kernel, out_shape=(jax.ShapeDtypeStruct((time_dev...  5.39 us
    ppermute x1, starting transfers between devices, body(): lax.ppermute(edge_up, 'space', [(i + 1, i) for i in range(n_space - 1)])  4.91 us
    ppermute x1, starting transfers between devices, body(): twin = lax.ppermute(twin, 'tm', [(i, i ^ 1) for i in range(n_tm)])  4.47 us
    ppermute x6, waiting for transfers between devices, along(): lax.ppermute(array, 'tm', [(i, (i + 2 * steps) % n_tm) for i in range(n_t...  3.16 us
  transfers between devices with their start and end apart: 9, of which 5 were waited for; matrix products, arithmetic and copies ran while one was open for 0% of the time, Pallas kernels for 0%

profile of v2, /device:TPU:3, one launch (start us, length us, event | category | flops | bytes accessed | tf_op | source)
XLA Modules:
  0.0 89.1 jit_solution(15614659972601591349)
XLA Ops:
  0.6 0.0 copy-start.3
  0.6 0.0 copy-start.1
  0.7 0.0 copy-start.2
  0.7 0.0 copy-start
  1.4 0.0 copy-start.4
  1.4 10.7 %forward.1 = (f32[128,4,384]{2,1,0:T(4,128)}, bf16[512,128,128]{2,1,0:T(8,128)(2,1)S(1)}) custom-call(s32[1]{0:T(128)} %bitcast.tm_ref, s32[1]{0:T(128)S(6)} %copy.10.count_ref, s32[3,512]{1,0:T(4,128)} %coords_ref.3, bf16[4,64,512]{2,1,0:T(8,128)(2,1)} %flux_ref.1, bf16[512,128,128]{2,1,0:T(8,128)(2,1)} %foot_ref.1), custom_call_target="tpu_custom_call" | custom-call | tf_op jit(solution)/shard_map/forward/pallas_call | solution.py:116
  12.1 26.2 %all_to_all.10.sums_ref = f32[128,4,384]{2,1,0:T(4,128)S(1)} all-to-all(f32[128,4,384]{2,1,0:T(4,128)} %get-tuple-element.11), channel_id=1, replica_groups=mesh['space'=16,'tm'=8] {'space','tm'}, dimensions={0} | all-to-all | bytes 1572864 | tf_op jit(solution)/shard_map/all_to_all | solution.py:386
  38.3 0.0 copy-done.1
  38.3 0.8 misfit.1
  39.1 16.6 %all_to_all.11.misfit_ref = bf16[128,4,384]{2,1,0:T(4,128)(2,1)S(1)} all-to-all(bf16[128,4,384]{2,1,0:T(4,128)(2,1)S(1)} %get-tuple-element.13), channel_id=1, replica_groups=mesh['space'=16,'tm'=8] {'space','tm'}, dimensions={0} | all-to-all | bytes 786432 | tf_op jit(solution)/shard_map/all_to_all | solution.py:388
  55.7 5.4 %adjoint.1 = (bf16[256,512]{1,0:T(8,128)(2,1)S(1)}, f32[24,512]{1,0:T(8,128)S(1)}, f32[24,512]{1,0:T(8,128)S(1)}) custom-call(s32[1]{0:T(128)S(6)} %copy.10.count_ref, s32[3,512]{1,0:T(4,128)S(1)} %copy-done.3, bf16[128,4,384]{2,1,0:T(4,128)(2,1)S(1)} %all_to_all.11.misfit_ref, bf16[512,128,128]{2,1,0:T(8,128)(2,1)S(1)} %get-tuple-element.14.foot_ref, ...), custom_call_target="tpu_custom_call" | custom-call | tf_op jit(solution)/shard_map/adjoint/pallas_call | solution.py:253
  61.1 1.1 %collective-permute-start.2 = (bf16[256,512]{1,0:T(8,128)(2,1)S(1)}, bf16[256,512]{1,0:T(8,128)(2,1)S(1)}, u32[]{:S(2)}, u32[]{:S(2)}) collective-permute-start(bf16[256,512]{1,0:T(8,128)(2,1)S(1)} %get-tuple-element.15.refs_0_), channel_id=1, source_target_pairs={{0,6},{1,7},{2,0},{3,1},{4,2},{5,3},{6,4},{7,5},{8,14},{9,15},{10,... | collective-permute-start | bytes 786440 | tf_op jit(solution)/shard_map/ppermute | solution.py:394
  62.2 0.5 collective-permute-start.1
  62.7 0.3 collective-permute-start
  63.0 2.5 %collective-permute-start.3 = (f32[24,512]{1,0:T(8,128)S(1)}, f32[24,512]{1,0:T(8,128)S(1)}, u32[]{:S(2)}, u32[]{:S(2)}) collective-permute-start(f32[24,512]{1,0:T(8,128)S(1)} %get-tuple-element.16), channel_id=1, source_target_pairs={{0,8},{8,16},{16,24},{24,32},{32,40},{40,48},{48,56},{56,64},{64,7... | collective-permute-start | bytes 147464 | tf_op jit(solution)/shard_map/ppermute | solution.py:397
  65.5 4.9 %collective-permute-start.4 = (f32[24,512]{1,0:T(8,128)S(1)}, f32[24,512]{1,0:T(8,128)S(1)}, u32[]{:S(2)}, u32[]{:S(2)}) collective-permute-start(f32[24,512]{1,0:T(8,128)S(1)} %get-tuple-element.17), channel_id=1, source_target_pairs={{8,0},{16,8},{24,16},{32,24},{40,32},{48,40},{56,48},{64,56},{72,6... | collective-permute-start | bytes 147464 | tf_op jit(solution)/shard_map/ppermute | solution.py:398
  70.4 0.0 collective-permute-done.3.before_ref
  70.4 1.1 %collective-permute-done.4.after_ref = f32[24,512]{1,0:T(8,128)S(1)} collective-permute-done((f32[24,512]{1,0:T(8,128)S(1)}, f32[24,512]{1,0:T(8,128)S(1)}, u32[]{:S(2)}, u32[]{:S(2)}) %collective-permute-start.4) | collective-permute-done | bytes 49184 | tf_op jit(solution)/shard_map/ppermute | solution.py:398
  71.6 2.4 %collective-permute-start.7 = (bf16[32,512]{1,0:T(8,128)(2,1)S(1)}, bf16[32,512]{1,0:T(8,128)(2,1)S(1)}, u32[]{:S(2)}, u32[]{:S(2)}) collective-permute-start(bf16[32,512]{1,0:T(8,128)(2,1)S(1)} %pad_maximum_fusion.refs_4_), channel_id=1, source_target_pairs={{0,6},{1,7},{2,0},{3,1},{4,2},{5,3},{6,4},{7,5},{8,14},{9,15},{10,... | collective-permute-start | bytes 98312 | tf_op jit(solution)/shard_map/ppermute | solution.py:394
  74.0 1.3 %collective-permute-start.6 = (bf16[32,512]{1,0:T(8,128)(2,1)S(1)}, bf16[32,512]{1,0:T(8,128)(2,1)S(1)}, u32[]{:S(2)}, u32[]{:S(2)}) collective-permute-start(bf16[32,512]{1,0:T(8,128)(2,1)S(1)} %pad_maximum_fusion.refs_4_), channel_id=1, source_target_pairs={{0,4},{1,5},{2,6},{3,7},{4,0},{5,1},{6,2},{7,3},{8,12},{9,13},{10,... | collective-permute-start | bytes 98312 | tf_op jit(solution)/shard_map/ppermute | solution.py:394
  75.3 0.2 collective-permute-done.7.refs_7_
  75.5 1.0 %collective-permute-start.5 = (bf16[32,512]{1,0:T(8,128)(2,1)S(1)}, bf16[32,512]{1,0:T(8,128)(2,1)S(1)}, u32[]{:S(2)}, u32[]{:S(2)}) collective-permute-start(bf16[32,512]{1,0:T(8,128)(2,1)S(1)} %pad_maximum_fusion.refs_4_), channel_id=1, source_target_pairs={{0,2},{1,3},{2,4},{3,5},{4,6},{5,7},{6,0},{7,1},{8,10},{9,11},{10,... | collective-permute-start | bytes 98312 | tf_op jit(solution)/shard_map/ppermute | solution.py:394
  76.5 1.7 %collective-permute-done.6.refs_6_ = bf16[32,512]{1,0:T(8,128)(2,1)S(1)} collective-permute-done((bf16[32,512]{1,0:T(8,128)(2,1)S(1)}, bf16[32,512]{1,0:T(8,128)(2,1)S(1)}, u32[]{:S(2)}, u32[]{:S(2)}) %collective-permute-start.6) | collective-permute-done | bytes 32800 | tf_op jit(solution)/shard_map/ppermute | solution.py:394
  78.2 1.2 %collective-permute-done.5.refs_5_ = bf16[32,512]{1,0:T(8,128)(2,1)S(1)} collective-permute-done((bf16[32,512]{1,0:T(8,128)(2,1)S(1)}, bf16[32,512]{1,0:T(8,128)(2,1)S(1)}, u32[]{:S(2)}, u32[]{:S(2)}) %collective-permute-start.5) | collective-permute-done | bytes 32800 | tf_op jit(solution)/shard_map/ppermute | solution.py:394
  79.5 0.0 collective-permute-done.2.refs_3_
  79.5 0.0 collective-permute-done.1.refs_2_
  79.5 0.0 collective-permute-done.refs_1_
  79.5 0.0 copy-done.4
  79.5 0.8 mix.1
  80.3 4.5 %collective-permute-start.8 = (f32[4,72,512]{2,1,0:T(8,128)S(1)}, f32[4,72,512]{2,1,0:T(8,128)S(1)}, u32[]{:S(2)}, u32[]{:S(2)}) collective-permute-start(f32[4,72,512]{2,1,0:T(8,128)S(1)} %get-tuple-element.19), channel_id=1, source_target_pairs={{0,1},{1,0},{2,3},{3,2},{4,5},{5,4},{6,7},{7,6},{8,9},{9,8},{10,11... | collective-permute-start | bytes 1769480 | tf_op jit(solution)/shard_map/ppermute | solution.py:403
  84.7 1.6 %collective-permute-done.8.twin_ref = f32[4,72,512]{2,1,0:T(8,128)S(1)} collective-permute-done((f32[4,72,512]{2,1,0:T(8,128)S(1)}, f32[4,72,512]{2,1,0:T(8,128)S(1)}, u32[]{:S(2)}, u32[]{:S(2)}) %collective-permute-start.8) | collective-permute-done | bytes 589856 | tf_op jit(solution)/shard_map/ppermute | solution.py:403
  86.4 2.7 %diffuse.1 = f32[4,64,512]{2,1,0:T(8,128)} custom-call(f32[4,72,512]{2,1,0:T(8,128)S(1)} %get-tuple-element.18.own_ref, f32[4,72,512]{2,1,0:T(8,128)S(1)} %collective-permute-done.8.twin_ref, f32[24,512]{1,0:T(8,128)S(1)} %collective-permute-done.3.before_ref, f32[64,512]{1,0:T(8,128)S(1)} %copy-done, f32[24,512]{1,0:T(8,128)S(1)} %collective-permute-done.4.after_ref), custom_call_target="tpu_custom_call" | custom-call | tf_op jit(solution)/shard_map/diffuse/pallas_call | solution.py:364
  (6 shorter events, 0.0 us)
Async XLA Ops:
  0.6 55.1 %copy-start.3 = (s32[3,512]{1,0:T(4,128)S(1)}, s32[3,512]{1,0:T(4,128)}, u32[]{:S(2)}) copy-start(s32[3,512]{1,0:T(4,128)} %coords_ref.3) | copy-start | bytes 18436
  0.6 37.7 %copy-start.1 = (f32[12288]{0:T(1024)S(1)}, f32[12288]{0:T(1024)}, u32[]{:S(2)}) copy-start(f32[12288]{0:T(1024)} %param.13) | copy-start | bytes 147460
  0.7 37.7 %copy-start.2 = (f32[12288]{0:T(1024)S(1)}, f32[12288]{0:T(1024)}, u32[]{:S(2)}) copy-start(f32[12288]{0:T(1024)} %param.12) | copy-start | bytes 147460
  0.7 55.1 %copy-start = (f32[64,512]{1,0:T(8,128)S(1)}, f32[64,512]{1,0:T(8,128)}, u32[]{:S(2)}) copy-start(f32[64,512]{1,0:T(8,128)} %diff_ref.3) | copy-start | bytes 393220
  1.4 78.1 %copy-start.4 = (f32[32,32]{1,0:T(8,128)S(1)}, f32[32,32]{1,0:T(8,128)}, u32[]{:S(2)}) copy-start(f32[32,32]{1,0:T(8,128)} %cov_ref.1) | copy-start | bytes 12292
  61.1 18.3 %collective-permute-start.2 = (bf16[256,512]{1,0:T(8,128)(2,1)S(1)}, bf16[256,512]{1,0:T(8,128)(2,1)S(1)}, u32[]{:S(2)}, u32[]{:S(2)}) collective-permute-start(bf16[256,512]{1,0:T(8,128)(2,1)S(1)} %get-tuple-element.15.refs_0_), channel_id=1, source_target_pairs={{0,6},{1,7},{2,0},{3,1},{4,2},{5,3},{6,4},{7,5},{8,14},{9,15},{10,... | collective-permute-start | bytes 786440 | tf_op jit(solution)/shard_map/ppermute | solution.py:394
  62.2 17.3 %collective-permute-start.1 = (bf16[256,512]{1,0:T(8,128)(2,1)S(1)}, bf16[256,512]{1,0:T(8,128)(2,1)S(1)}, u32[]{:S(2)}, u32[]{:S(2)}) collective-permute-start(bf16[256,512]{1,0:T(8,128)(2,1)S(1)} %get-tuple-element.15.refs_0_), channel_id=1, source_target_pairs={{0,4},{1,5},{2,6},{3,7},{4,0},{5,1},{6,2},{7,3},{8,12},{9,13},{10,... | collective-permute-start | bytes 786440 | tf_op jit(solution)/shard_map/ppermute | solution.py:394
  62.7 16.8 %collective-permute-start = (bf16[256,512]{1,0:T(8,128)(2,1)S(1)}, bf16[256,512]{1,0:T(8,128)(2,1)S(1)}, u32[]{:S(2)}, u32[]{:S(2)}) collective-permute-start(bf16[256,512]{1,0:T(8,128)(2,1)S(1)} %get-tuple-element.15.refs_0_), channel_id=1, source_target_pairs={{0,2},{1,3},{2,4},{3,5},{4,6},{5,7},{6,0},{7,1},{8,10},{9,11},{10,... | collective-permute-start | bytes 786440 | tf_op jit(solution)/shard_map/ppermute | solution.py:394
  63.0 7.4 %collective-permute-start.3 = (f32[24,512]{1,0:T(8,128)S(1)}, f32[24,512]{1,0:T(8,128)S(1)}, u32[]{:S(2)}, u32[]{:S(2)}) collective-permute-start(f32[24,512]{1,0:T(8,128)S(1)} %get-tuple-element.16), channel_id=1, source_target_pairs={{0,8},{8,16},{16,24},{24,32},{32,40},{40,48},{48,56},{56,64},{64,7... | collective-permute-start | bytes 147464 | tf_op jit(solution)/shard_map/ppermute | solution.py:397
  65.5 6.1 %collective-permute-start.4 = (f32[24,512]{1,0:T(8,128)S(1)}, f32[24,512]{1,0:T(8,128)S(1)}, u32[]{:S(2)}, u32[]{:S(2)}) collective-permute-start(f32[24,512]{1,0:T(8,128)S(1)} %get-tuple-element.17), channel_id=1, source_target_pairs={{8,0},{16,8},{24,16},{32,24},{40,32},{48,40},{56,48},{64,56},{72,6... | collective-permute-start | bytes 147464 | tf_op jit(solution)/shard_map/ppermute | solution.py:398
  71.6 3.9 %collective-permute-start.7 = (bf16[32,512]{1,0:T(8,128)(2,1)S(1)}, bf16[32,512]{1,0:T(8,128)(2,1)S(1)}, u32[]{:S(2)}, u32[]{:S(2)}) collective-permute-start(bf16[32,512]{1,0:T(8,128)(2,1)S(1)} %pad_maximum_fusion.refs_4_), channel_id=1, source_target_pairs={{0,6},{1,7},{2,0},{3,1},{4,2},{5,3},{6,4},{7,5},{8,14},{9,15},{10,... | collective-permute-start | bytes 98312 | tf_op jit(solution)/shard_map/ppermute | solution.py:394
  74.0 4.3 %collective-permute-start.6 = (bf16[32,512]{1,0:T(8,128)(2,1)S(1)}, bf16[32,512]{1,0:T(8,128)(2,1)S(1)}, u32[]{:S(2)}, u32[]{:S(2)}) collective-permute-start(bf16[32,512]{1,0:T(8,128)(2,1)S(1)} %pad_maximum_fusion.refs_4_), channel_id=1, source_target_pairs={{0,4},{1,5},{2,6},{3,7},{4,0},{5,1},{6,2},{7,3},{8,12},{9,13},{10,... | collective-permute-start | bytes 98312 | tf_op jit(solution)/shard_map/ppermute | solution.py:394
  75.5 4.0 %collective-permute-start.5 = (bf16[32,512]{1,0:T(8,128)(2,1)S(1)}, bf16[32,512]{1,0:T(8,128)(2,1)S(1)}, u32[]{:S(2)}, u32[]{:S(2)}) collective-permute-start(bf16[32,512]{1,0:T(8,128)(2,1)S(1)} %pad_maximum_fusion.refs_4_), channel_id=1, source_target_pairs={{0,2},{1,3},{2,4},{3,5},{4,6},{5,7},{6,0},{7,1},{8,10},{9,11},{10,... | collective-permute-start | bytes 98312 | tf_op jit(solution)/shard_map/ppermute | solution.py:394
  80.3 6.1 %collective-permute-start.8 = (f32[4,72,512]{2,1,0:T(8,128)S(1)}, f32[4,72,512]{2,1,0:T(8,128)S(1)}, u32[]{:S(2)}, u32[]{:S(2)}) collective-permute-start(f32[4,72,512]{2,1,0:T(8,128)S(1)} %get-tuple-element.19), channel_id=1, source_target_pairs={{0,1},{1,0},{2,3},{3,2},{4,5},{5,4},{6,7},{7,6},{8,9},{9,8},{10,11... | collective-permute-start | bytes 1769480 | tf_op jit(solution)/shard_map/ppermute | solution.py:403

commit v3 on v2

v3 whole, which is shorter than its diff:
```python
import jax
import jax.numpy as jnp
from jax import lax
from jax.experimental import pallas as pl
from jax.experimental.pallas import tpu as pltpu
from jax.sharding import PartitionSpec as P

SWEEPS = 4
LANES = 128
EDGE = 8
MIB = 1024 * 1024

f32 = jnp.float32
bf16 = jnp.bfloat16


def split2(x):
    hi = x.astype(bf16)
    return hi, (x - hi.astype(f32)).astype(bf16)


def iota(shape, dim):
    return lax.broadcasted_iota(jnp.int32, shape, dim)


def onehot(equal):
    return jnp.where(equal, 1.0, 0.0).astype(bf16)


def dot(a, b, precision=None):
    return lax.dot_general(
        a, b, (((1,), (0,)), ((), ())), preferred_element_type=f32, precision=precision
    )


def column(row):
    wide = jnp.broadcast_to(row.astype(f32), (LANES, LANES))
    return jnp.transpose(wide, (1, 0)).astype(jnp.int32)


def forward_kernel(
    tm_ref,
    count_ref,
    coords_hbm,
    flux_hbm,
    foot_ref,
    out_ref,
    keep_ref,
    coords_ref,
    flux_ref,
    rhs,
    spread,
    early,
    sems,
    small_sems,
):
    slots = foot_ref.shape[0]
    groups = slots // LANES
    time_dev, tile_rows, width = flux_ref.shape
    across = width // LANES
    steps = time_dev * tile_rows
    bounds = [0] + list(range(LANES // 2, slots, LANES)) + [slots]
    chunks = len(bounds) - 1

    def fetch(k):
        part = pl.ds(bounds[k], bounds[k + 1] - bounds[k])
        return pltpu.make_async_copy(foot_ref.at[part], keep_ref.at[part], sems.at[k])

    small = (
        pltpu.make_async_copy(coords_hbm, coords_ref, small_sems.at[0]),
        pltpu.make_async_copy(flux_hbm, flux_ref, small_sems.at[1]),
    )
    for copy in small:
        copy.start()
    fetch(0).start()
    fetch(1).start()
    for copy in small:
        copy.wait()

    flux = flux_ref[...].reshape(steps, width)
    flux = jnp.concatenate([flux[:, l * LANES : (l + 1) * LANES] for l in range(across)], axis=0)
    lane = iota((LANES, LANES), 1)
    even = (lane & 1) == 0
    for g in range(groups):
        cut = slice(g * LANES, (g + 1) * LANES)
        cell = coords_ref[1:2, cut]
        code = (cell % across) * steps + coords_ref[0:1, cut] * tile_rows + cell // across
        code = column(code)
        pick = jnp.concatenate(
            [onehot(code == lane + j * LANES) for j in range(across * steps // LANES)], axis=1
        )
        piece = jnp.transpose(dot(pick, flux), (1, 0))
        rhs[g, :LANES, :] = jnp.where(even, piece, 0.0).astype(bf16)
        rhs[g, LANES:, :] = jnp.where(even, 0.0, piece).astype(bf16)

    slot = iota((1, slots), 1)
    block = jnp.where(slot < count_ref[0], coords_ref[2:3, :], -1)
    rows = out_ref.shape[0] * out_ref.shape[1]
    cols = out_ref.shape[2] // LANES

    def summed(l, low, high):
        mine = iota((rows, high - low), 0) * cols + l
        full = dot(onehot(mine == block[:, low:high]), spread[low:high, :])
        return full[:, :LANES] + full[:, LANES:]

    pair_of_lane = lane // 2
    batch = 8
    total = None
    for k in range(chunks):
        fetch(k).wait()
        if k + 2 < chunks:
            fetch(k + 2).start()
        for b in range(bounds[k], bounds[k + 1], 2 * batch):
            g = b // LANES
            if b % LANES == 0:
                total = jnp.zeros((LANES, LANES), f32)
            blocks = keep_ref[b : b + 2 * batch].reshape(batch, 2, LANES, LANES)
            both = jnp.concatenate([blocks[:, 0], blocks[:, 1]], axis=-1)
            result = dot(both.reshape(batch * LANES, 2 * LANES), rhs[g])
            for j in range(batch):
                p = (b % LANES) // 2 + j
                total = jnp.where(pair_of_lane == p, result[j * LANES : (j + 1) * LANES], total)
            if (b + 2 * batch) % LANES == 0:
                for n, part in enumerate(split2(jnp.transpose(total, (1, 0)))):
                    spread[g * LANES : (g + 1) * LANES, n * LANES : (n + 1) * LANES] = part
                if g == groups - 2:
                    for l in range(cols):
                        early[l] = summed(l, 0, slots - LANES)
    for l in range(cols):
        full = early[l] + summed(l, slots - LANES, slots)
        out_ref[:, :, l * LANES : (l + 1) * LANES] = full.reshape(
            out_ref.shape[0], out_ref.shape[1], LANES
        )


def forward(tm, count, coords, fluxes, footprints, devices, obs_blocks):
    per = obs_blocks // devices
    slots = footprints.shape[0]
    cols = per // 4
    vmem = pl.BlockSpec(memory_space=pltpu.VMEM)
    smem = pl.BlockSpec(memory_space=pltpu.SMEM)
    hbm = pl.BlockSpec(memory_space=pltpu.HBM)
    return pl.pallas_call(
        forward_kernel,
        out_shape=(
            pltpu.VMEM((devices, 4, cols * LANES), f32),
            pltpu.VMEM(footprints.shape, bf16),
        ),
        in_specs=[smem, smem, hbm, hbm, hbm],
        out_specs=(vmem, vmem),
        scratch_shapes=[
            pltpu.VMEM(coords.shape, jnp.int32),
            pltpu.VMEM(fluxes.shape, bf16),
            pltpu.VMEM((slots // LANES, 2 * LANES, LANES), bf16),
            pltpu.VMEM((slots, 2 * LANES), bf16),
            pltpu.VMEM((cols, devices * 4, LANES), f32),
            pltpu.SemaphoreType.DMA((slots // LANES + 1,)),
            pltpu.SemaphoreType.DMA((2,)),
        ],
        compiler_params=pltpu.CompilerParams(vmem_limit_bytes=38 * MIB),
        name="forward",
    )(tm, count, coords, fluxes, footprints)


def misfit_kernel(tm_ref, sums_ref, weight_ref, observed_ref, out_ref, half_ref):
    devices, quarter, wide = sums_ref.shape
    cols = wide // LANES
    total = jnp.sum(sums_ref[...], axis=0)
    base = tm_ref[0] * (quarter * cols)

    def own(ref):
        return jnp.concatenate(
            [ref[pl.ds(base + l, quarter, stride=cols), :] for l in range(cols)], axis=1
        )

    misfit = own(weight_ref) * (total - own(observed_ref))
    for q in range(quarter):
        for l in range(cols):
            out_ref[q * cols + l : q * cols + l + 1, :] = misfit[
                q : q + 1, l * LANES : (l + 1) * LANES
            ]
    half_ref[...] = jnp.broadcast_to(misfit[None], half_ref.shape).astype(bf16)


def misfit_of(tm, sums, weight, observed):
    devices, quarter, wide = sums.shape
    vmem = pl.BlockSpec(memory_space=pltpu.VMEM)
    return pl.pallas_call(
        misfit_kernel,
        out_shape=(
            jax.ShapeDtypeStruct((quarter * wide // LANES, LANES), f32),
            jax.ShapeDtypeStruct(sums.shape, bf16),
        ),
        in_specs=[pl.BlockSpec(memory_space=pltpu.SMEM), vmem, vmem, vmem],
        out_specs=(vmem, vmem),
        compiler_params=pltpu.CompilerParams(vmem_limit_bytes=4 * MIB),
        name="misfit",
    )(tm, sums, weight.reshape(-1, LANES), observed.reshape(-1, LANES))


def adjoint_kernel(
    tm_ref,
    count_ref,
    coords_ref,
    misfit_ref,
    foot_ref,
    diff_ref,
    main_ref,
    mine_ref,
    other_ref,
    contrib,
    spread,
    rows_ref,
):
    slots = foot_ref.shape[0]
    groups = slots // LANES
    devices, quarter, wide = misfit_ref.shape
    cols = wide // LANES
    rows = devices * quarter
    tile_rows = diff_ref.shape[0]
    lane = iota((LANES, LANES), 1)
    rows_ref[...] = misfit_ref[...].astype(f32).reshape(rows, wide).astype(bf16)
    for g in range(groups):
        block = column(coords_ref[2:3, g * LANES : (g + 1) * LANES])
        chosen = jnp.zeros((LANES, LANES), f32)
        for l in range(cols):
            pick = jnp.concatenate(
                [onehot(block == (lane + j * LANES) * cols + l) for j in range(rows // LANES)], axis=1
            )
            chosen = chosen + dot(pick, rows_ref[:, l * LANES : (l + 1) * LANES])
        contrib[g * LANES : (g + 1) * LANES, :] = chosen

    batch = 16
    sub = iota((batch, LANES), 0)
    for at in range(0, slots, batch):
        some = contrib[at : at + batch, :]
        left = jnp.concatenate(
            [jnp.where(sub == j, some, 0.0).astype(bf16) for j in range(batch)], axis=1
        )
        blocks = foot_ref[at : at + batch].reshape(batch * LANES, LANES)
        for n, part in enumerate(split2(dot(left, blocks))):
            spread[at : at + batch, n * LANES : (n + 1) * LANES] = part

    time_dev = main_ref.shape[0] // tile_rows
    width = main_ref.shape[1]
    across = width // LANES
    steps = time_dev * tile_rows
    first_core = tm_ref[0] % 2 == 0
    slot = iota((1, slots), 1)
    cell = coords_ref[1:2, :]
    code = coords_ref[0:1, :] * tile_rows + cell // across
    code = jnp.where(slot < count_ref[0], code, -1)
    for l in range(across):
        cut = slice(l * LANES, (l + 1) * LANES)
        pick = onehot(iota((steps, slots), 0) == jnp.where(cell % across == l, code, -1))
        full = dot(pick, spread[...])
        summed = full[:, :LANES] + full[:, LANES:]
        main_ref[:, cut] = summed.astype(bf16)
        for t in range(time_dev):
            row, at = t * tile_rows, t * SWEEPS
            down = summed[row + tile_rows - SWEEPS : row + tile_rows]
            up = summed[row : row + SWEEPS]
            mine_ref[at : at + SWEEPS, cut] = jnp.where(first_core, down, up)
            other_ref[at : at + SWEEPS, cut] = jnp.where(first_core, up, down)
    mine_ref[time_dev * SWEEPS :, :] = jnp.where(
        first_core, diff_ref[tile_rows - EDGE :, :], diff_ref[:EDGE, :]
    )


def adjoint_of(tm, count, coords, misfit_rows, footprints, diffusivity, time_dev):
    slots = footprints.shape[0]
    tile_rows, width = diffusivity.shape
    devices, quarter, wide = misfit_rows.shape
    edge = time_dev * SWEEPS
    vmem = pl.BlockSpec(memory_space=pltpu.VMEM)
    smem = pl.BlockSpec(memory_space=pltpu.SMEM)
    return pl.pallas_call(
        adjoint_kernel,
        out_shape=(
            jax.ShapeDtypeStruct((time_dev * tile_rows, width), bf16),
            jax.ShapeDtypeStruct((edge + EDGE, width), f32),
            jax.ShapeDtypeStruct((edge, width), f32),
        ),
        in_specs=[smem, smem, vmem, vmem, vmem, vmem],
        out_specs=(vmem, vmem, vmem),
        scratch_shapes=[
            pltpu.VMEM((slots, LANES), f32),
            pltpu.VMEM((slots, 2 * LANES), bf16),
            pltpu.VMEM((devices * quarter, wide), bf16),
        ],
        compiler_params=pltpu.CompilerParams(vmem_limit_bytes=12 * MIB),
        name="adjoint",
    )(tm, count, coords, misfit_rows, footprints, diffusivity)


def spread_cov(cov, row_time, col_time, per):
    times = cov.shape[0]
    rows, cols = row_time.shape[0], col_time.shape[1]
    tall = onehot(row_time == iota((rows, times), 1)).astype(f32)
    broad = onehot(col_time == iota((times, cols), 0)).astype(f32)
    highest = lax.Precision.HIGHEST
    wide = dot(dot(tall, cov, highest), broad, highest)
    same = iota((rows, cols), 0) % per == iota((rows, cols), 1) % per
    return jnp.concatenate(split2(jnp.where(same, wide, 0.0)), axis=0)


def mix_kernel(tm_ref, cov_ref, *refs):
    mains, halos, received_ref, (own_ref, twin_ref) = refs[:4], refs[4:8], refs[8], refs[9:]
    time_dev, ext_rows, width = own_ref.shape
    tile_rows = ext_rows - EDGE
    times = cov_ref.shape[0]
    depth, core = tm_ref[0] // 2, tm_ref[0] % 2

    def target_time(per):
        row = iota((2 * time_dev * per, times), 0)
        core_of = jnp.where(row < time_dev * per, core, 1 - core)
        return (2 * depth + core_of) * time_dev + row % (time_dev * per) // per

    def depth_of(col, block):
        return (depth + 4 - col // block) % 4

    def put(full, at, count):
        half = full.shape[0] // 2
        full = full[:half] + full[half:]
        for t in range(time_dev):
            row = t * count
            own_ref[t, at : at + count, :] = full[row : row + count]
            row += time_dev * count
            twin_ref[t, at : at + count, :] = full[row : row + count]

    block = EDGE * time_dev
    col = iota((times, 4 * block), 1)
    source = (2 * depth_of(col, block) + core) * time_dev + col % block // EDGE
    wide = spread_cov(cov_ref[...], target_time(EDGE), source, EDGE)
    for r in range(0, tile_rows, EDGE):
        pieces = [
            main[u * tile_rows + r : u * tile_rows + r + EDGE, :].astype(f32)
            for main in mains
            for u in range(time_dev)
        ]
        put(dot(wide, jnp.concatenate(pieces, axis=0).astype(bf16)), r, EDGE)

    half = SWEEPS * time_dev
    col = iota((times, 8 * half), 1)
    core_of = jnp.where(col % (2 * half) < half, 1 - core, core)
    source = (2 * depth_of(col, 2 * half) + core_of) * time_dev + col % half // SWEEPS
    wide = spread_cov(cov_ref[...], target_time(SWEEPS), source, SWEEPS)
    edges = jnp.concatenate([halo[...] for halo in halos], axis=0)
    put(dot(wide, edges), tile_rows, SWEEPS)
    for t in range(time_dev):
        n = 2 * half + (t % 2) * SWEEPS
        for ref in (own_ref, twin_ref):
            ref[t, tile_rows + SWEEPS :, :] = received_ref[n : n + SWEEPS, :]


def mix(tm, cov, mains, halos, received, shape):
    vmem = pl.BlockSpec(memory_space=pltpu.VMEM)
    whole = jax.ShapeDtypeStruct((shape[0], shape[1] + EDGE, shape[2]), f32)
    return pl.pallas_call(
        mix_kernel,
        out_shape=(whole, whole),
        in_specs=[pl.BlockSpec(memory_space=pltpu.SMEM)] + [vmem] * 10,
        out_specs=(vmem, vmem),
        compiler_params=pltpu.CompilerParams(vmem_limit_bytes=8 * MIB),
        name="mix",
    )(tm, cov, *mains, *halos, received)


def diffuse_kernel(tm_ref, own_ref, twin_ref, diff_ref, out_ref, field, other):
    time_dev, tile_rows, width = out_ref.shape
    ext_rows = field.shape[1]
    first, last = 2 * EDGE, 2 * EDGE + tile_rows
    first_core = tm_ref[0] % 2 == 0
    lower = tile_rows + SWEEPS

    def halo_of(ref):
        return jnp.concatenate([ref[0, lower:, :], ref[1, lower:, :]], axis=0)

    def ordered(a, b):
        return jnp.where(first_core, a, b), jnp.where(first_core, b, a)

    before, after = ordered(halo_of(own_ref), halo_of(twin_ref))
    diff = jnp.concatenate([before, diff_ref[...], after], axis=0)
    column_of = iota(diff.shape, 1)
    here = slice(EDGE, ext_rows - EDGE)
    for buffer in (field, other):
        for t in range(time_dev):
            buffer[t, :first, :] = jnp.zeros((first, width), f32)
            buffer[t, last:, :] = jnp.zeros((ext_rows - last, width), f32)
    for t in range(time_dev):
        field[t, first:last, :] = own_ref[t, :tile_rows, :] + twin_ref[t, :tile_rows, :]
        above, below = ordered(own_ref[t, tile_rows:lower, :], twin_ref[t, tile_rows:lower, :])
        field[t, first - SWEEPS : first, :] = above
        field[t, last : last + SWEEPS, :] = below
    source, target = field, other
    for sweep in range(SWEEPS):
        for t in range(time_dev):
            centre = source[t, here, :]
            left = jnp.where(column_of == 0, 0.0, pltpu.roll(centre, 1, 1))
            right = jnp.where(column_of == width - 1, 0.0, pltpu.roll(centre, width - 1, 1))
            above = source[t, EDGE - 1 : ext_rows - EDGE - 1, :]
            below = source[t, EDGE + 1 : ext_rows - EDGE + 1, :]
            moved = centre + diff * (below + above + right + left - 4.0 * centre)
            if sweep + 1 < SWEEPS:
                target[t, here, :] = moved
            else:
                out_ref[t] = moved[EDGE : EDGE + tile_rows]
        source, target = target, source


def diffuse(tm, own, twin, diffusivity):
    time_dev = own.shape[0]
    tile_rows, width = diffusivity.shape
    field = pltpu.VMEM((time_dev, tile_rows + 4 * EDGE, width), f32)
    vmem = pl.BlockSpec(memory_space=pltpu.VMEM)
    return pl.pallas_call(
        diffuse_kernel,
        out_shape=jax.ShapeDtypeStruct((time_dev, tile_rows, width), f32),
        in_specs=[pl.BlockSpec(memory_space=pltpu.SMEM)] + [vmem] * 3,
        out_specs=vmem,
        scratch_shapes=[field, field],
        compiler_params=pltpu.CompilerParams(vmem_limit_bytes=8 * MIB),
        name="diffuse",
    )(tm, own, twin, diffusivity)


def body(
    fluxes, footprints, block_coords, block_count, observed, obs_weight, time_cov, diffusivity
):
    time_dev, tile_rows, width = fluxes.shape
    n_space, n_tm = lax.axis_size("space"), lax.axis_size("tm")
    devices = n_space * n_tm
    obs_blocks = observed.shape[0] * n_space // LANES
    tm = lax.axis_index("tm").astype(jnp.int32).reshape(1)
    both = ("space", "tm")

    sums, kept = forward(tm, block_count, block_coords, fluxes, footprints, devices, obs_blocks)
    sums = lax.all_to_all(sums, both, 0, 0, tiled=True)
    misfit, halves = misfit_of(tm, sums, obs_weight, observed)
    halves = lax.all_to_all(halves, both, 0, 0, tiled=True)
    main, mine, other = adjoint_of(
        tm, block_count, block_coords, halves, kept, diffusivity, time_dev
    )

    def along(array, steps):
        return lax.ppermute(array, "tm", [(i, (i + 2 * steps) % n_tm) for i in range(n_tm)])

    swap = [(i, i ^ 1) for i in range(n_tm)]
    other = lax.ppermute(other, "tm", swap)
    mains = [main] + [along(main, k) for k in (1, 2, 3)]
    moves = []
    for s in range(n_space - 1):
        for t in range(0, n_tm, 2):
            moves.append((s * n_tm + t, (s + 1) * n_tm + t))
            moves.append(((s + 1) * n_tm + t + 1, s * n_tm + t + 1))
    received = lax.ppermute(jnp.concatenate([other, mine], axis=0), both, moves)
    halo = received[: 2 * time_dev * SWEEPS].astype(bf16)
    halo, mains[3] = lax.optimization_barrier((halo, mains[3]))
    halos = [halo] + [along(halo, k) for k in (1, 2, 3)]
    own, twin = mix(tm, time_cov, mains, halos, received, fluxes.shape)
    twin = lax.ppermute(twin, "tm", swap)
    gradient = diffuse(tm, own, twin, diffusivity)
    return misfit.reshape(-1), gradient


def solution(mesh):
    placed = (
        P("tm", "space", None),
        P(("space", "tm"), None, None),
        P(None, ("space", "tm")),
        P(("space", "tm")),
        P("space"),
        P("space"),
        P(),
        P("space", None),
    )
    return jax.shard_map(
        body,
        mesh=mesh,
        in_specs=placed,
        out_specs=(P(("space", "tm")), P("tm", "space", None)),
        check_vma=False,
    )
```

time: 90.8 us -> 85.5 us (0.942); the launches traced: 89.1 us -> 85.3 us
  Pallas kernels: 20.4 us -> 17 us
  starting transfers between devices: 18.5 us -> 17 us
  waiting for transfers between devices: 5.93 us -> 7.16 us
    pallas_call x1, Pallas kernels: 5.39 us -> 3.31 us  [adjoint_of(): pl.pallas_call(adjoint_kernel, out_shape=(jax.ShapeDtypeStruct((time_dev...]
    pallas_call x1, Pallas kernels: 10.7 us -> 9.13 us  [forward(): pl.pallas_call(forward_kernel, out_shape=(pltpu.VMEM((devices, 4, cols *...]
    ppermute x3, starting transfers between devices: 11.9 us -> 10.3 us  [the longest x1 4.82 us: body(): twin = lax.ppermute(twin, 'tm', swap)]
    ppermute x3, waiting for transfers between devices: 2.77 us -> 3.95 us  [the longest x1 1.63 us: body(): twin = lax.ppermute(twin, 'tm', swap)]
  transfers between devices with their start and end apart: 9 -> 9, of which waited for: 5 -> 6; matrix products, arithmetic and copies ran while one was open for 0% -> 0% of each run, Pallas kernels for 0% -> 0%
where the time goes in v3:
time: 85.5 us; the launch traced here: 85.3 us
  blocking collectives  42.6 us (50%)
  Pallas kernels  17 us (20%)
  starting transfers between devices  17 us (20%)
  waiting for transfers between devices  7.16 us (8%)
  between operations  1.41 us (2%)
    all_to_all x1, blocking collectives, body(): sums = lax.all_to_all(sums, both, 0, 0, tiled=True)  26 us
    all_to_all x1, blocking collectives, body(): halves = lax.all_to_all(halves, both, 0, 0, tiled=True)  16.6 us
    pallas_call x1, Pallas kernels, forward(): pl.pallas_call(forward_kernel, out_shape=(pltpu.VMEM((devices, 4, cols *...  9.13 us
    ppermute x6, starting transfers between devices, along(): lax.ppermute(array, 'tm', [(i, (i + 2 * steps) % n_tm) for i in range(n_t...  6.7 us
    ppermute x1, starting transfers between devices, body(): twin = lax.ppermute(twin, 'tm', swap)  4.82 us
    ppermute x1, starting transfers between devices, body(): received = lax.ppermute(jnp.concatenate([other, mine], axis=0), both, moves)  4.1 us
    pallas_call x1, Pallas kernels, adjoint_of(): pl.pallas_call(adjoint_kernel, out_shape=(jax.ShapeDtypeStruct((time_dev...  3.31 us
    ppermute x6, waiting for transfers between devices, along(): lax.ppermute(array, 'tm', [(i, (i + 2 * steps) % n_tm) for i in range(n_t...  3.21 us
  transfers between devices with their start and end apart: 9, of which 6 were waited for; matrix products, arithmetic and copies ran while one was open for 0% of the time, Pallas kernels for 0%

profile of v3, /device:TPU:3, one launch (start us, length us, event | category | flops | bytes accessed | tf_op | source)
XLA Modules:
  0.0 85.3 jit_solution(5211147338989939318)
XLA Ops:
  0.6 0.0 copy-start.3
  0.6 0.0 copy-start.1
  0.7 0.0 copy-start.2
  0.7 0.0 copy-start
  1.4 0.0 copy-start.4
  1.4 9.1 %forward.1 = (f32[128,4,384]{2,1,0:T(4,128)S(1)}, bf16[512,128,128]{2,1,0:T(8,128)(2,1)S(1)}) custom-call(s32[1]{0:T(128)} %bitcast.tm_ref, s32[1]{0:T(128)S(6)} %copy.10.count_ref, s32[3,512]{1,0:T(4,128)} %coords_ref.1, bf16[4,64,512]{2,1,0:T(8,128)(2,1)} %flux_hbm.1, bf16[512,128,128]{2,1,0:T(8,128)(2,1)} %foot_ref.1), custom_call_target="tpu_custom_call" | custom-call | tf_op jit(solution)/shard_map/forward/pallas_call | solution.py:143
  10.5 26.0 %all_to_all.10.sums_ref = f32[128,4,384]{2,1,0:T(4,128)S(1)} all-to-all(f32[128,4,384]{2,1,0:T(4,128)S(1)} %get-tuple-element.13), channel_id=1, replica_groups=mesh['space'=16,'tm'=8] {'space','tm'}, dimensions={0} | all-to-all | bytes 1572864 | tf_op jit(solution)/shard_map/all_to_all | solution.py:438
  36.5 0.0 copy-done.1
  36.6 0.8 misfit.1
  37.3 16.6 %all_to_all.11.misfit_ref = bf16[128,4,384]{2,1,0:T(4,128)(2,1)S(1)} all-to-all(bf16[128,4,384]{2,1,0:T(4,128)(2,1)S(1)} %get-tuple-element.15), channel_id=1, replica_groups=mesh['space'=16,'tm'=8] {'space','tm'}, dimensions={0} | all-to-all | bytes 786432 | tf_op jit(solution)/shard_map/all_to_all | solution.py:440
  54.0 3.3 %adjoint.1 = (bf16[256,512]{1,0:T(8,128)(2,1)S(1)}, f32[24,512]{1,0:T(8,128)S(1)}, f32[16,512]{1,0:T(8,128)S(1)}) custom-call(s32[1]{0:T(128)} %bitcast.tm_ref, s32[1]{0:T(128)S(6)} %copy.10.count_ref, s32[3,512]{1,0:T(4,128)S(1)} %copy-done.3, bf16[128,4,384]{2,1,0:T(4,128)(2,1)S(1)} %all_to_all.11.misfit_ref, ...), custom_call_target="tpu_custom_call" | custom-call | tf_op jit(solution)/shard_map/adjoint/pallas_call | solution.py:277
  57.3 1.0 %collective-permute-start.4 = (bf16[256,512]{1,0:T(8,128)(2,1)S(1)}, bf16[256,512]{1,0:T(8,128)(2,1)S(1)}, u32[]{:S(2)}, u32[]{:S(2)}) collective-permute-start(bf16[256,512]{1,0:T(8,128)(2,1)S(1)} %get-tuple-element.17.refs_0_), channel_id=1, source_target_pairs={{0,6},{1,7},{2,0},{3,1},{4,2},{5,3},{6,4},{7,5},{8,14},{9,15},{10,... | collective-permute-start | bytes 786440 | tf_op jit(solution)/shard_map/ppermute | solution.py:446
  58.3 0.5 collective-permute-start.1
  58.8 0.3 collective-permute-start
  59.1 1.4 %collective-permute-start.2 = (f32[16,512]{1,0:T(8,128)S(1)}, f32[16,512]{1,0:T(8,128)S(1)}, u32[]{:S(2)}, u32[]{:S(2)}) collective-permute-start(f32[16,512]{1,0:T(8,128)S(1)} %get-tuple-element.18), channel_id=1, source_target_pairs={{0,1},{1,0},{2,3},{3,2},{4,5},{5,4},{6,7},{7,6},{8,9},{9,8},{10,11... | collective-permute-start | bytes 98312 | tf_op jit(solution)/shard_map/ppermute | solution.py:449
  60.5 0.9 %collective-permute-done.2 = f32[16,512]{1,0:T(8,128)S(1)} collective-permute-done((f32[16,512]{1,0:T(8,128)S(1)}, f32[16,512]{1,0:T(8,128)S(1)}, u32[]{:S(2)}, u32[]{:S(2)}) %collective-permute-start.2) | collective-permute-done | bytes 32800 | tf_op jit(solution)/shard_map/ppermute | solution.py:449
  61.4 4.1 %collective-permute-start.3 = (f32[40,512]{1,0:T(8,128)S(1)}, f32[40,512]{1,0:T(8,128)S(1)}, u32[]{:S(2)}, u32[]{:S(2)}) collective-permute-start(f32[40,512]{1,0:T(8,128)S(1)} %pad_maximum_fusion), channel_id=1, source_target_pairs={{0,8},{9,1},{2,10},{11,3},{4,12},{13,5},{6,14},{15,7},{8,16},{17,9... | collective-permute-start | bytes 245768 | tf_op jit(solution)/shard_map/ppermute | solution.py:456
  65.5 1.5 %collective-permute-done.3.refs_8_ = f32[40,512]{1,0:T(8,128)S(1)} collective-permute-done((f32[40,512]{1,0:T(8,128)S(1)}, f32[40,512]{1,0:T(8,128)S(1)}, u32[]{:S(2)}, u32[]{:S(2)}) %collective-permute-start.3) | collective-permute-done | bytes 81952 | tf_op jit(solution)/shard_map/ppermute | solution.py:456
  67.0 0.0 collective-permute-done.4.refs_3_
  67.0 2.7 %collective-permute-start.7 = (bf16[32,512]{1,0:T(8,128)(2,1)S(1)}, bf16[32,512]{1,0:T(8,128)(2,1)S(1)}, u32[]{:S(2)}, u32[]{:S(2)}) collective-permute-start(bf16[32,512]{1,0:T(8,128)(2,1)S(1)} %slice.7.refs_4_), channel_id=1, source_target_pairs={{0,6},{1,7},{2,0},{3,1},{4,2},{5,3},{6,4},{7,5},{8,14},{9,15},{10,... | collective-permute-start | bytes 98312 | tf_op jit(solution)/shard_map/ppermute | solution.py:446
  69.7 1.4 %collective-permute-start.6 = (bf16[32,512]{1,0:T(8,128)(2,1)S(1)}, bf16[32,512]{1,0:T(8,128)(2,1)S(1)}, u32[]{:S(2)}, u32[]{:S(2)}) collective-permute-start(bf16[32,512]{1,0:T(8,128)(2,1)S(1)} %slice.7.refs_4_), channel_id=1, source_target_pairs={{0,4},{1,5},{2,6},{3,7},{4,0},{5,1},{6,2},{7,3},{8,12},{9,13},{10,... | collective-permute-start | bytes 98312 | tf_op jit(solution)/shard_map/ppermute | solution.py:446
  71.1 0.8 collective-permute-start.5
  71.8 0.0 collective-permute-done.1.refs_2_
  71.8 1.8 %collective-permute-done.refs_1_ = bf16[256,512]{1,0:T(8,128)(2,1)S(1)} collective-permute-done((bf16[256,512]{1,0:T(8,128)(2,1)S(1)}, bf16[256,512]{1,0:T(8,128)(2,1)S(1)}, u32[]{:S(2)}, u32[]{:S(2)}) %collective-permute-start) | collective-permute-done | bytes 262176 | tf_op jit(solution)/shard_map/ppermute | solution.py:446
  73.7 0.0 collective-permute-done.7.refs_7_
  73.7 0.3 collective-permute-done.6.refs_6_
  73.9 1.1 %collective-permute-done.5.refs_5_ = bf16[32,512]{1,0:T(8,128)(2,1)S(1)} collective-permute-done((bf16[32,512]{1,0:T(8,128)(2,1)S(1)}, bf16[32,512]{1,0:T(8,128)(2,1)S(1)}, u32[]{:S(2)}, u32[]{:S(2)}) %collective-permute-start.5) | collective-permute-done | bytes 32800 | tf_op jit(solution)/shard_map/ppermute | solution.py:446
  75.0 0.0 copy-done.4
  75.1 1.0 %mix.1 = (f32[4,72,512]{2,1,0:T(8,128)S(1)}, f32[4,72,512]{2,1,0:T(8,128)S(1)}) custom-call(s32[1]{0:T(128)} %bitcast.tm_ref, f32[32,32]{1,0:T(8,128)S(1)} %copy-done.4, bf16[256,512]{1,0:T(8,128)(2,1)S(1)} %get-tuple-element.17.refs_0_, bf16[256,512]{1,0:T(8,128)(2,1)S(1)} %collective-permute-done.refs_1_, ...), custom_call_target="tpu_custom_call" | custom-call | tf_op jit(solution)/shard_map/mix/pallas_call | solution.py:359
  76.1 4.8 %collective-permute-start.8 = (f32[4,72,512]{2,1,0:T(8,128)S(1)}, f32[4,72,512]{2,1,0:T(8,128)S(1)}, u32[]{:S(2)}, u32[]{:S(2)}) collective-permute-start(f32[4,72,512]{2,1,0:T(8,128)S(1)} %get-tuple-element.23), channel_id=1, source_target_pairs={{0,1},{1,0},{2,3},{3,2},{4,5},{5,4},{6,7},{7,6},{8,9},{9,8},{10,11... | collective-permute-start | bytes 1769480 | tf_op jit(solution)/shard_map/ppermute | solution.py:461
  80.9 1.6 %collective-permute-done.8.twin_ref = f32[4,72,512]{2,1,0:T(8,128)S(1)} collective-permute-done((f32[4,72,512]{2,1,0:T(8,128)S(1)}, f32[4,72,512]{2,1,0:T(8,128)S(1)}, u32[]{:S(2)}, u32[]{:S(2)}) %collective-permute-start.8) | collective-permute-done | bytes 589856 | tf_op jit(solution)/shard_map/ppermute | solution.py:461
  82.6 2.7 %diffuse.1 = f32[4,64,512]{2,1,0:T(8,128)} custom-call(s32[1]{0:T(128)} %bitcast.tm_ref, f32[4,72,512]{2,1,0:T(8,128)S(1)} %get-tuple-element.22.own_ref, f32[4,72,512]{2,1,0:T(8,128)S(1)} %collective-permute-done.8.twin_ref, f32[64,512]{1,0:T(8,128)S(1)} %copy-done), custom_call_target="tpu_custom_call" | custom-call | tf_op jit(solution)/shard_map/diffuse/pallas_call | solution.py:416
  (5 shorter events, 0.0 us)
Async XLA Ops:
  0.6 53.3 %copy-start.3 = (s32[3,512]{1,0:T(4,128)S(1)}, s32[3,512]{1,0:T(4,128)}, u32[]{:S(2)}) copy-start(s32[3,512]{1,0:T(4,128)} %coords_ref.1) | copy-start | bytes 18436
  0.6 35.9 %copy-start.1 = (f32[12288]{0:T(1024)S(1)}, f32[12288]{0:T(1024)}, u32[]{:S(2)}) copy-start(f32[12288]{0:T(1024)} %param.13) | copy-start | bytes 147460
  0.7 35.9 %copy-start.2 = (f32[12288]{0:T(1024)S(1)}, f32[12288]{0:T(1024)}, u32[]{:S(2)}) copy-start(f32[12288]{0:T(1024)} %param.12) | copy-start | bytes 147460
  0.7 53.3 %copy-start = (f32[64,512]{1,0:T(8,128)S(1)}, f32[64,512]{1,0:T(8,128)}, u32[]{:S(2)}) copy-start(f32[64,512]{1,0:T(8,128)} %diff_ref.3) | copy-start | bytes 393220
  1.4 73.7 %copy-start.4 = (f32[32,32]{1,0:T(8,128)S(1)}, f32[32,32]{1,0:T(8,128)}, u32[]{:S(2)}) copy-start(f32[32,32]{1,0:T(8,128)} %cov_ref.1) | copy-start | bytes 12292
  57.3 9.7 %collective-permute-start.4 = (bf16[256,512]{1,0:T(8,128)(2,1)S(1)}, bf16[256,512]{1,0:T(8,128)(2,1)S(1)}, u32[]{:S(2)}, u32[]{:S(2)}) collective-permute-start(bf16[256,512]{1,0:T(8,128)(2,1)S(1)} %get-tuple-element.17.refs_0_), channel_id=1, source_target_pairs={{0,6},{1,7},{2,0},{3,1},{4,2},{5,3},{6,4},{7,5},{8,14},{9,15},{10,... | collective-permute-start | bytes 786440 | tf_op jit(solution)/shard_map/ppermute | solution.py:446
  58.3 13.5 %collective-permute-start.1 = (bf16[256,512]{1,0:T(8,128)(2,1)S(1)}, bf16[256,512]{1,0:T(8,128)(2,1)S(1)}, u32[]{:S(2)}, u32[]{:S(2)}) collective-permute-start(bf16[256,512]{1,0:T(8,128)(2,1)S(1)} %get-tuple-element.17.refs_0_), channel_id=1, source_target_pairs={{0,4},{1,5},{2,6},{3,7},{4,0},{5,1},{6,2},{7,3},{8,12},{9,13},{10,... | collective-permute-start | bytes 786440 | tf_op jit(solution)/shard_map/ppermute | solution.py:446
  58.8 14.9 %collective-permute-start = (bf16[256,512]{1,0:T(8,128)(2,1)S(1)}, bf16[256,512]{1,0:T(8,128)(2,1)S(1)}, u32[]{:S(2)}, u32[]{:S(2)}) collective-permute-start(bf16[256,512]{1,0:T(8,128)(2,1)S(1)} %get-tuple-element.17.refs_0_), channel_id=1, source_target_pairs={{0,2},{1,3},{2,4},{3,5},{4,6},{5,7},{6,0},{7,1},{8,10},{9,11},{10,... | collective-permute-start | bytes 786440 | tf_op jit(solution)/shard_map/ppermute | solution.py:446
  59.1 2.3 %collective-permute-start.2 = (f32[16,512]{1,0:T(8,128)S(1)}, f32[16,512]{1,0:T(8,128)S(1)}, u32[]{:S(2)}, u32[]{:S(2)}) collective-permute-start(f32[16,512]{1,0:T(8,128)S(1)} %get-tuple-element.18), channel_id=1, source_target_pairs={{0,1},{1,0},{2,3},{3,2},{4,5},{5,4},{6,7},{7,6},{8,9},{9,8},{10,11... | collective-permute-start | bytes 98312 | tf_op jit(solution)/shard_map/ppermute | solution.py:449
  61.4 5.6 %collective-permute-start.3 = (f32[40,512]{1,0:T(8,128)S(1)}, f32[40,512]{1,0:T(8,128)S(1)}, u32[]{:S(2)}, u32[]{:S(2)}) collective-permute-start(f32[40,512]{1,0:T(8,128)S(1)} %pad_maximum_fusion), channel_id=1, source_target_pairs={{0,8},{9,1},{2,10},{11,3},{4,12},{13,5},{6,14},{15,7},{8,16},{17,9... | collective-permute-start | bytes 245768 | tf_op jit(solution)/shard_map/ppermute | solution.py:456
  67.0 6.7 %collective-permute-start.7 = (bf16[32,512]{1,0:T(8,128)(2,1)S(1)}, bf16[32,512]{1,0:T(8,128)(2,1)S(1)}, u32[]{:S(2)}, u32[]{:S(2)}) collective-permute-start(bf16[32,512]{1,0:T(8,128)(2,1)S(1)} %slice.7.refs_4_), channel_id=1, source_target_pairs={{0,6},{1,7},{2,0},{3,1},{4,2},{5,3},{6,4},{7,5},{8,14},{9,15},{10,... | collective-permute-start | bytes 98312 | tf_op jit(solution)/shard_map/ppermute | solution.py:446
  69.7 4.3 %collective-permute-start.6 = (bf16[32,512]{1,0:T(8,128)(2,1)S(1)}, bf16[32,512]{1,0:T(8,128)(2,1)S(1)}, u32[]{:S(2)}, u32[]{:S(2)}) collective-permute-start(bf16[32,512]{1,0:T(8,128)(2,1)S(1)} %slice.7.refs_4_), channel_id=1, source_target_pairs={{0,4},{1,5},{2,6},{3,7},{4,0},{5,1},{6,2},{7,3},{8,12},{9,13},{10,... | collective-permute-start | bytes 98312 | tf_op jit(solution)/shard_map/ppermute | solution.py:446
  71.1 4.0 %collective-permute-start.5 = (bf16[32,512]{1,0:T(8,128)(2,1)S(1)}, bf16[32,512]{1,0:T(8,128)(2,1)S(1)}, u32[]{:S(2)}, u32[]{:S(2)}) collective-permute-start(bf16[32,512]{1,0:T(8,128)(2,1)S(1)} %slice.7.refs_4_), channel_id=1, source_target_pairs={{0,2},{1,3},{2,4},{3,5},{4,6},{5,7},{6,0},{7,1},{8,10},{9,11},{10,... | collective-permute-start | bytes 98312 | tf_op jit(solution)/shard_map/ppermute | solution.py:446
  76.1 6.5 %collective-permute-start.8 = (f32[4,72,512]{2,1,0:T(8,128)S(1)}, f32[4,72,512]{2,1,0:T(8,128)S(1)}, u32[]{:S(2)}, u32[]{:S(2)}) collective-permute-start(f32[4,72,512]{2,1,0:T(8,128)S(1)} %get-tuple-element.23), channel_id=1, source_target_pairs={{0,1},{1,0},{2,3},{3,2},{4,5},{5,4},{6,7},{7,6},{8,9},{9,8},{10,11... | collective-permute-start | bytes 1769480 | tf_op jit(solution)/shard_map/ppermute | solution.py:461

commit v4 on v3

--- a/solution.py
+++ b/solution.py
@@ -44,7 +44,8 @@
     coords_hbm,
     flux_hbm,
     foot_ref,
-    out_ref,
+    mine_ref,
+    other_ref,
     keep_ref,
     coords_ref,
     flux_ref,
@@ -95,12 +96,15 @@
 
     slot = iota((1, slots), 1)
     block = jnp.where(slot < count_ref[0], coords_ref[2:3, :], -1)
-    rows = out_ref.shape[0] * out_ref.shape[1]
-    cols = out_ref.shape[2] // LANES
-
-    def summed(l, low, high):
-        mine = iota((rows, high - low), 0) * cols + l
-        full = dot(onehot(mine == block[:, low:high]), spread[low:high, :])
+    chips, quarter, wide = mine_ref.shape
+    cols = wide // LANES
+    core = tm_ref[0] % 2
+
+    def summed(n, low, high):
+        row = iota((chips * quarter, high - low), 0)
+        owner = row // quarter * 2 + (core if n < cols else 1 - core)
+        row = (owner * quarter + row % quarter) * cols + n % cols
+        full = dot(onehot(row == block[:, low:high]), spread[low:high, :])
         return full[:, :LANES] + full[:, LANES:]
 
     pair_of_lane = lane // 2
@@ -124,13 +128,12 @@
                 for n, part in enumerate(split2(jnp.transpose(total, (1, 0)))):
                     spread[g * LANES : (g + 1) * LANES, n * LANES : (n + 1) * LANES] = part
                 if g == groups - 2:
-                    for l in range(cols):
-                        early[l] = summed(l, 0, slots - LANES)
-    for l in range(cols):
-        full = early[l] + summed(l, slots - LANES, slots)
-        out_ref[:, :, l * LANES : (l + 1) * LANES] = full.reshape(
-            out_ref.shape[0], out_ref.shape[1], LANES
-        )
+                    for n in range(2 * cols):
+                        early[n] = summed(n, 0, slots - LANES)
+    for n in range(2 * cols):
+        full = early[n] + summed(n, slots - LANES, slots)
+        ref = mine_ref if n < cols else other_ref
+        ref[:, :, n % cols * LANES : (n % cols + 1) * LANES] = full.reshape(chips, quarter, LANES)
 
 
 def forward(tm, count, coords, fluxes, footprints, devices, obs_blocks):
@@ -143,17 +146,18 @@
     return pl.pallas_call(
         forward_kernel,
         out_shape=(
-            pltpu.VMEM((devices, 4, cols * LANES), f32),
+            pltpu.VMEM((devices // 2, 4, cols * LANES), f32),
+            pltpu.VMEM((devices // 2, 4, cols * LANES), f32),
             pltpu.VMEM(footprints.shape, bf16),
         ),
         in_specs=[smem, smem, hbm, hbm, hbm],
-        out_specs=(vmem, vmem),
+        out_specs=(vmem, vmem, vmem),
         scratch_shapes=[
             pltpu.VMEM(coords.shape, jnp.int32),
             pltpu.VMEM(fluxes.shape, bf16),
             pltpu.VMEM((slots // LANES, 2 * LANES, LANES), bf16),
             pltpu.VMEM((slots, 2 * LANES), bf16),
-            pltpu.VMEM((cols, devices * 4, LANES), f32),
+            pltpu.VMEM((2 * cols, devices * 2, LANES), f32),
             pltpu.SemaphoreType.DMA((slots // LANES + 1,)),
             pltpu.SemaphoreType.DMA((2,)),
         ],
@@ -189,7 +193,7 @@
         misfit_kernel,
         out_shape=(
             jax.ShapeDtypeStruct((quarter * wide // LANES, LANES), f32),
-            jax.ShapeDtypeStruct(sums.shape, bf16),
+            jax.ShapeDtypeStruct((2 * devices, quarter, wide), bf16),
         ),
         in_specs=[pl.BlockSpec(memory_space=pltpu.SMEM), vmem, vmem, vmem],
         out_specs=(vmem, vmem),
@@ -434,8 +438,13 @@
     tm = lax.axis_index("tm").astype(jnp.int32).reshape(1)
     both = ("space", "tm")
 
-    sums, kept = forward(tm, block_count, block_coords, fluxes, footprints, devices, obs_blocks)
-    sums = lax.all_to_all(sums, both, 0, 0, tiled=True)
+    swap = [(i, i ^ 1) for i in range(n_tm)]
+    parity = [list(range(n, devices, 2)) for n in range(2)]
+    sums, other, kept = forward(
+        tm, block_count, block_coords, fluxes, footprints, devices, obs_blocks
+    )
+    sums = sums + lax.ppermute(other, "tm", swap)
+    sums = lax.all_to_all(sums, both, 0, 0, axis_index_groups=parity, tiled=True)
     misfit, halves = misfit_of(tm, sums, obs_weight, observed)
     halves = lax.all_to_all(halves, both, 0, 0, tiled=True)
     main, mine, other = adjoint_of(
@@ -445,7 +454,6 @@
     def along(array, steps):
         return lax.ppermute(array, "tm", [(i, (i + 2 * steps) % n_tm) for i in range(n_tm)])
 
-    swap = [(i, i ^ 1) for i in range(n_tm)]
     other = lax.ppermute(other, "tm", swap)
     mains = [main] + [along(main, k) for k in (1, 2, 3)]
     moves = []

time: 85.5 us -> 83.1 us (0.972)
  blocking collectives: 42.6 us -> 38.3 us
  waiting for transfers between devices: 7.16 us -> 8.51 us
    all_to_all x1, blocking collectives: 26 us -> 21 us  [body(): lax.all_to_all(sums, both, 0, 0, axis_index_groups=parity, tiled=True)]
    ppermute x0 -> x1, waiting for transfers between devices: none -> 1.35 us  [body(): sums = sums + lax.ppermute(other, 'tm', swap)]
  transfers between devices with their start and end apart: 9 -> 10, of which waited for: 6 -> 7; matrix products, arithmetic and copies ran while one was open for 0% -> 0% of each run, Pallas kernels for 0% -> 0%
where the time goes in v4:
time: 83.1 us; the launch traced here: 82.9 us
  blocking collectives  38.3 us (46%)
  starting transfers between devices  17.6 us (21%)
  Pallas kernels  16.9 us (20%)
  waiting for transfers between devices  8.51 us (10%)
  between operations  1.42 us (2%)
    all_to_all x1, blocking collectives, body(): lax.all_to_all(sums, both, 0, 0, axis_index_groups=parity, tiled=True)  21 us
    all_to_all x1, blocking collectives, body(): halves = lax.all_to_all(halves, both, 0, 0, tiled=True)  17.3 us
    pallas_call x1, Pallas kernels, forward(): pl.pallas_call(forward_kernel, out_shape=(pltpu.VMEM((devices // 2, 4, co...  9.06 us
    ppermute x6, starting transfers between devices, along(): lax.ppermute(array, 'tm', [(i, (i + 2 * steps) % n_tm) for i in range(n_t...  6.5 us
    ppermute x1, starting transfers between devices, body(): twin = lax.ppermute(twin, 'tm', swap)  4.83 us
    ppermute x1, starting transfers between devices, body(): received = lax.ppermute(jnp.concatenate([other, mine], axis=0), both, moves)  4.1 us
    pallas_call x1, Pallas kernels, adjoint_of(): pl.pallas_call(adjoint_kernel, out_shape=(jax.ShapeDtypeStruct((time_dev...  3.32 us
    ppermute x6, waiting for transfers between devices, along(): lax.ppermute(array, 'tm', [(i, (i + 2 * steps) % n_tm) for i in range(n_t...  3.21 us
  transfers between devices with their start and end apart: 10, of which 7 were waited for; matrix products, arithmetic and copies ran while one was open for 0% of the time, Pallas kernels for 0%

profile of v4, /device:TPU:3, one launch (start us, length us, event | category | flops | bytes accessed | tf_op | source)
XLA Modules:
  0.0 82.9 jit_solution(3314452640407063715)
XLA Ops:
  0.6 0.0 copy-start.3
  0.6 0.0 copy-start.1
  0.7 0.0 copy-start.2
  0.7 0.0 copy-start
  1.4 9.1 %forward.1 = (f32[64,4,384]{2,1,0:T(4,128)S(1)}, f32[64,4,384]{2,1,0:T(4,128)S(1)}, bf16[512,128,128]{2,1,0:T(8,128)(2,1)S(1)}) custom-call(s32[1]{0:T(128)} %bitcast.tm_ref, s32[1]{0:T(128)S(6)} %copy.10.count_ref, s32[3,512]{1,0:T(4,128)} %coords_ref.1, bf16[4,64,512]{2,1,0:T(8,128)(2,1)} %flux_hbm.1, bf16[512,128,128]{2,1,0:T(8,128)(2,1)} %foot_ref.1), custom_call_target="tpu_custom_call" | custom-call | tf_op jit(solution)/shard_map/forward/pallas_call | solution.py:146
  10.4 0.8 collective-permute-start
  11.2 1.3 %collective-permute-done = f32[64,4,384]{2,1,0:T(4,128)S(1)} collective-permute-done((f32[64,4,384]{2,1,0:T(4,128)S(1)}, f32[64,4,384]{2,1,0:T(4,128)S(1)}, u32[]{:S(2)}, u32[]{:S(2)}) %collective-permute-start) | collective-permute-done | bytes 393248 | tf_op jit(solution)/shard_map/ppermute | solution.py:446
  12.5 0.1 add.3
  12.6 21.0 %all_to_all.10.sums_ref = f32[64,4,384]{2,1,0:T(4,128)S(1)} all-to-all(f32[64,4,384]{2,1,0:T(4,128)S(1)} %add.3), channel_id=1, replica_groups={{0,2,4,6,8,10,12,14,16,18,20,22,24,26,28,30,32,34,36,38,40,42,44,46,48,..., dimensions={0} | all-to-all | bytes 786432 | tf_op jit(solution)/shard_map/all_to_all | solution.py:447
  33.7 0.7 misfit.1
  34.4 17.3 %all_to_all.11.misfit_ref = bf16[128,4,384]{2,1,0:T(4,128)(2,1)S(1)} all-to-all(bf16[128,4,384]{2,1,0:T(4,128)(2,1)S(1)} %get-tuple-element.17), channel_id=1, replica_groups=mesh['space'=16,'tm'=8] {'space','tm'}, dimensions={0} | all-to-all | bytes 786432 | tf_op jit(solution)/shard_map/all_to_all | solution.py:449
  51.7 3.3 %adjoint.1 = (bf16[256,512]{1,0:T(8,128)(2,1)S(1)}, f32[24,512]{1,0:T(8,128)S(1)}, f32[16,512]{1,0:T(8,128)S(1)}) custom-call(s32[1]{0:T(128)} %bitcast.tm_ref, s32[1]{0:T(128)S(6)} %copy.10.count_ref, s32[3,512]{1,0:T(4,128)S(1)} %copy-done.3, bf16[128,4,384]{2,1,0:T(4,128)(2,1)S(1)} %all_to_all.11.misfit_ref, ...), custom_call_target="tpu_custom_call" | custom-call | tf_op jit(solution)/shard_map/adjoint/pallas_call | solution.py:281
  55.0 1.0 %collective-permute-start.5 = (bf16[256,512]{1,0:T(8,128)(2,1)S(1)}, bf16[256,512]{1,0:T(8,128)(2,1)S(1)}, u32[]{:S(2)}, u32[]{:S(2)}) collective-permute-start(bf16[256,512]{1,0:T(8,128)(2,1)S(1)} %get-tuple-element.19.refs_0_), channel_id=1, source_target_pairs={{0,6},{1,7},{2,0},{3,1},{4,2},{5,3},{6,4},{7,5},{8,14},{9,15},{10,... | collective-permute-start | bytes 786440 | tf_op jit(solution)/shard_map/ppermute | solution.py:455
  56.1 0.5 collective-permute-start.2
  56.5 0.3 collective-permute-start.1
  56.8 1.4 %collective-permute-start.3 = (f32[16,512]{1,0:T(8,128)S(1)}, f32[16,512]{1,0:T(8,128)S(1)}, u32[]{:S(2)}, u32[]{:S(2)}) collective-permute-start(f32[16,512]{1,0:T(8,128)S(1)} %get-tuple-element.20), channel_id=1, source_target_pairs={{0,1},{1,0},{2,3},{3,2},{4,5},{5,4},{6,7},{7,6},{8,9},{9,8},{10,11... | collective-permute-start | bytes 98312 | tf_op jit(solution)/shard_map/ppermute | solution.py:457
  58.3 0.9 %collective-permute-done.3 = f32[16,512]{1,0:T(8,128)S(1)} collective-permute-done((f32[16,512]{1,0:T(8,128)S(1)}, f32[16,512]{1,0:T(8,128)S(1)}, u32[]{:S(2)}, u32[]{:S(2)}) %collective-permute-start.3) | collective-permute-done | bytes 32800 | tf_op jit(solution)/shard_map/ppermute | solution.py:457
  59.1 4.1 %collective-permute-start.4 = (f32[40,512]{1,0:T(8,128)S(1)}, f32[40,512]{1,0:T(8,128)S(1)}, u32[]{:S(2)}, u32[]{:S(2)}) collective-permute-start(f32[40,512]{1,0:T(8,128)S(1)} %pad_maximum_fusion), channel_id=1, source_target_pairs={{0,8},{9,1},{2,10},{11,3},{4,12},{13,5},{6,14},{15,7},{8,16},{17,9... | collective-permute-start | bytes 245768 | tf_op jit(solution)/shard_map/ppermute | solution.py:464
  63.2 1.5 %collective-permute-done.4.refs_8_ = f32[40,512]{1,0:T(8,128)S(1)} collective-permute-done((f32[40,512]{1,0:T(8,128)S(1)}, f32[40,512]{1,0:T(8,128)S(1)}, u32[]{:S(2)}, u32[]{:S(2)}) %collective-permute-start.4) | collective-permute-done | bytes 81952 | tf_op jit(solution)/shard_map/ppermute | solution.py:464
  64.7 0.0 collective-permute-done.5.refs_3_
  64.7 2.5 %collective-permute-start.8 = (bf16[32,512]{1,0:T(8,128)(2,1)S(1)}, bf16[32,512]{1,0:T(8,128)(2,1)S(1)}, u32[]{:S(2)}, u32[]{:S(2)}) collective-permute-start(bf16[32,512]{1,0:T(8,128)(2,1)S(1)} %slice.7.refs_4_), channel_id=1, source_target_pairs={{0,6},{1,7},{2,0},{3,1},{4,2},{5,3},{6,4},{7,5},{8,14},{9,15},{10,... | collective-permute-start | bytes 98312 | tf_op jit(solution)/shard_map/ppermute | solution.py:455
  67.2 1.4 %collective-permute-start.7 = (bf16[32,512]{1,0:T(8,128)(2,1)S(1)}, bf16[32,512]{1,0:T(8,128)(2,1)S(1)}, u32[]{:S(2)}, u32[]{:S(2)}) collective-permute-start(bf16[32,512]{1,0:T(8,128)(2,1)S(1)} %slice.7.refs_4_), channel_id=1, source_target_pairs={{0,4},{1,5},{2,6},{3,7},{4,0},{5,1},{6,2},{7,3},{8,12},{9,13},{10,... | collective-permute-start | bytes 98312 | tf_op jit(solution)/shard_map/ppermute | solution.py:455
  68.6 0.8 collective-permute-start.6
  69.4 0.0 collective-permute-done.2.refs_2_
  69.4 2.0 %collective-permute-done.1.refs_1_ = bf16[256,512]{1,0:T(8,128)(2,1)S(1)} collective-permute-done((bf16[256,512]{1,0:T(8,128)(2,1)S(1)}, bf16[256,512]{1,0:T(8,128)(2,1)S(1)}, u32[]{:S(2)}, u32[]{:S(2)}) %collective-permute-start.1) | collective-permute-done | bytes 262176 | tf_op jit(solution)/shard_map/ppermute | solution.py:455
  71.4 0.0 collective-permute-done.8.refs_7_
  71.4 0.2 collective-permute-done.7.refs_6_
  71.6 1.0 %collective-permute-done.6.refs_5_ = bf16[32,512]{1,0:T(8,128)(2,1)S(1)} collective-permute-done((bf16[32,512]{1,0:T(8,128)(2,1)S(1)}, bf16[32,512]{1,0:T(8,128)(2,1)S(1)}, u32[]{:S(2)}, u32[]{:S(2)}) %collective-permute-start.6) | collective-permute-done | bytes 32800 | tf_op jit(solution)/shard_map/ppermute | solution.py:455
  72.6 1.0 %mix.1 = (f32[4,72,512]{2,1,0:T(8,128)S(1)}, f32[4,72,512]{2,1,0:T(8,128)S(1)}) custom-call(s32[1]{0:T(128)} %bitcast.tm_ref, f32[32,32]{1,0:T(8,128)S(1)} %copy-done.4, bf16[256,512]{1,0:T(8,128)(2,1)S(1)} %get-tuple-element.19.refs_0_, bf16[256,512]{1,0:T(8,128)(2,1)S(1)} %collective-permute-done.1.refs_1_, ...), custom_call_target="tpu_custom_call" | custom-call | tf_op jit(solution)/shard_map/mix/pallas_call | solution.py:363
  73.7 4.8 %collective-permute-start.9 = (f32[4,72,512]{2,1,0:T(8,128)S(1)}, f32[4,72,512]{2,1,0:T(8,128)S(1)}, u32[]{:S(2)}, u32[]{:S(2)}) collective-permute-start(f32[4,72,512]{2,1,0:T(8,128)S(1)} %get-tuple-element.25), channel_id=1, source_target_pairs={{0,1},{1,0},{2,3},{3,2},{4,5},{5,4},{6,7},{7,6},{8,9},{9,8},{10,11... | collective-permute-start | bytes 1769480 | tf_op jit(solution)/shard_map/ppermute | solution.py:469
  78.5 1.6 %collective-permute-done.9.twin_ref = f32[4,72,512]{2,1,0:T(8,128)S(1)} collective-permute-done((f32[4,72,512]{2,1,0:T(8,128)S(1)}, f32[4,72,512]{2,1,0:T(8,128)S(1)}, u32[]{:S(2)}, u32[]{:S(2)}) %collective-permute-start.9) | collective-permute-done | bytes 589856 | tf_op jit(solution)/shard_map/ppermute | solution.py:469
  80.1 2.7 %diffuse.1 = f32[4,64,512]{2,1,0:T(8,128)} custom-call(s32[1]{0:T(128)} %bitcast.tm_ref, f32[4,72,512]{2,1,0:T(8,128)S(1)} %get-tuple-element.24.own_ref, f32[4,72,512]{2,1,0:T(8,128)S(1)} %collective-permute-done.9.twin_ref, f32[64,512]{1,0:T(8,128)S(1)} %copy-done), custom_call_target="tpu_custom_call" | custom-call | tf_op jit(solution)/shard_map/diffuse/pallas_call | solution.py:420
  (8 shorter events, 0.0 us)
Async XLA Ops:
  0.6 51.1 %copy-start.3 = (s32[3,512]{1,0:T(4,128)S(1)}, s32[3,512]{1,0:T(4,128)}, u32[]{:S(2)}) copy-start(s32[3,512]{1,0:T(4,128)} %coords_ref.1) | copy-start | bytes 18436
  0.6 33.0 %copy-start.1 = (f32[12288]{0:T(1024)S(1)}, f32[12288]{0:T(1024)}, u32[]{:S(2)}) copy-start(f32[12288]{0:T(1024)} %param.13) | copy-start | bytes 147460
  0.7 33.0 %copy-start.2 = (f32[12288]{0:T(1024)S(1)}, f32[12288]{0:T(1024)}, u32[]{:S(2)}) copy-start(f32[12288]{0:T(1024)} %param.12) | copy-start | bytes 147460
  0.7 51.0 %copy-start = (f32[64,512]{1,0:T(8,128)S(1)}, f32[64,512]{1,0:T(8,128)}, u32[]{:S(2)}) copy-start(f32[64,512]{1,0:T(8,128)} %diff_ref.3) | copy-start | bytes 393220
  1.4 71.2 %copy-start.4 = (f32[32,32]{1,0:T(8,128)S(1)}, f32[32,32]{1,0:T(8,128)}, u32[]{:S(2)}) copy-start(f32[32,32]{1,0:T(8,128)} %cov_ref.1) | copy-start | bytes 12292
  10.4 2.1 %collective-permute-start = (f32[64,4,384]{2,1,0:T(4,128)S(1)}, f32[64,4,384]{2,1,0:T(4,128)S(1)}, u32[]{:S(2)}, u32[]{:S(2)}) collective-permute-start(f32[64,4,384]{2,1,0:T(4,128)S(1)} %get-tuple-element.15), channel_id=1, source_target_pairs={{0,1},{1,0},{2,3},{3,2},{4,5},{5,4},{6,7},{7,6},{8,9},{9,8},{10,11... | collective-permute-start | bytes 1179656 | tf_op jit(solution)/shard_map/ppermute | solution.py:446
  55.0 9.7 %collective-permute-start.5 = (bf16[256,512]{1,0:T(8,128)(2,1)S(1)}, bf16[256,512]{1,0:T(8,128)(2,1)S(1)}, u32[]{:S(2)}, u32[]{:S(2)}) collective-permute-start(bf16[256,512]{1,0:T(8,128)(2,1)S(1)} %get-tuple-element.19.refs_0_), channel_id=1, source_target_pairs={{0,6},{1,7},{2,0},{3,1},{4,2},{5,3},{6,4},{7,5},{8,14},{9,15},{10,... | collective-permute-start | bytes 786440 | tf_op jit(solution)/shard_map/ppermute | solution.py:455
  56.1 13.3 %collective-permute-start.2 = (bf16[256,512]{1,0:T(8,128)(2,1)S(1)}, bf16[256,512]{1,0:T(8,128)(2,1)S(1)}, u32[]{:S(2)}, u32[]{:S(2)}) collective-permute-start(bf16[256,512]{1,0:T(8,128)(2,1)S(1)} %get-tuple-element.19.refs_0_), channel_id=1, source_target_pairs={{0,4},{1,5},{2,6},{3,7},{4,0},{5,1},{6,2},{7,3},{8,12},{9,13},{10,... | collective-permute-start | bytes 786440 | tf_op jit(solution)/shard_map/ppermute | solution.py:455
  56.5 14.9 %collective-permute-start.1 = (bf16[256,512]{1,0:T(8,128)(2,1)S(1)}, bf16[256,512]{1,0:T(8,128)(2,1)S(1)}, u32[]{:S(2)}, u32[]{:S(2)}) collective-permute-start(bf16[256,512]{1,0:T(8,128)(2,1)S(1)} %get-tuple-element.19.refs_0_), channel_id=1, source_target_pairs={{0,2},{1,3},{2,4},{3,5},{4,6},{5,7},{6,0},{7,1},{8,10},{9,11},{10,... | collective-permute-start | bytes 786440 | tf_op jit(solution)/shard_map/ppermute | solution.py:455
  56.8 2.3 %collective-permute-start.3 = (f32[16,512]{1,0:T(8,128)S(1)}, f32[16,512]{1,0:T(8,128)S(1)}, u32[]{:S(2)}, u32[]{:S(2)}) collective-permute-start(f32[16,512]{1,0:T(8,128)S(1)} %get-tuple-element.20), channel_id=1, source_target_pairs={{0,1},{1,0},{2,3},{3,2},{4,5},{5,4},{6,7},{7,6},{8,9},{9,8},{10,11... | collective-permute-start | bytes 98312 | tf_op jit(solution)/shard_map/ppermute | solution.py:457
  59.1 5.6 %collective-permute-start.4 = (f32[40,512]{1,0:T(8,128)S(1)}, f32[40,512]{1,0:T(8,128)S(1)}, u32[]{:S(2)}, u32[]{:S(2)}) collective-permute-start(f32[40,512]{1,0:T(8,128)S(1)} %pad_maximum_fusion), channel_id=1, source_target_pairs={{0,8},{9,1},{2,10},{11,3},{4,12},{13,5},{6,14},{15,7},{8,16},{17,9... | collective-permute-start | bytes 245768 | tf_op jit(solution)/shard_map/ppermute | solution.py:464
  64.7 6.7 %collective-permute-start.8 = (bf16[32,512]{1,0:T(8,128)(2,1)S(1)}, bf16[32,512]{1,0:T(8,128)(2,1)S(1)}, u32[]{:S(2)}, u32[]{:S(2)}) collective-permute-start(bf16[32,512]{1,0:T(8,128)(2,1)S(1)} %slice.7.refs_4_), channel_id=1, source_target_pairs={{0,6},{1,7},{2,0},{3,1},{4,2},{5,3},{6,4},{7,5},{8,14},{9,15},{10,... | collective-permute-start | bytes 98312 | tf_op jit(solution)/shard_map/ppermute | solution.py:455
  67.2 4.4 %collective-permute-start.7 = (bf16[32,512]{1,0:T(8,128)(2,1)S(1)}, bf16[32,512]{1,0:T(8,128)(2,1)S(1)}, u32[]{:S(2)}, u32[]{:S(2)}) collective-permute-start(bf16[32,512]{1,0:T(8,128)(2,1)S(1)} %slice.7.refs_4_), channel_id=1, source_target_pairs={{0,4},{1,5},{2,6},{3,7},{4,0},{5,1},{6,2},{7,3},{8,12},{9,13},{10,... | collective-permute-start | bytes 98312 | tf_op jit(solution)/shard_map/ppermute | solution.py:455
  68.6 4.0 %collective-permute-start.6 = (bf16[32,512]{1,0:T(8,128)(2,1)S(1)}, bf16[32,512]{1,0:T(8,128)(2,1)S(1)}, u32[]{:S(2)}, u32[]{:S(2)}) collective-permute-start(bf16[32,512]{1,0:T(8,128)(2,1)S(1)} %slice.7.refs_4_), channel_id=1, source_target_pairs={{0,2},{1,3},{2,4},{3,5},{4,6},{5,7},{6,0},{7,1},{8,10},{9,11},{10,... | collective-permute-start | bytes 98312 | tf_op jit(solution)/shard_map/ppermute | solution.py:455
  73.7 6.5 %collective-permute-start.9 = (f32[4,72,512]{2,1,0:T(8,128)S(1)}, f32[4,72,512]{2,1,0:T(8,128)S(1)}, u32[]{:S(2)}, u32[]{:S(2)}) collective-permute-start(f32[4,72,512]{2,1,0:T(8,128)S(1)} %get-tuple-element.25), channel_id=1, source_target_pairs={{0,1},{1,0},{2,3},{3,2},{4,5},{5,4},{6,7},{7,6},{8,9},{9,8},{10,11... | collective-permute-start | bytes 1769480 | tf_op jit(solution)/shard_map/ppermute | solution.py:469

commit v5 on v4

--- a/solution.py
+++ b/solution.py
@@ -1,3 +1,5 @@
+import functools
+
 import jax
 import jax.numpy as jnp
 from jax import lax
@@ -308,34 +310,59 @@
     return jnp.concatenate(split2(jnp.where(same, wide, 0.0)), axis=0)
 
 
-def mix_kernel(tm_ref, cov_ref, *refs):
-    mains, halos, received_ref, (own_ref, twin_ref) = refs[:4], refs[4:8], refs[8], refs[9:]
-    time_dev, ext_rows, width = own_ref.shape
-    tile_rows = ext_rows - EDGE
+def weights_kernel(tm_ref, cov_ref, main_ref, halo_ref):
     times = cov_ref.shape[0]
+    time_dev = main_ref.shape[2] // (4 * EDGE)
     depth, core = tm_ref[0] // 2, tm_ref[0] % 2
 
-    def target_time(per):
-        row = iota((2 * time_dev * per, times), 0)
-        core_of = jnp.where(row < time_dev * per, core, 1 - core)
-        return (2 * depth + core_of) * time_dev + row % (time_dev * per) // per
+    def target_time(per, n):
+        row = iota((time_dev * per, times), 0)
+        return (2 * depth + (core if n == 0 else 1 - core)) * time_dev + row // per
 
     def depth_of(col, block):
         return (depth + 4 - col // block) % 4
+
+    block = EDGE * time_dev
+    col = iota((times, 4 * block), 1)
+    source = (2 * depth_of(col, block) + core) * time_dev + col % block // EDGE
+    half = SWEEPS * time_dev
+    col = iota((times, 8 * half), 1)
+    core_of = jnp.where(col % (2 * half) < half, 1 - core, core)
+    edge_source = (2 * depth_of(col, 2 * half) + core_of) * time_dev + col % half // SWEEPS
+    for n in range(2):
+        main_ref[n] = spread_cov(cov_ref[...], target_time(EDGE, n), source, EDGE)
+        halo_ref[n] = spread_cov(cov_ref[...], target_time(SWEEPS, n), edge_source, SWEEPS)
+
+
+def weights(tm, cov, time_dev):
+    vmem = pl.BlockSpec(memory_space=pltpu.VMEM)
+    block = time_dev * EDGE
+    half = time_dev * SWEEPS
+    return pl.pallas_call(
+        weights_kernel,
+        out_shape=(
+            jax.ShapeDtypeStruct((2, 2 * block, 4 * block), bf16),
+            jax.ShapeDtypeStruct((2, 2 * half, 8 * half), bf16),
+        ),
+        in_specs=[pl.BlockSpec(memory_space=pltpu.SMEM), vmem],
+        out_specs=(vmem, vmem),
+        compiler_params=pltpu.CompilerParams(vmem_limit_bytes=2 * MIB),
+        name="weights",
+    )(tm, cov)
+
+
+def mix_kernel(twin, main_weight_ref, halo_weight_ref, *refs):
+    mains, halos, received_ref, out_ref = refs[:4], refs[4:8], refs[8], refs[9]
+    time_dev, ext_rows, width = out_ref.shape
+    tile_rows = ext_rows - EDGE
 
     def put(full, at, count):
         half = full.shape[0] // 2
         full = full[:half] + full[half:]
         for t in range(time_dev):
-            row = t * count
-            own_ref[t, at : at + count, :] = full[row : row + count]
-            row += time_dev * count
-            twin_ref[t, at : at + count, :] = full[row : row + count]
-
-    block = EDGE * time_dev
-    col = iota((times, 4 * block), 1)
-    source = (2 * depth_of(col, block) + core) * time_dev + col % block // EDGE
-    wide = spread_cov(cov_ref[...], target_time(EDGE), source, EDGE)
+            out_ref[t, at : at + count, :] = full[t * count : (t + 1) * count]
+
+    wide = main_weight_ref[int(twin)]
     for r in range(0, tile_rows, EDGE):
         pieces = [
             main[u * tile_rows + r : u * tile_rows + r + EDGE, :].astype(f32)
@@ -343,35 +370,28 @@
             for u in range(time_dev)
         ]
         put(dot(wide, jnp.concatenate(pieces, axis=0).astype(bf16)), r, EDGE)
-
-    half = SWEEPS * time_dev
-    col = iota((times, 8 * half), 1)
-    core_of = jnp.where(col % (2 * half) < half, 1 - core, core)
-    source = (2 * depth_of(col, 2 * half) + core_of) * time_dev + col % half // SWEEPS
-    wide = spread_cov(cov_ref[...], target_time(SWEEPS), source, SWEEPS)
     edges = jnp.concatenate([halo[...] for halo in halos], axis=0)
-    put(dot(wide, edges), tile_rows, SWEEPS)
+    put(dot(halo_weight_ref[int(twin)], edges), tile_rows, SWEEPS)
+    base = 2 * time_dev * SWEEPS
     for t in range(time_dev):
-        n = 2 * half + (t % 2) * SWEEPS
-        for ref in (own_ref, twin_ref):
-            ref[t, tile_rows + SWEEPS :, :] = received_ref[n : n + SWEEPS, :]
-
-
-def mix(tm, cov, mains, halos, received, shape):
+        n = base + (t % 2) * SWEEPS
+        out_ref[t, tile_rows + SWEEPS :, :] = received_ref[n : n + SWEEPS, :]
+
+
+def mix(twin, wide, mains, halos, received, shape):
     vmem = pl.BlockSpec(memory_space=pltpu.VMEM)
-    whole = jax.ShapeDtypeStruct((shape[0], shape[1] + EDGE, shape[2]), f32)
     return pl.pallas_call(
-        mix_kernel,
-        out_shape=(whole, whole),
-        in_specs=[pl.BlockSpec(memory_space=pltpu.SMEM)] + [vmem] * 10,
-        out_specs=(vmem, vmem),
+        functools.partial(mix_kernel, twin),
+        out_shape=jax.ShapeDtypeStruct((shape[0], shape[1] + EDGE, shape[2]), f32),
+        in_specs=[vmem] * 11,
+        out_specs=vmem,
         compiler_params=pltpu.CompilerParams(vmem_limit_bytes=8 * MIB),
-        name="mix",
-    )(tm, cov, *mains, *halos, received)
-
-
-def diffuse_kernel(tm_ref, own_ref, twin_ref, diff_ref, out_ref, field, other):
-    time_dev, tile_rows, width = out_ref.shape
+        name="mix_twin" if twin else "mix_own",
+    )(*wide, *mains, *halos, received)
+
+
+def diffuse_kernel(tm_ref, own_ref, twin_ref, diff_ref, out_ref, field, other, staged, sems):
+    time_dev, tile_rows, width = staged.shape
     ext_rows = field.shape[1]
     first, last = 2 * EDGE, 2 * EDGE + tile_rows
     first_core = tm_ref[0] % 2 == 0
@@ -383,8 +403,12 @@
     def ordered(a, b):
         return jnp.where(first_core, a, b), jnp.where(first_core, b, a)
 
+    def leave(t):
+        return pltpu.make_async_copy(staged.at[t], out_ref.at[t], sems.at[t])
+
     before, after = ordered(halo_of(own_ref), halo_of(twin_ref))
     diff = jnp.concatenate([before, diff_ref[...], after], axis=0)
+    keep = 1.0 - 4.0 * diff
     column_of = iota(diff.shape, 1)
     here = slice(EDGE, ext_rows - EDGE)
     for buffer in (field, other):
@@ -404,12 +428,15 @@
             right = jnp.where(column_of == width - 1, 0.0, pltpu.roll(centre, width - 1, 1))
             above = source[t, EDGE - 1 : ext_rows - EDGE - 1, :]
             below = source[t, EDGE + 1 : ext_rows - EDGE + 1, :]
-            moved = centre + diff * (below + above + right + left - 4.0 * centre)
+            moved = keep * centre + diff * (below + above + right + left)
             if sweep + 1 < SWEEPS:
                 target[t, here, :] = moved
             else:
-                out_ref[t] = moved[EDGE : EDGE + tile_rows]
+                staged[t] = moved[EDGE : EDGE + tile_rows]
+                leave(t).start()
         source, target = target, source
+    for t in range(time_dev):
+        leave(t).wait()
 
 
 def diffuse(tm, own, twin, diffusivity):
@@ -417,13 +444,14 @@
     tile_rows, width = diffusivity.shape
     field = pltpu.VMEM((time_dev, tile_rows + 4 * EDGE, width), f32)
     vmem = pl.BlockSpec(memory_space=pltpu.VMEM)
+    shape = (time_dev, tile_rows, width)
     return pl.pallas_call(
         diffuse_kernel,
-        out_shape=jax.ShapeDtypeStruct((time_dev, tile_rows, width), f32),
+        out_shape=jax.ShapeDtypeStruct(shape, f32),
         in_specs=[pl.BlockSpec(memory_space=pltpu.SMEM)] + [vmem] * 3,
-        out_specs=vmem,
-        scratch_shapes=[field, field],
-        compiler_params=pltpu.CompilerParams(vmem_limit_bytes=8 * MIB),
+        out_specs=pl.BlockSpec(memory_space=pltpu.HBM),
+        scratch_shapes=[field, field, pltpu.VMEM(shape, f32), pltpu.SemaphoreType.DMA((time_dev,))],
+        compiler_params=pltpu.CompilerParams(vmem_limit_bytes=10 * MIB),
         name="diffuse",
     )(tm, own, twin, diffusivity)
 
@@ -461,12 +489,15 @@
         for t in range(0, n_tm, 2):
             moves.append((s * n_tm + t, (s + 1) * n_tm + t))
             moves.append(((s + 1) * n_tm + t + 1, s * n_tm + t + 1))
-    received = lax.ppermute(jnp.concatenate([other, mine], axis=0), both, moves)
+    payload, cov = lax.optimization_barrier((jnp.concatenate([other, mine], axis=0), time_cov))
+    received = lax.ppermute(payload, both, moves)
+    wide = weights(tm, cov, time_dev)
     halo = received[: 2 * time_dev * SWEEPS].astype(bf16)
     halo, mains[3] = lax.optimization_barrier((halo, mains[3]))
     halos = [halo] + [along(halo, k) for k in (1, 2, 3)]
-    own, twin = mix(tm, time_cov, mains, halos, received, fluxes.shape)
-    twin = lax.ppermute(twin, "tm", swap)
+    held = (wide, mains, halos, received, fluxes.shape)
+    twin = lax.ppermute(mix(True, *held), "tm", swap)
+    own = mix(False, *held)
     gradient = diffuse(tm, own, twin, diffusivity)
     return misfit.reshape(-1), gradient
 

time: 83.1 us -> 82.2 us (0.989)
    pallas_call x2 -> x4, Pallas kernels: 3.78 us -> 3.51 us  [the longest x1 2.45 us: diffuse(): pl.pallas_call(diffuse_kernel, out_shape=jax.ShapeDtypeStruct(shape, f32)...]
  transfers between devices with their start and end apart: 10 -> 10, of which waited for: 7 -> 7; matrix products, arithmetic and copies ran while one was open for 0% -> 0% of each run, Pallas kernels for 0% -> 1%
where the time goes in v5:
time: 82.2 us; the launch traced here: 82 us
  blocking collectives  38.3 us (47%)
  starting transfers between devices  17.6 us (21%)
  Pallas kernels  16.6 us (20%)
  waiting for transfers between devices  7.76 us (9%)
  between operations  1.56 us (2%)
    all_to_all x1, blocking collectives, body(): lax.all_to_all(sums, both, 0, 0, axis_index_groups=parity, tiled=True)  21 us
    all_to_all x1, blocking collectives, body(): halves = lax.all_to_all(halves, both, 0, 0, tiled=True)  17.3 us
    pallas_call x1, Pallas kernels, forward(): pl.pallas_call(forward_kernel, out_shape=(pltpu.VMEM((devices // 2, 4, co...  9.06 us
    ppermute x6, starting transfers between devices, along(): lax.ppermute(array, 'tm', [(i, (i + 2 * steps) % n_tm) for i in range(n_t...  6.5 us
    ppermute x1, starting transfers between devices, body(): twin = lax.ppermute(mix(True, *held), 'tm', swap)  4.82 us
    ppermute x1, starting transfers between devices, body(): received = lax.ppermute(payload, both, moves)  4.1 us
    pallas_call x1, Pallas kernels, adjoint_of(): pl.pallas_call(adjoint_kernel, out_shape=(jax.ShapeDtypeStruct((time_dev...  3.32 us
    ppermute x6, waiting for transfers between devices, along(): lax.ppermute(array, 'tm', [(i, (i + 2 * steps) % n_tm) for i in range(n_t...  2.77 us
  transfers between devices with their start and end apart: 10, of which 7 were waited for; matrix products, arithmetic and copies ran while one was open for 0% of the time, Pallas kernels for 1%

profile of v5, /device:TPU:3, one launch (start us, length us, event | category | flops | bytes accessed | tf_op | source)
XLA Modules:
  0.0 82.0 jit_solution(11882161907196956212)
XLA Ops:
  1.4 0.0 copy-start.4
  1.4 9.1 %forward.1 = (f32[64,4,384]{2,1,0:T(4,128)S(1)}, f32[64,4,384]{2,1,0:T(4,128)S(1)}, bf16[512,128,128]{2,1,0:T(8,128)(2,1)S(1)}) custom-call(s32[1]{0:T(128)} %bitcast.tm_ref, s32[1]{0:T(128)S(6)} %copy.10.count_ref, s32[3,512]{1,0:T(4,128)} %coords_ref.1, bf16[4,64,512]{2,1,0:T(8,128)(2,1)} %flux_hbm.1, bf16[512,128,128]{2,1,0:T(8,128)(2,1)} %foot_ref.1), custom_call_target="tpu_custom_call" | custom-call | tf_op jit(solution)/shard_map/forward/pallas_call | solution.py:148
  10.4 0.8 collective-permute-start
  11.2 1.3 %collective-permute-done = f32[64,4,384]{2,1,0:T(4,128)S(1)} collective-permute-done((f32[64,4,384]{2,1,0:T(4,128)S(1)}, f32[64,4,384]{2,1,0:T(4,128)S(1)}, u32[]{:S(2)}, u32[]{:S(2)}) %collective-permute-start) | collective-permute-done | bytes 393248 | tf_op jit(solution)/shard_map/ppermute | solution.py:474
  12.5 0.1 add.3
  12.6 21.0 %all_to_all.10.sums_ref = f32[64,4,384]{2,1,0:T(4,128)S(1)} all-to-all(f32[64,4,384]{2,1,0:T(4,128)S(1)} %add.3), channel_id=1, replica_groups={{0,2,4,6,8,10,12,14,16,18,20,22,24,26,28,30,32,34,36,38,40,42,44,46,48,..., dimensions={0} | all-to-all | bytes 786432 | tf_op jit(solution)/shard_map/all_to_all | solution.py:475
  33.7 0.7 misfit.1
  34.4 17.3 %all_to_all.11.misfit_ref = bf16[128,4,384]{2,1,0:T(4,128)(2,1)S(1)} all-to-all(bf16[128,4,384]{2,1,0:T(4,128)(2,1)S(1)} %get-tuple-element.19), channel_id=1, replica_groups=mesh['space'=16,'tm'=8] {'space','tm'}, dimensions={0} | all-to-all | bytes 786432 | tf_op jit(solution)/shard_map/all_to_all | solution.py:477
  51.7 0.0 copy-done
  51.7 3.3 %adjoint.1 = (bf16[256,512]{1,0:T(8,128)(2,1)S(1)}, f32[24,512]{1,0:T(8,128)S(1)}, f32[16,512]{1,0:T(8,128)S(1)}) custom-call(s32[1]{0:T(128)} %bitcast.tm_ref, s32[1]{0:T(128)S(6)} %copy.10.count_ref, s32[3,512]{1,0:T(4,128)S(1)} %copy-done.3, bf16[128,4,384]{2,1,0:T(4,128)(2,1)S(1)} %all_to_all.11.misfit_ref, ...), custom_call_target="tpu_custom_call" | custom-call | tf_op jit(solution)/shard_map/adjoint/pallas_call | solution.py:283
  55.0 1.0 %collective-permute-start.5 = (bf16[256,512]{1,0:T(8,128)(2,1)S(1)}, bf16[256,512]{1,0:T(8,128)(2,1)S(1)}, u32[]{:S(2)}, u32[]{:S(2)}) collective-permute-start(bf16[256,512]{1,0:T(8,128)(2,1)S(1)} %get-tuple-element.26.refs_0_), channel_id=1, source_target_pairs={{0,6},{1,7},{2,0},{3,1},{4,2},{5,3},{6,4},{7,5},{8,14},{9,15},{10,... | collective-permute-start | bytes 786440 | tf_op jit(solution)/shard_map/ppermute | solution.py:483
  56.1 0.5 collective-permute-start.3
  56.5 0.3 collective-permute-start.2
  56.8 1.4 %collective-permute-start.1 = (f32[16,512]{1,0:T(8,128)S(1)}, f32[16,512]{1,0:T(8,128)S(1)}, u32[]{:S(2)}, u32[]{:S(2)}) collective-permute-start(f32[16,512]{1,0:T(8,128)S(1)} %get-tuple-element.21), channel_id=1, source_target_pairs={{0,1},{1,0},{2,3},{3,2},{4,5},{5,4},{6,7},{7,6},{8,9},{9,8},{10,11... | collective-permute-start | bytes 98312 | tf_op jit(solution)/shard_map/ppermute | solution.py:485
  58.3 0.9 %collective-permute-done.1 = f32[16,512]{1,0:T(8,128)S(1)} collective-permute-done((f32[16,512]{1,0:T(8,128)S(1)}, f32[16,512]{1,0:T(8,128)S(1)}, u32[]{:S(2)}, u32[]{:S(2)}) %collective-permute-start.1) | collective-permute-done | bytes 32800 | tf_op jit(solution)/shard_map/ppermute | solution.py:485
  59.1 4.1 %collective-permute-start.4 = (f32[40,512]{1,0:T(8,128)S(1)}, f32[40,512]{1,0:T(8,128)S(1)}, u32[]{:S(2)}, u32[]{:S(2)}) collective-permute-start(f32[40,512]{1,0:T(8,128)S(1)} %pad_maximum_fusion), channel_id=1, source_target_pairs={{0,8},{9,1},{2,10},{11,3},{4,12},{13,5},{6,14},{15,7},{8,16},{17,9... | collective-permute-start | bytes 245768 | tf_op jit(solution)/shard_map/ppermute | solution.py:493
  63.2 1.5 %collective-permute-done.4.refs_8_ = f32[40,512]{1,0:T(8,128)S(1)} collective-permute-done((f32[40,512]{1,0:T(8,128)S(1)}, f32[40,512]{1,0:T(8,128)S(1)}, u32[]{:S(2)}, u32[]{:S(2)}) %collective-permute-start.4) | collective-permute-done | bytes 81952 | tf_op jit(solution)/shard_map/ppermute | solution.py:493
  64.7 0.0 collective-permute-done.5.refs_3_
  64.7 2.5 %collective-permute-start.8 = (bf16[32,512]{1,0:T(8,128)(2,1)S(1)}, bf16[32,512]{1,0:T(8,128)(2,1)S(1)}, u32[]{:S(2)}, u32[]{:S(2)}) collective-permute-start(bf16[32,512]{1,0:T(8,128)(2,1)S(1)} %slice.7.refs_4_), channel_id=1, source_target_pairs={{0,6},{1,7},{2,0},{3,1},{4,2},{5,3},{6,4},{7,5},{8,14},{9,15},{10,... | collective-permute-start | bytes 98312 | tf_op jit(solution)/shard_map/ppermute | solution.py:483
  67.2 1.4 %collective-permute-start.7 = (bf16[32,512]{1,0:T(8,128)(2,1)S(1)}, bf16[32,512]{1,0:T(8,128)(2,1)S(1)}, u32[]{:S(2)}, u32[]{:S(2)}) collective-permute-start(bf16[32,512]{1,0:T(8,128)(2,1)S(1)} %slice.7.refs_4_), channel_id=1, source_target_pairs={{0,4},{1,5},{2,6},{3,7},{4,0},{5,1},{6,2},{7,3},{8,12},{9,13},{10,... | collective-permute-start | bytes 98312 | tf_op jit(solution)/shard_map/ppermute | solution.py:483
  68.6 0.8 collective-permute-start.6
  69.4 0.4 weights.1
  69.8 0.0 collective-permute-done.3.refs_2_
  69.8 1.6 %collective-permute-done.2.refs_1_ = bf16[256,512]{1,0:T(8,128)(2,1)S(1)} collective-permute-done((bf16[256,512]{1,0:T(8,128)(2,1)S(1)}, bf16[256,512]{1,0:T(8,128)(2,1)S(1)}, u32[]{:S(2)}, u32[]{:S(2)}) %collective-permute-start.2) | collective-permute-done | bytes 262176 | tf_op jit(solution)/shard_map/ppermute | solution.py:483
  71.4 0.0 collective-permute-done.8.refs_7_
  71.4 0.2 collective-permute-done.7.refs_6_
  71.6 1.0 %collective-permute-done.6.refs_5_ = bf16[32,512]{1,0:T(8,128)(2,1)S(1)} collective-permute-done((bf16[32,512]{1,0:T(8,128)(2,1)S(1)}, bf16[32,512]{1,0:T(8,128)(2,1)S(1)}, u32[]{:S(2)}, u32[]{:S(2)}) %collective-permute-start.6) | collective-permute-done | bytes 32800 | tf_op jit(solution)/shard_map/ppermute | solution.py:483
  72.6 0.3 mix_twin.1
  72.9 4.8 %collective-permute-start.9 = (f32[4,72,512]{2,1,0:T(8,128)S(1)}, f32[4,72,512]{2,1,0:T(8,128)S(1)}, u32[]{:S(2)}, u32[]{:S(2)}) collective-permute-start(f32[4,72,512]{2,1,0:T(8,128)S(1)} %mix_twin.1), channel_id=1, source_target_pairs={{0,1},{1,0},{2,3},{3,2},{4,5},{5,4},{6,7},{7,6},{8,9},{9,8},{10,11... | collective-permute-start | bytes 1769480 | tf_op jit(solution)/shard_map/ppermute | solution.py:499
  77.7 0.3 mix_own.1.own_ref
  78.1 1.3 %collective-permute-done.9.twin_ref = f32[4,72,512]{2,1,0:T(8,128)S(1)} collective-permute-done((f32[4,72,512]{2,1,0:T(8,128)S(1)}, f32[4,72,512]{2,1,0:T(8,128)S(1)}, u32[]{:S(2)}, u32[]{:S(2)}) %collective-permute-start.9) | collective-permute-done | bytes 589856 | tf_op jit(solution)/shard_map/ppermute | solution.py:499
  79.4 2.5 %diffuse.1 = f32[4,64,512]{2,1,0:T(8,128)} custom-call(s32[1]{0:T(128)} %bitcast.tm_ref, f32[4,72,512]{2,1,0:T(8,128)S(1)} %mix_own.1.own_ref, f32[4,72,512]{2,1,0:T(8,128)S(1)} %collective-permute-done.9.twin_ref, f32[64,512]{1,0:T(8,128)S(1)} %copy-done), custom_call_target="tpu_custom_call" | custom-call | tf_op jit(solution)/shard_map/diffuse/pallas_call | solution.py:448
  (10 shorter events, 0.0 us)
Async XLA Ops:
  0.6 51.1 %copy-start.3 = (s32[3,512]{1,0:T(4,128)S(1)}, s32[3,512]{1,0:T(4,128)}, u32[]{:S(2)}) copy-start(s32[3,512]{1,0:T(4,128)} %coords_ref.1) | copy-start | bytes 18436
  0.6 33.0 %copy-start.1 = (f32[12288]{0:T(1024)S(1)}, f32[12288]{0:T(1024)}, u32[]{:S(2)}) copy-start(f32[12288]{0:T(1024)} %param.13) | copy-start | bytes 147460
  0.7 33.0 %copy-start.2 = (f32[12288]{0:T(1024)S(1)}, f32[12288]{0:T(1024)}, u32[]{:S(2)}) copy-start(f32[12288]{0:T(1024)} %param.12) | copy-start | bytes 147460
  0.7 51.0 %copy-start = (f32[64,512]{1,0:T(8,128)S(1)}, f32[64,512]{1,0:T(8,128)}, u32[]{:S(2)}) copy-start(f32[64,512]{1,0:T(8,128)} %diff_ref.3) | copy-start | bytes 393220
  1.4 68.0 %copy-start.4 = (f32[32,32]{1,0:T(8,128)S(1)}, f32[32,32]{1,0:T(8,128)}, u32[]{:S(2)}) copy-start(f32[32,32]{1,0:T(8,128)} %cov_ref) | copy-start | bytes 12292
  10.4 2.1 %collective-permute-start = (f32[64,4,384]{2,1,0:T(4,128)S(1)}, f32[64,4,384]{2,1,0:T(4,128)S(1)}, u32[]{:S(2)}, u32[]{:S(2)}) collective-permute-start(f32[64,4,384]{2,1,0:T(4,128)S(1)} %get-tuple-element.17), channel_id=1, source_target_pairs={{0,1},{1,0},{2,3},{3,2},{4,5},{5,4},{6,7},{7,6},{8,9},{9,8},{10,11... | collective-permute-start | bytes 1179656 | tf_op jit(solution)/shard_map/ppermute | solution.py:474
  55.0 9.7 %collective-permute-start.5 = (bf16[256,512]{1,0:T(8,128)(2,1)S(1)}, bf16[256,512]{1,0:T(8,128)(2,1)S(1)}, u32[]{:S(2)}, u32[]{:S(2)}) collective-permute-start(bf16[256,512]{1,0:T(8,128)(2,1)S(1)} %get-tuple-element.26.refs_0_), channel_id=1, source_target_pairs={{0,6},{1,7},{2,0},{3,1},{4,2},{5,3},{6,4},{7,5},{8,14},{9,15},{10,... | collective-permute-start | bytes 786440 | tf_op jit(solution)/shard_map/ppermute | solution.py:483
  56.1 13.8 %collective-permute-start.3 = (bf16[256,512]{1,0:T(8,128)(2,1)S(1)}, bf16[256,512]{1,0:T(8,128)(2,1)S(1)}, u32[]{:S(2)}, u32[]{:S(2)}) collective-permute-start(bf16[256,512]{1,0:T(8,128)(2,1)S(1)} %get-tuple-element.26.refs_0_), channel_id=1, source_target_pairs={{0,4},{1,5},{2,6},{3,7},{4,0},{5,1},{6,2},{7,3},{8,12},{9,13},{10,... | collective-permute-start | bytes 786440 | tf_op jit(solution)/shard_map/ppermute | solution.py:483
  56.5 14.9 %collective-permute-start.2 = (bf16[256,512]{1,0:T(8,128)(2,1)S(1)}, bf16[256,512]{1,0:T(8,128)(2,1)S(1)}, u32[]{:S(2)}, u32[]{:S(2)}) collective-permute-start(bf16[256,512]{1,0:T(8,128)(2,1)S(1)} %get-tuple-element.26.refs_0_), channel_id=1, source_target_pairs={{0,2},{1,3},{2,4},{3,5},{4,6},{5,7},{6,0},{7,1},{8,10},{9,11},{10,... | collective-permute-start | bytes 786440 | tf_op jit(solution)/shard_map/ppermute | solution.py:483
  56.8 2.3 %collective-permute-start.1 = (f32[16,512]{1,0:T(8,128)S(1)}, f32[16,512]{1,0:T(8,128)S(1)}, u32[]{:S(2)}, u32[]{:S(2)}) collective-permute-start(f32[16,512]{1,0:T(8,128)S(1)} %get-tuple-element.21), channel_id=1, source_target_pairs={{0,1},{1,0},{2,3},{3,2},{4,5},{5,4},{6,7},{7,6},{8,9},{9,8},{10,11... | collective-permute-start | bytes 98312 | tf_op jit(solution)/shard_map/ppermute | solution.py:485
  59.1 5.6 %collective-permute-start.4 = (f32[40,512]{1,0:T(8,128)S(1)}, f32[40,512]{1,0:T(8,128)S(1)}, u32[]{:S(2)}, u32[]{:S(2)}) collective-permute-start(f32[40,512]{1,0:T(8,128)S(1)} %pad_maximum_fusion), channel_id=1, source_target_pairs={{0,8},{9,1},{2,10},{11,3},{4,12},{13,5},{6,14},{15,7},{8,16},{17,9... | collective-permute-start | bytes 245768 | tf_op jit(solution)/shard_map/ppermute | solution.py:493
  64.7 6.7 %collective-permute-start.8 = (bf16[32,512]{1,0:T(8,128)(2,1)S(1)}, bf16[32,512]{1,0:T(8,128)(2,1)S(1)}, u32[]{:S(2)}, u32[]{:S(2)}) collective-permute-start(bf16[32,512]{1,0:T(8,128)(2,1)S(1)} %slice.7.refs_4_), channel_id=1, source_target_pairs={{0,6},{1,7},{2,0},{3,1},{4,2},{5,3},{6,4},{7,5},{8,14},{9,15},{10,... | collective-permute-start | bytes 98312 | tf_op jit(solution)/shard_map/ppermute | solution.py:483
  67.2 4.4 %collective-permute-start.7 = (bf16[32,512]{1,0:T(8,128)(2,1)S(1)}, bf16[32,512]{1,0:T(8,128)(2,1)S(1)}, u32[]{:S(2)}, u32[]{:S(2)}) collective-permute-start(bf16[32,512]{1,0:T(8,128)(2,1)S(1)} %slice.7.refs_4_), channel_id=1, source_target_pairs={{0,4},{1,5},{2,6},{3,7},{4,0},{5,1},{6,2},{7,3},{8,12},{9,13},{10,... | collective-permute-start | bytes 98312 | tf_op jit(solution)/shard_map/ppermute | solution.py:483
  68.6 4.0 %collective-permute-start.6 = (bf16[32,512]{1,0:T(8,128)(2,1)S(1)}, bf16[32,512]{1,0:T(8,128)(2,1)S(1)}, u32[]{:S(2)}, u32[]{:S(2)}) collective-permute-start(bf16[32,512]{1,0:T(8,128)(2,1)S(1)} %slice.7.refs_4_), channel_id=1, source_target_pairs={{0,2},{1,3},{2,4},{3,5},{4,6},{5,7},{6,0},{7,1},{8,10},{9,11},{10,... | collective-permute-start | bytes 98312 | tf_op jit(solution)/shard_map/ppermute | solution.py:483
  72.9 6.4 %collective-permute-start.9 = (f32[4,72,512]{2,1,0:T(8,128)S(1)}, f32[4,72,512]{2,1,0:T(8,128)S(1)}, u32[]{:S(2)}, u32[]{:S(2)}) collective-permute-start(f32[4,72,512]{2,1,0:T(8,128)S(1)} %mix_twin.1), channel_id=1, source_target_pairs={{0,1},{1,0},{2,3},{3,2},{4,5},{5,4},{6,7},{7,6},{8,9},{9,8},{10,11... | collective-permute-start | bytes 1769480 | tf_op jit(solution)/shard_map/ppermute | solution.py:499

commit v6 on v5

--- a/solution.py
+++ b/solution.py
@@ -175,8 +175,15 @@
     base = tm_ref[0] * (quarter * cols)
 
     def own(ref):
+        block = ref[pl.ds(base, quarter * cols), :]
         return jnp.concatenate(
-            [ref[pl.ds(base + l, quarter, stride=cols), :] for l in range(cols)], axis=1
+            [
+                jnp.concatenate(
+                    [block[q * cols + l : q * cols + l + 1] for q in range(quarter)], axis=0
+                )
+                for l in range(cols)
+            ],
+            axis=1,
         )
 
     misfit = own(weight_ref) * (total - own(observed_ref))
@@ -483,18 +490,18 @@
         return lax.ppermute(array, "tm", [(i, (i + 2 * steps) % n_tm) for i in range(n_tm)])
 
     other = lax.ppermute(other, "tm", swap)
-    mains = [main] + [along(main, k) for k in (1, 2, 3)]
     moves = []
     for s in range(n_space - 1):
         for t in range(0, n_tm, 2):
             moves.append((s * n_tm + t, (s + 1) * n_tm + t))
             moves.append(((s + 1) * n_tm + t + 1, s * n_tm + t + 1))
     payload, cov = lax.optimization_barrier((jnp.concatenate([other, mine], axis=0), time_cov))
+    mains = [main] + [along(main, k) for k in (1, 2, 3)]
     received = lax.ppermute(payload, both, moves)
     wide = weights(tm, cov, time_dev)
     halo = received[: 2 * time_dev * SWEEPS].astype(bf16)
-    halo, mains[3] = lax.optimization_barrier((halo, mains[3]))
-    halos = [halo] + [along(halo, k) for k in (1, 2, 3)]
+    last, mains[2] = lax.optimization_barrier((halo, mains[2]))
+    halos = [halo, along(last, 1), along(halo, 2), along(halo, 3)]
     held = (wide, mains, halos, received, fluxes.shape)
     twin = lax.ppermute(mix(True, *held), "tm", swap)
     own = mix(False, *held)

time: 82.2 us -> 80.6 us (0.981)
  starting transfers between devices: 17.6 us -> 15.9 us
    ppermute x6, starting transfers between devices: 6.5 us -> 5.16 us  [along(): lax.ppermute(array, 'tm', [(i, (i + 2 * steps) % n_tm) for i in range(n_t...]
where the time goes in v6:
time: 80.6 us; the launch traced here: 80.4 us
  blocking collectives  38.3 us (48%)
  Pallas kernels  16.6 us (21%)
  starting transfers between devices  15.9 us (20%)
  waiting for transfers between devices  7.9 us (10%)
  between operations  1.56 us (2%)
    all_to_all x1, blocking collectives, body(): lax.all_to_all(sums, both, 0, 0, axis_index_groups=parity, tiled=True)  21 us
    all_to_all x1, blocking collectives, body(): halves = lax.all_to_all(halves, both, 0, 0, tiled=True)  17.3 us
    pallas_call x1, Pallas kernels, forward(): pl.pallas_call(forward_kernel, out_shape=(pltpu.VMEM((devices // 2, 4, co...  9.06 us
    ppermute x6, starting transfers between devices, along(): lax.ppermute(array, 'tm', [(i, (i + 2 * steps) % n_tm) for i in range(n_t...  5.16 us
    ppermute x1, starting transfers between devices, body(): twin = lax.ppermute(mix(True, *held), 'tm', swap)  4.68 us
    ppermute x1, starting transfers between devices, body(): received = lax.ppermute(payload, both, moves)  4.29 us
    pallas_call x1, Pallas kernels, adjoint_of(): pl.pallas_call(adjoint_kernel, out_shape=(jax.ShapeDtypeStruct((time_dev...  3.3 us
    ppermute x6, waiting for transfers between devices, along(): lax.ppermute(array, 'tm', [(i, (i + 2 * steps) % n_tm) for i in range(n_t...  3.12 us
  transfers between devices with their start and end apart: 10, of which 7 were waited for; matrix products, arithmetic and copies ran while one was open for 0% of the time, Pallas kernels for 1%

profile of v6, /device:TPU:3, one launch (start us, length us, event | category | flops | bytes accessed | tf_op | source)
XLA Modules:
  0.0 80.4 jit_solution(8442228766836542216)
XLA Ops:
  1.4 9.1 %forward.1 = (f32[64,4,384]{2,1,0:T(4,128)S(1)}, f32[64,4,384]{2,1,0:T(4,128)S(1)}, bf16[512,128,128]{2,1,0:T(8,128)(2,1)S(1)}) custom-call(s32[1]{0:T(128)} %bitcast.tm_ref, s32[1]{0:T(128)S(6)} %copy.10.count_ref, s32[3,512]{1,0:T(4,128)} %coords_ref.1, bf16[4,64,512]{2,1,0:T(8,128)(2,1)} %flux_hbm.1, bf16[512,128,128]{2,1,0:T(8,128)(2,1)} %foot_ref.1), custom_call_target="tpu_custom_call" | custom-call | tf_op jit(solution)/shard_map/forward/pallas_call | solution.py:148
  10.4 0.8 collective-permute-start
  11.2 1.3 %collective-permute-done = f32[64,4,384]{2,1,0:T(4,128)S(1)} collective-permute-done((f32[64,4,384]{2,1,0:T(4,128)S(1)}, f32[64,4,384]{2,1,0:T(4,128)S(1)}, u32[]{:S(2)}, u32[]{:S(2)}) %collective-permute-start) | collective-permute-done | bytes 393248 | tf_op jit(solution)/shard_map/ppermute | solution.py:481
  12.5 0.1 add.3
  12.6 21.0 %all_to_all.10.sums_ref = f32[64,4,384]{2,1,0:T(4,128)S(1)} all-to-all(f32[64,4,384]{2,1,0:T(4,128)S(1)} %add.3), channel_id=1, replica_groups={{0,2,4,6,8,10,12,14,16,18,20,22,24,26,28,30,32,34,36,38,40,42,44,46,48,..., dimensions={0} | all-to-all | bytes 786432 | tf_op jit(solution)/shard_map/all_to_all | solution.py:482
  33.6 0.0 copy-done.2
  33.7 0.7 misfit.1
  34.4 17.3 %all_to_all.11.misfit_ref = bf16[128,4,384]{2,1,0:T(4,128)(2,1)S(1)} all-to-all(bf16[128,4,384]{2,1,0:T(4,128)(2,1)S(1)} %get-tuple-element.19), channel_id=1, replica_groups=mesh['space'=16,'tm'=8] {'space','tm'}, dimensions={0} | all-to-all | bytes 786432 | tf_op jit(solution)/shard_map/all_to_all | solution.py:484
  51.7 0.0 copy-done
  51.7 3.3 %adjoint.1 = (bf16[256,512]{1,0:T(8,128)(2,1)S(1)}, f32[24,512]{1,0:T(8,128)S(1)}, f32[16,512]{1,0:T(8,128)S(1)}) custom-call(s32[1]{0:T(128)} %bitcast.tm_ref, s32[1]{0:T(128)S(6)} %copy.10.count_ref, s32[3,512]{1,0:T(4,128)S(1)} %copy-done.3, bf16[128,4,384]{2,1,0:T(4,128)(2,1)S(1)} %all_to_all.11.misfit_ref, ...), custom_call_target="tpu_custom_call" | custom-call | tf_op jit(solution)/shard_map/adjoint/pallas_call | solution.py:290
  55.0 1.0 %collective-permute-start.4 = (bf16[256,512]{1,0:T(8,128)(2,1)S(1)}, bf16[256,512]{1,0:T(8,128)(2,1)S(1)}, u32[]{:S(2)}, u32[]{:S(2)}) collective-permute-start(bf16[256,512]{1,0:T(8,128)(2,1)S(1)} %get-tuple-element.26.refs_0_), channel_id=1, source_target_pairs={{0,4},{1,5},{2,6},{3,7},{4,0},{5,1},{6,2},{7,3},{8,12},{9,13},{10,... | collective-permute-start | bytes 786440 | tf_op jit(solution)/shard_map/ppermute | solution.py:490
  56.0 1.1 %collective-permute-start.5 = (bf16[256,512]{1,0:T(8,128)(2,1)S(1)}, bf16[256,512]{1,0:T(8,128)(2,1)S(1)}, u32[]{:S(2)}, u32[]{:S(2)}) collective-permute-start(bf16[256,512]{1,0:T(8,128)(2,1)S(1)} %get-tuple-element.26.refs_0_), channel_id=1, source_target_pairs={{0,6},{1,7},{2,0},{3,1},{4,2},{5,3},{6,4},{7,5},{8,14},{9,15},{10,... | collective-permute-start | bytes 786440 | tf_op jit(solution)/shard_map/ppermute | solution.py:490
  57.1 1.0 %collective-permute-start.1 = (f32[16,512]{1,0:T(8,128)S(1)}, f32[16,512]{1,0:T(8,128)S(1)}, u32[]{:S(2)}, u32[]{:S(2)}) collective-permute-start(f32[16,512]{1,0:T(8,128)S(1)} %get-tuple-element.21), channel_id=1, source_target_pairs={{0,1},{1,0},{2,3},{3,2},{4,5},{5,4},{6,7},{7,6},{8,9},{9,8},{10,11... | collective-permute-start | bytes 98312 | tf_op jit(solution)/shard_map/ppermute | solution.py:492
  58.2 0.2 collective-permute-start.2
  58.4 0.6 collective-permute-done.1
  59.0 4.3 %collective-permute-start.3 = (f32[40,512]{1,0:T(8,128)S(1)}, f32[40,512]{1,0:T(8,128)S(1)}, u32[]{:S(2)}, u32[]{:S(2)}) collective-permute-start(f32[40,512]{1,0:T(8,128)S(1)} %pad_maximum_fusion), channel_id=1, source_target_pairs={{0,8},{9,1},{2,10},{11,3},{4,12},{13,5},{6,14},{15,7},{8,16},{17,9... | collective-permute-start | bytes 245768 | tf_op jit(solution)/shard_map/ppermute | solution.py:500
  63.3 1.5 %collective-permute-done.3.refs_8_ = f32[40,512]{1,0:T(8,128)S(1)} collective-permute-done((f32[40,512]{1,0:T(8,128)S(1)}, f32[40,512]{1,0:T(8,128)S(1)}, u32[]{:S(2)}, u32[]{:S(2)}) %collective-permute-start.3) | collective-permute-done | bytes 81952 | tf_op jit(solution)/shard_map/ppermute | solution.py:500
  64.8 1.8 %collective-permute-start.8 = (bf16[32,512]{1,0:T(8,128)(2,1)S(1)}, bf16[32,512]{1,0:T(8,128)(2,1)S(1)}, u32[]{:S(2)}, u32[]{:S(2)}) collective-permute-start(bf16[32,512]{1,0:T(8,128)(2,1)S(1)} %slice.7.refs_4_), channel_id=1, source_target_pairs={{0,6},{1,7},{2,0},{3,1},{4,2},{5,3},{6,4},{7,5},{8,14},{9,15},{10,... | collective-permute-start | bytes 98312 | tf_op jit(solution)/shard_map/ppermute | solution.py:490
  66.7 0.2 collective-permute-start.7
  66.9 0.0 collective-permute-done.4.refs_2_
  66.9 0.8 collective-permute-start.6
  67.6 0.4 weights.1
  68.1 1.0 %collective-permute-done.8.refs_7_ = bf16[32,512]{1,0:T(8,128)(2,1)S(1)} collective-permute-done((bf16[32,512]{1,0:T(8,128)(2,1)S(1)}, bf16[32,512]{1,0:T(8,128)(2,1)S(1)}, u32[]{:S(2)}, u32[]{:S(2)}) %collective-permute-start.8) | collective-permute-done | bytes 32800 | tf_op jit(solution)/shard_map/ppermute | solution.py:490
  69.0 2.0 %collective-permute-done.7.refs_6_ = bf16[32,512]{1,0:T(8,128)(2,1)S(1)} collective-permute-done((bf16[32,512]{1,0:T(8,128)(2,1)S(1)}, bf16[32,512]{1,0:T(8,128)(2,1)S(1)}, u32[]{:S(2)}, u32[]{:S(2)}) %collective-permute-start.7) | collective-permute-done | bytes 32800 | tf_op jit(solution)/shard_map/ppermute | solution.py:490
  71.0 0.0 collective-permute-done.5.refs_3_
  71.0 0.0 collective-permute-done.2.refs_1_
  71.0 0.2 collective-permute-done.6.refs_5_
  71.2 0.3 mix_twin.1
  71.5 4.7 %collective-permute-start.9 = (f32[4,72,512]{2,1,0:T(8,128)S(1)}, f32[4,72,512]{2,1,0:T(8,128)S(1)}, u32[]{:S(2)}, u32[]{:S(2)}) collective-permute-start(f32[4,72,512]{2,1,0:T(8,128)S(1)} %mix_twin.1), channel_id=1, source_target_pairs={{0,1},{1,0},{2,3},{3,2},{4,5},{5,4},{6,7},{7,6},{8,9},{9,8},{10,11... | collective-permute-start | bytes 1769480 | tf_op jit(solution)/shard_map/ppermute | solution.py:506
  76.2 0.3 mix_own.1.own_ref
  76.5 1.3 %collective-permute-done.9.twin_ref = f32[4,72,512]{2,1,0:T(8,128)S(1)} collective-permute-done((f32[4,72,512]{2,1,0:T(8,128)S(1)}, f32[4,72,512]{2,1,0:T(8,128)S(1)}, u32[]{:S(2)}, u32[]{:S(2)}) %collective-permute-start.9) | collective-permute-done | bytes 589856 | tf_op jit(solution)/shard_map/ppermute | solution.py:506
  77.8 2.5 %diffuse.1 = f32[4,64,512]{2,1,0:T(8,128)} custom-call(s32[1]{0:T(128)} %bitcast.tm_ref, f32[4,72,512]{2,1,0:T(8,128)S(1)} %mix_own.1.own_ref, f32[4,72,512]{2,1,0:T(8,128)S(1)} %collective-permute-done.9.twin_ref, f32[64,512]{1,0:T(8,128)S(1)} %copy-done), custom_call_target="tpu_custom_call" | custom-call | tf_op jit(solution)/shard_map/diffuse/pallas_call | solution.py:455
  (10 shorter events, 0.0 us)
Async XLA Ops:
  0.6 51.1 %copy-start.3 = (s32[3,512]{1,0:T(4,128)S(1)}, s32[3,512]{1,0:T(4,128)}, u32[]{:S(2)}) copy-start(s32[3,512]{1,0:T(4,128)} %coords_ref.1) | copy-start | bytes 18436
  0.6 33.0 %copy-start.1 = (f32[12288]{0:T(1024)S(1)}, f32[12288]{0:T(1024)}, u32[]{:S(2)}) copy-start(f32[12288]{0:T(1024)} %param.13) | copy-start | bytes 147460
  0.7 33.0 %copy-start.2 = (f32[12288]{0:T(1024)S(1)}, f32[12288]{0:T(1024)}, u32[]{:S(2)}) copy-start(f32[12288]{0:T(1024)} %param.12) | copy-start | bytes 147460
  0.7 51.0 %copy-start = (f32[64,512]{1,0:T(8,128)S(1)}, f32[64,512]{1,0:T(8,128)}, u32[]{:S(2)}) copy-start(f32[64,512]{1,0:T(8,128)} %diff_ref.3) | copy-start | bytes 393220
  1.4 66.3 %copy-start.4 = (f32[32,32]{1,0:T(8,128)S(1)}, f32[32,32]{1,0:T(8,128)}, u32[]{:S(2)}) copy-start(f32[32,32]{1,0:T(8,128)} %cov_ref) | copy-start | bytes 12292
  10.4 2.1 %collective-permute-start = (f32[64,4,384]{2,1,0:T(4,128)S(1)}, f32[64,4,384]{2,1,0:T(4,128)S(1)}, u32[]{:S(2)}, u32[]{:S(2)}) collective-permute-start(f32[64,4,384]{2,1,0:T(4,128)S(1)} %get-tuple-element.17), channel_id=1, source_target_pairs={{0,1},{1,0},{2,3},{3,2},{4,5},{5,4},{6,7},{7,6},{8,9},{9,8},{10,11... | collective-permute-start | bytes 1179656 | tf_op jit(solution)/shard_map/ppermute | solution.py:481
  55.0 11.9 %collective-permute-start.4 = (bf16[256,512]{1,0:T(8,128)(2,1)S(1)}, bf16[256,512]{1,0:T(8,128)(2,1)S(1)}, u32[]{:S(2)}, u32[]{:S(2)}) collective-permute-start(bf16[256,512]{1,0:T(8,128)(2,1)S(1)} %get-tuple-element.26.refs_0_), channel_id=1, source_target_pairs={{0,4},{1,5},{2,6},{3,7},{4,0},{5,1},{6,2},{7,3},{8,12},{9,13},{10,... | collective-permute-start | bytes 786440 | tf_op jit(solution)/shard_map/ppermute | solution.py:490
  56.0 15.0 %collective-permute-start.5 = (bf16[256,512]{1,0:T(8,128)(2,1)S(1)}, bf16[256,512]{1,0:T(8,128)(2,1)S(1)}, u32[]{:S(2)}, u32[]{:S(2)}) collective-permute-start(bf16[256,512]{1,0:T(8,128)(2,1)S(1)} %get-tuple-element.26.refs_0_), channel_id=1, source_target_pairs={{0,6},{1,7},{2,0},{3,1},{4,2},{5,3},{6,4},{7,5},{8,14},{9,15},{10,... | collective-permute-start | bytes 786440 | tf_op jit(solution)/shard_map/ppermute | solution.py:490
  57.1 1.9 %collective-permute-start.1 = (f32[16,512]{1,0:T(8,128)S(1)}, f32[16,512]{1,0:T(8,128)S(1)}, u32[]{:S(2)}, u32[]{:S(2)}) collective-permute-start(f32[16,512]{1,0:T(8,128)S(1)} %get-tuple-element.21), channel_id=1, source_target_pairs={{0,1},{1,0},{2,3},{3,2},{4,5},{5,4},{6,7},{7,6},{8,9},{9,8},{10,11... | collective-permute-start | bytes 98312 | tf_op jit(solution)/shard_map/ppermute | solution.py:492
  58.2 12.9 %collective-permute-start.2 = (bf16[256,512]{1,0:T(8,128)(2,1)S(1)}, bf16[256,512]{1,0:T(8,128)(2,1)S(1)}, u32[]{:S(2)}, u32[]{:S(2)}) collective-permute-start(bf16[256,512]{1,0:T(8,128)(2,1)S(1)} %get-tuple-element.26.refs_0_), channel_id=1, source_target_pairs={{0,2},{1,3},{2,4},{3,5},{4,6},{5,7},{6,0},{7,1},{8,10},{9,11},{10,... | collective-permute-start | bytes 786440 | tf_op jit(solution)/shard_map/ppermute | solution.py:490
  59.0 5.8 %collective-permute-start.3 = (f32[40,512]{1,0:T(8,128)S(1)}, f32[40,512]{1,0:T(8,128)S(1)}, u32[]{:S(2)}, u32[]{:S(2)}) collective-permute-start(f32[40,512]{1,0:T(8,128)S(1)} %pad_maximum_fusion), channel_id=1, source_target_pairs={{0,8},{9,1},{2,10},{11,3},{4,12},{13,5},{6,14},{15,7},{8,16},{17,9... | collective-permute-start | bytes 245768 | tf_op jit(solution)/shard_map/ppermute | solution.py:500
  64.8 4.2 %collective-permute-start.8 = (bf16[32,512]{1,0:T(8,128)(2,1)S(1)}, bf16[32,512]{1,0:T(8,128)(2,1)S(1)}, u32[]{:S(2)}, u32[]{:S(2)}) collective-permute-start(bf16[32,512]{1,0:T(8,128)(2,1)S(1)} %slice.7.refs_4_), channel_id=1, source_target_pairs={{0,6},{1,7},{2,0},{3,1},{4,2},{5,3},{6,4},{7,5},{8,14},{9,15},{10,... | collective-permute-start | bytes 98312 | tf_op jit(solution)/shard_map/ppermute | solution.py:490
  66.7 4.4 %collective-permute-start.7 = (bf16[32,512]{1,0:T(8,128)(2,1)S(1)}, bf16[32,512]{1,0:T(8,128)(2,1)S(1)}, u32[]{:S(2)}, u32[]{:S(2)}) collective-permute-start(bf16[32,512]{1,0:T(8,128)(2,1)S(1)} %slice.7.refs_4_), channel_id=1, source_target_pairs={{0,4},{1,5},{2,6},{3,7},{4,0},{5,1},{6,2},{7,3},{8,12},{9,13},{10,... | collective-permute-start | bytes 98312 | tf_op jit(solution)/shard_map/ppermute | solution.py:490
  66.9 4.3 %collective-permute-start.6 = (bf16[32,512]{1,0:T(8,128)(2,1)S(1)}, bf16[32,512]{1,0:T(8,128)(2,1)S(1)}, u32[]{:S(2)}, u32[]{:S(2)}) collective-permute-start(bf16[32,512]{1,0:T(8,128)(2,1)S(1)} %slice.7.refs_4_), channel_id=1, source_target_pairs={{0,2},{1,3},{2,4},{3,5},{4,6},{5,7},{6,0},{7,1},{8,10},{9,11},{10,... | collective-permute-start | bytes 98312 | tf_op jit(solution)/shard_map/ppermute | solution.py:490
  71.5 6.3 %collective-permute-start.9 = (f32[4,72,512]{2,1,0:T(8,128)S(1)}, f32[4,72,512]{2,1,0:T(8,128)S(1)}, u32[]{:S(2)}, u32[]{:S(2)}) collective-permute-start(f32[4,72,512]{2,1,0:T(8,128)S(1)} %mix_twin.1), channel_id=1, source_target_pairs={{0,1},{1,0},{2,3},{3,2},{4,5},{5,4},{6,7},{7,6},{8,9},{9,8},{10,11... | collective-permute-start | bytes 1769480 | tf_op jit(solution)/shard_map/ppermute | solution.py:506

commit v7 on v6

--- a/solution.py
+++ b/solution.py
@@ -501,7 +501,7 @@
     wide = weights(tm, cov, time_dev)
     halo = received[: 2 * time_dev * SWEEPS].astype(bf16)
     last, mains[2] = lax.optimization_barrier((halo, mains[2]))
-    halos = [halo, along(last, 1), along(halo, 2), along(halo, 3)]
+    halos = [halo, along(halo, 1), along(halo, 2), along(last, 3)]
     held = (wide, mains, halos, received, fluxes.shape)
     twin = lax.ppermute(mix(True, *held), "tm", swap)
     own = mix(False, *held)

time: 80.6 us -> 80.3 us (level)
  waiting for transfers between devices: 7.9 us -> 5.84 us
  starting transfers between devices: 15.9 us -> 17.6 us
    ppermute x6, waiting for transfers between devices: 3.12 us -> 1.06 us  [along(): lax.ppermute(array, 'tm', [(i, (i + 2 * steps) % n_tm) for i in range(n_t...]
    ppermute x6, starting transfers between devices: 5.16 us -> 6.98 us  [along(): lax.ppermute(array, 'tm', [(i, (i + 2 * steps) % n_tm) for i in range(n_t...]
  transfers between devices with their start and end apart: 10 -> 10, of which waited for: 7 -> 5; matrix products, arithmetic and copies ran while one was open for 0% -> 0% of each run, Pallas kernels for 1% -> 1%
where the time goes in v7:
time: 80.3 us; the launch traced here: 80.1 us
  blocking collectives  38.3 us (48%)
  starting transfers between devices  17.6 us (22%)
  Pallas kernels  16.6 us (21%)
  waiting for transfers between devices  5.84 us (7%)
  between operations  1.56 us (2%)
    all_to_all x1, blocking collectives, body(): lax.all_to_all(sums, both, 0, 0, axis_index_groups=parity, tiled=True)  21 us
    all_to_all x1, blocking collectives, body(): halves = lax.all_to_all(halves, both, 0, 0, tiled=True)  17.3 us
    pallas_call x1, Pallas kernels, forward(): pl.pallas_call(forward_kernel, out_shape=(pltpu.VMEM((devices // 2, 4, co...  9.06 us
    ppermute x6, starting transfers between devices, along(): lax.ppermute(array, 'tm', [(i, (i + 2 * steps) % n_tm) for i in range(n_t...  6.98 us
    ppermute x1, starting transfers between devices, body(): twin = lax.ppermute(mix(True, *held), 'tm', swap)  4.56 us
    ppermute x1, starting transfers between devices, body(): received = lax.ppermute(payload, both, moves)  4.29 us
    pallas_call x1, Pallas kernels, adjoint_of(): pl.pallas_call(adjoint_kernel, out_shape=(jax.ShapeDtypeStruct((time_dev...  3.3 us
    pallas_call x1, Pallas kernels, diffuse(): pl.pallas_call(diffuse_kernel, out_shape=jax.ShapeDtypeStruct(shape, f32)...  2.45 us
  transfers between devices with their start and end apart: 10, of which 5 were waited for; matrix products, arithmetic and copies ran while one was open for 0% of the time, Pallas kernels for 1%

profile of v7, /device:TPU:3, one launch (start us, length us, event | category | flops | bytes accessed | tf_op | source)
XLA Modules:
  0.0 80.1 jit_solution(1627454533951421642)
XLA Ops:
  1.4 9.1 %forward.1 = (f32[64,4,384]{2,1,0:T(4,128)S(1)}, f32[64,4,384]{2,1,0:T(4,128)S(1)}, bf16[512,128,128]{2,1,0:T(8,128)(2,1)S(1)}) custom-call(s32[1]{0:T(128)} %bitcast.tm_ref, s32[1]{0:T(128)S(6)} %copy.10.count_ref, s32[3,512]{1,0:T(4,128)} %coords_ref.1, bf16[4,64,512]{2,1,0:T(8,128)(2,1)} %flux_hbm.1, bf16[512,128,128]{2,1,0:T(8,128)(2,1)} %foot_ref.1), custom_call_target="tpu_custom_call" | custom-call | tf_op jit(solution)/shard_map/forward/pallas_call | solution.py:148
  10.4 0.8 collective-permute-start
  11.2 1.3 %collective-permute-done = f32[64,4,384]{2,1,0:T(4,128)S(1)} collective-permute-done((f32[64,4,384]{2,1,0:T(4,128)S(1)}, f32[64,4,384]{2,1,0:T(4,128)S(1)}, u32[]{:S(2)}, u32[]{:S(2)}) %collective-permute-start) | collective-permute-done | bytes 393248 | tf_op jit(solution)/shard_map/ppermute | solution.py:481
  12.5 0.1 add.3
  12.6 21.0 %all_to_all.10.sums_ref = f32[64,4,384]{2,1,0:T(4,128)S(1)} all-to-all(f32[64,4,384]{2,1,0:T(4,128)S(1)} %add.3), channel_id=1, replica_groups={{0,2,4,6,8,10,12,14,16,18,20,22,24,26,28,30,32,34,36,38,40,42,44,46,48,..., dimensions={0} | all-to-all | bytes 786432 | tf_op jit(solution)/shard_map/all_to_all | solution.py:482
  33.7 0.7 misfit.1
  34.4 17.3 %all_to_all.11.misfit_ref = bf16[128,4,384]{2,1,0:T(4,128)(2,1)S(1)} all-to-all(bf16[128,4,384]{2,1,0:T(4,128)(2,1)S(1)} %get-tuple-element.19), channel_id=1, replica_groups=mesh['space'=16,'tm'=8] {'space','tm'}, dimensions={0} | all-to-all | bytes 786432 | tf_op jit(solution)/shard_map/all_to_all | solution.py:484
  51.7 0.0 copy-done.3
  51.7 3.3 %adjoint.1 = (bf16[256,512]{1,0:T(8,128)(2,1)S(1)}, f32[24,512]{1,0:T(8,128)S(1)}, f32[16,512]{1,0:T(8,128)S(1)}) custom-call(s32[1]{0:T(128)} %bitcast.tm_ref, s32[1]{0:T(128)S(6)} %copy.10.count_ref, s32[3,512]{1,0:T(4,128)S(1)} %copy-done.3, bf16[128,4,384]{2,1,0:T(4,128)(2,1)S(1)} %all_to_all.11.misfit_ref, ...), custom_call_target="tpu_custom_call" | custom-call | tf_op jit(solution)/shard_map/adjoint/pallas_call | solution.py:290
  55.0 1.0 %collective-permute-start.4 = (bf16[256,512]{1,0:T(8,128)(2,1)S(1)}, bf16[256,512]{1,0:T(8,128)(2,1)S(1)}, u32[]{:S(2)}, u32[]{:S(2)}) collective-permute-start(bf16[256,512]{1,0:T(8,128)(2,1)S(1)} %get-tuple-element.26.refs_0_), channel_id=1, source_target_pairs={{0,4},{1,5},{2,6},{3,7},{4,0},{5,1},{6,2},{7,3},{8,12},{9,13},{10,... | collective-permute-start | bytes 786440 | tf_op jit(solution)/shard_map/ppermute | solution.py:490
  56.0 1.1 %collective-permute-start.5 = (bf16[256,512]{1,0:T(8,128)(2,1)S(1)}, bf16[256,512]{1,0:T(8,128)(2,1)S(1)}, u32[]{:S(2)}, u32[]{:S(2)}) collective-permute-start(bf16[256,512]{1,0:T(8,128)(2,1)S(1)} %get-tuple-element.26.refs_0_), channel_id=1, source_target_pairs={{0,6},{1,7},{2,0},{3,1},{4,2},{5,3},{6,4},{7,5},{8,14},{9,15},{10,... | collective-permute-start | bytes 786440 | tf_op jit(solution)/shard_map/ppermute | solution.py:490
  57.1 1.0 %collective-permute-start.1 = (f32[16,512]{1,0:T(8,128)S(1)}, f32[16,512]{1,0:T(8,128)S(1)}, u32[]{:S(2)}, u32[]{:S(2)}) collective-permute-start(f32[16,512]{1,0:T(8,128)S(1)} %get-tuple-element.21), channel_id=1, source_target_pairs={{0,1},{1,0},{2,3},{3,2},{4,5},{5,4},{6,7},{7,6},{8,9},{9,8},{10,11... | collective-permute-start | bytes 98312 | tf_op jit(solution)/shard_map/ppermute | solution.py:492
  58.2 0.2 collective-permute-start.2
  58.4 0.6 collective-permute-done.1
  59.0 4.3 %collective-permute-start.3 = (f32[40,512]{1,0:T(8,128)S(1)}, f32[40,512]{1,0:T(8,128)S(1)}, u32[]{:S(2)}, u32[]{:S(2)}) collective-permute-start(f32[40,512]{1,0:T(8,128)S(1)} %pad_maximum_fusion), channel_id=1, source_target_pairs={{0,8},{9,1},{2,10},{11,3},{4,12},{13,5},{6,14},{15,7},{8,16},{17,9... | collective-permute-start | bytes 245768 | tf_op jit(solution)/shard_map/ppermute | solution.py:500
  63.3 1.5 %collective-permute-done.3.refs_8_ = f32[40,512]{1,0:T(8,128)S(1)} collective-permute-done((f32[40,512]{1,0:T(8,128)S(1)}, f32[40,512]{1,0:T(8,128)S(1)}, u32[]{:S(2)}, u32[]{:S(2)}) %collective-permute-start.3) | collective-permute-done | bytes 81952 | tf_op jit(solution)/shard_map/ppermute | solution.py:500
  64.8 2.0 %collective-permute-start.7 = (bf16[32,512]{1,0:T(8,128)(2,1)S(1)}, bf16[32,512]{1,0:T(8,128)(2,1)S(1)}, u32[]{:S(2)}, u32[]{:S(2)}) collective-permute-start(bf16[32,512]{1,0:T(8,128)(2,1)S(1)} %slice.7.refs_4_), channel_id=1, source_target_pairs={{0,4},{1,5},{2,6},{3,7},{4,0},{5,1},{6,2},{7,3},{8,12},{9,13},{10,... | collective-permute-start | bytes 98312 | tf_op jit(solution)/shard_map/ppermute | solution.py:490
  66.8 0.5 collective-permute-start.6
  67.2 0.0 collective-permute-done.4.refs_2_
  67.2 2.2 %collective-permute-start.8 = (bf16[32,512]{1,0:T(8,128)(2,1)S(1)}, bf16[32,512]{1,0:T(8,128)(2,1)S(1)}, u32[]{:S(2)}, u32[]{:S(2)}) collective-permute-start(bf16[32,512]{1,0:T(8,128)(2,1)S(1)} %slice.7.refs_4_), channel_id=1, source_target_pairs={{0,6},{1,7},{2,0},{3,1},{4,2},{5,3},{6,4},{7,5},{8,14},{9,15},{10,... | collective-permute-start | bytes 98312 | tf_op jit(solution)/shard_map/ppermute | solution.py:490
  69.5 0.0 copy-done.4
  69.5 0.4 weights.1
  69.9 0.0 collective-permute-done.7.refs_6_
  69.9 1.1 %collective-permute-done.6.refs_5_ = bf16[32,512]{1,0:T(8,128)(2,1)S(1)} collective-permute-done((bf16[32,512]{1,0:T(8,128)(2,1)S(1)}, bf16[32,512]{1,0:T(8,128)(2,1)S(1)}, u32[]{:S(2)}, u32[]{:S(2)}) %collective-permute-start.6) | collective-permute-done | bytes 32800 | tf_op jit(solution)/shard_map/ppermute | solution.py:490
  70.9 0.0 collective-permute-done.5.refs_3_
  70.9 0.0 collective-permute-done.2.refs_1_
  70.9 0.0 collective-permute-done.8.refs_7_
  71.0 0.3 mix_twin.1
  71.3 4.6 %collective-permute-start.9 = (f32[4,72,512]{2,1,0:T(8,128)S(1)}, f32[4,72,512]{2,1,0:T(8,128)S(1)}, u32[]{:S(2)}, u32[]{:S(2)}) collective-permute-start(f32[4,72,512]{2,1,0:T(8,128)S(1)} %mix_twin.1), channel_id=1, source_target_pairs={{0,1},{1,0},{2,3},{3,2},{4,5},{5,4},{6,7},{7,6},{8,9},{9,8},{10,11... | collective-permute-start | bytes 1769480 | tf_op jit(solution)/shard_map/ppermute | solution.py:506
  75.8 0.3 mix_own.1.own_ref
  76.1 1.3 %collective-permute-done.9.twin_ref = f32[4,72,512]{2,1,0:T(8,128)S(1)} collective-permute-done((f32[4,72,512]{2,1,0:T(8,128)S(1)}, f32[4,72,512]{2,1,0:T(8,128)S(1)}, u32[]{:S(2)}, u32[]{:S(2)}) %collective-permute-start.9) | collective-permute-done | bytes 589856 | tf_op jit(solution)/shard_map/ppermute | solution.py:506
  77.5 2.5 %diffuse.1 = f32[4,64,512]{2,1,0:T(8,128)} custom-call(s32[1]{0:T(128)} %bitcast.tm_ref, f32[4,72,512]{2,1,0:T(8,128)S(1)} %mix_own.1.own_ref, f32[4,72,512]{2,1,0:T(8,128)S(1)} %collective-permute-done.9.twin_ref, f32[64,512]{1,0:T(8,128)S(1)} %copy-done), custom_call_target="tpu_custom_call" | custom-call | tf_op jit(solution)/shard_map/diffuse/pallas_call | solution.py:455
  (10 shorter events, 0.0 us)
Async XLA Ops:
  0.6 51.1 %copy-start.3 = (s32[3,512]{1,0:T(4,128)S(1)}, s32[3,512]{1,0:T(4,128)}, u32[]{:S(2)}) copy-start(s32[3,512]{1,0:T(4,128)} %coords_ref.1) | copy-start | bytes 18436
  0.6 33.0 %copy-start.1 = (f32[12288]{0:T(1024)S(1)}, f32[12288]{0:T(1024)}, u32[]{:S(2)}) copy-start(f32[12288]{0:T(1024)} %param.13) | copy-start | bytes 147460
  0.7 33.0 %copy-start.2 = (f32[12288]{0:T(1024)S(1)}, f32[12288]{0:T(1024)}, u32[]{:S(2)}) copy-start(f32[12288]{0:T(1024)} %param.12) | copy-start | bytes 147460
  0.7 51.0 %copy-start = (f32[64,512]{1,0:T(8,128)S(1)}, f32[64,512]{1,0:T(8,128)}, u32[]{:S(2)}) copy-start(f32[64,512]{1,0:T(8,128)} %diff_ref.3) | copy-start | bytes 393220
  1.4 68.1 %copy-start.4 = (f32[32,32]{1,0:T(8,128)S(1)}, f32[32,32]{1,0:T(8,128)}, u32[]{:S(2)}) copy-start(f32[32,32]{1,0:T(8,128)} %cov_ref) | copy-start | bytes 12292
  10.4 2.1 %collective-permute-start = (f32[64,4,384]{2,1,0:T(4,128)S(1)}, f32[64,4,384]{2,1,0:T(4,128)S(1)}, u32[]{:S(2)}, u32[]{:S(2)}) collective-permute-start(f32[64,4,384]{2,1,0:T(4,128)S(1)} %get-tuple-element.17), channel_id=1, source_target_pairs={{0,1},{1,0},{2,3},{3,2},{4,5},{5,4},{6,7},{7,6},{8,9},{9,8},{10,11... | collective-permute-start | bytes 1179656 | tf_op jit(solution)/shard_map/ppermute | solution.py:481
  55.0 12.2 %collective-permute-start.4 = (bf16[256,512]{1,0:T(8,128)(2,1)S(1)}, bf16[256,512]{1,0:T(8,128)(2,1)S(1)}, u32[]{:S(2)}, u32[]{:S(2)}) collective-permute-start(bf16[256,512]{1,0:T(8,128)(2,1)S(1)} %get-tuple-element.26.refs_0_), channel_id=1, source_target_pairs={{0,4},{1,5},{2,6},{3,7},{4,0},{5,1},{6,2},{7,3},{8,12},{9,13},{10,... | collective-permute-start | bytes 786440 | tf_op jit(solution)/shard_map/ppermute | solution.py:490
  56.0 14.9 %collective-permute-start.5 = (bf16[256,512]{1,0:T(8,128)(2,1)S(1)}, bf16[256,512]{1,0:T(8,128)(2,1)S(1)}, u32[]{:S(2)}, u32[]{:S(2)}) collective-permute-start(bf16[256,512]{1,0:T(8,128)(2,1)S(1)} %get-tuple-element.26.refs_0_), channel_id=1, source_target_pairs={{0,6},{1,7},{2,0},{3,1},{4,2},{5,3},{6,4},{7,5},{8,14},{9,15},{10,... | collective-permute-start | bytes 786440 | tf_op jit(solution)/shard_map/ppermute | solution.py:490
  57.1 1.9 %collective-permute-start.1 = (f32[16,512]{1,0:T(8,128)S(1)}, f32[16,512]{1,0:T(8,128)S(1)}, u32[]{:S(2)}, u32[]{:S(2)}) collective-permute-start(f32[16,512]{1,0:T(8,128)S(1)} %get-tuple-element.21), channel_id=1, source_target_pairs={{0,1},{1,0},{2,3},{3,2},{4,5},{5,4},{6,7},{7,6},{8,9},{9,8},{10,11... | collective-permute-start | bytes 98312 | tf_op jit(solution)/shard_map/ppermute | solution.py:492
  58.2 12.8 %collective-permute-start.2 = (bf16[256,512]{1,0:T(8,128)(2,1)S(1)}, bf16[256,512]{1,0:T(8,128)(2,1)S(1)}, u32[]{:S(2)}, u32[]{:S(2)}) collective-permute-start(bf16[256,512]{1,0:T(8,128)(2,1)S(1)} %get-tuple-element.26.refs_0_), channel_id=1, source_target_pairs={{0,2},{1,3},{2,4},{3,5},{4,6},{5,7},{6,0},{7,1},{8,10},{9,11},{10,... | collective-permute-start | bytes 786440 | tf_op jit(solution)/shard_map/ppermute | solution.py:490
  59.0 5.8 %collective-permute-start.3 = (f32[40,512]{1,0:T(8,128)S(1)}, f32[40,512]{1,0:T(8,128)S(1)}, u32[]{:S(2)}, u32[]{:S(2)}) collective-permute-start(f32[40,512]{1,0:T(8,128)S(1)} %pad_maximum_fusion), channel_id=1, source_target_pairs={{0,8},{9,1},{2,10},{11,3},{4,12},{13,5},{6,14},{15,7},{8,16},{17,9... | collective-permute-start | bytes 245768 | tf_op jit(solution)/shard_map/ppermute | solution.py:500
  64.8 5.1 %collective-permute-start.7 = (bf16[32,512]{1,0:T(8,128)(2,1)S(1)}, bf16[32,512]{1,0:T(8,128)(2,1)S(1)}, u32[]{:S(2)}, u32[]{:S(2)}) collective-permute-start(bf16[32,512]{1,0:T(8,128)(2,1)S(1)} %slice.7.refs_4_), channel_id=1, source_target_pairs={{0,4},{1,5},{2,6},{3,7},{4,0},{5,1},{6,2},{7,3},{8,12},{9,13},{10,... | collective-permute-start | bytes 98312 | tf_op jit(solution)/shard_map/ppermute | solution.py:490
  66.8 4.2 %collective-permute-start.6 = (bf16[32,512]{1,0:T(8,128)(2,1)S(1)}, bf16[32,512]{1,0:T(8,128)(2,1)S(1)}, u32[]{:S(2)}, u32[]{:S(2)}) collective-permute-start(bf16[32,512]{1,0:T(8,128)(2,1)S(1)} %slice.7.refs_4_), channel_id=1, source_target_pairs={{0,2},{1,3},{2,4},{3,5},{4,6},{5,7},{6,0},{7,1},{8,10},{9,11},{10,... | collective-permute-start | bytes 98312 | tf_op jit(solution)/shard_map/ppermute | solution.py:490
  67.2 3.7 %collective-permute-start.8 = (bf16[32,512]{1,0:T(8,128)(2,1)S(1)}, bf16[32,512]{1,0:T(8,128)(2,1)S(1)}, u32[]{:S(2)}, u32[]{:S(2)}) collective-permute-start(bf16[32,512]{1,0:T(8,128)(2,1)S(1)} %slice.7.refs_4_), channel_id=1, source_target_pairs={{0,6},{1,7},{2,0},{3,1},{4,2},{5,3},{6,4},{7,5},{8,14},{9,15},{10,... | collective-permute-start | bytes 98312 | tf_op jit(solution)/shard_map/ppermute | solution.py:490
  71.3 6.2 %collective-permute-start.9 = (f32[4,72,512]{2,1,0:T(8,128)S(1)}, f32[4,72,512]{2,1,0:T(8,128)S(1)}, u32[]{:S(2)}, u32[]{:S(2)}) collective-permute-start(f32[4,72,512]{2,1,0:T(8,128)S(1)} %mix_twin.1), channel_id=1, source_target_pairs={{0,1},{1,0},{2,3},{3,2},{4,5},{5,4},{6,7},{7,6},{8,9},{9,8},{10,11... | collective-permute-start | bytes 1769480 | tf_op jit(solution)/shard_map/ppermute | solution.py:506

commit v8 on v7

--- a/solution.py
+++ b/solution.py
@@ -269,15 +269,22 @@
         full = dot(pick, spread[...])
         summed = full[:, :LANES] + full[:, LANES:]
         main_ref[:, cut] = summed.astype(bf16)
-        for t in range(time_dev):
-            row, at = t * tile_rows, t * SWEEPS
-            down = summed[row + tile_rows - SWEEPS : row + tile_rows]
-            up = summed[row : row + SWEEPS]
-            mine_ref[at : at + SWEEPS, cut] = jnp.where(first_core, down, up)
-            other_ref[at : at + SWEEPS, cut] = jnp.where(first_core, up, down)
-    mine_ref[time_dev * SWEEPS :, :] = jnp.where(
-        first_core, diff_ref[tile_rows - EDGE :, :], diff_ref[:EDGE, :]
-    )
+        up, down = (
+            jnp.concatenate(
+                [summed[n * tile_rows + at : n * tile_rows + at + SWEEPS] for n in range(time_dev)],
+                axis=0,
+            )
+            for at in (0, tile_rows - SWEEPS)
+        )
+        mine_ref[: time_dev * SWEEPS, cut] = jnp.where(first_core, down, up).astype(bf16)
+        other_ref[:, cut] = jnp.where(first_core, up, down).astype(bf16)
+    edge = jnp.where(first_core, diff_ref[tile_rows - EDGE :, :], diff_ref[:EDGE, :])
+    high, rest = split2(edge)
+    low = edge - high.astype(f32) - rest.astype(f32)
+    parts = jnp.concatenate(
+        [high.astype(f32), rest.astype(f32), low, jnp.zeros_like(low)], axis=0
+    )
+    mine_ref[time_dev * SWEEPS :, :] = parts.astype(bf16)
 
 
 def adjoint_of(tm, count, coords, misfit_rows, footprints, diffusivity, time_dev):
@@ -291,8 +298,8 @@
         adjoint_kernel,
         out_shape=(
             jax.ShapeDtypeStruct((time_dev * tile_rows, width), bf16),
-            jax.ShapeDtypeStruct((edge + EDGE, width), f32),
-            jax.ShapeDtypeStruct((edge, width), f32),
+            jax.ShapeDtypeStruct((edge + 4 * EDGE, width), bf16),
+            jax.ShapeDtypeStruct((edge, width), bf16),
         ),
         in_specs=[smem, smem, vmem, vmem, vmem, vmem],
         out_specs=(vmem, vmem, vmem),
@@ -379,10 +386,11 @@
         put(dot(wide, jnp.concatenate(pieces, axis=0).astype(bf16)), r, EDGE)
     edges = jnp.concatenate([halo[...] for halo in halos], axis=0)
     put(dot(halo_weight_ref[int(twin)], edges), tile_rows, SWEEPS)
-    base = 2 * time_dev * SWEEPS
+    parts = received_ref[2 * time_dev * SWEEPS :, :].astype(f32)
+    diff = parts[:EDGE] + parts[EDGE : 2 * EDGE] + parts[2 * EDGE : 3 * EDGE]
     for t in range(time_dev):
-        n = base + (t % 2) * SWEEPS
-        out_ref[t, tile_rows + SWEEPS :, :] = received_ref[n : n + SWEEPS, :]
+        n = (t % 2) * SWEEPS
+        out_ref[t, tile_rows + SWEEPS :, :] = diff[n : n + SWEEPS]
 
 
 def mix(twin, wide, mains, halos, received, shape):
@@ -499,7 +507,7 @@
     mains = [main] + [along(main, k) for k in (1, 2, 3)]
     received = lax.ppermute(payload, both, moves)
     wide = weights(tm, cov, time_dev)
-    halo = received[: 2 * time_dev * SWEEPS].astype(bf16)
+    halo = received[: 2 * time_dev * SWEEPS]
     last, mains[2] = lax.optimization_barrier((halo, mains[2]))
     halos = [halo, along(halo, 1), along(halo, 2), along(last, 3)]
     held = (wide, mains, halos, received, fluxes.shape)

time: 80.3 us -> 81.2 us (1.011)
  starting transfers between devices: 17.6 us -> 18.8 us
where the time goes in v8:
time: 81.2 us; the launch traced here: 81 us
  blocking collectives  38.3 us (47%)
  starting transfers between devices  18.8 us (23%)
  Pallas kernels  16.6 us (20%)
  waiting for transfers between devices  5.69 us (7%)
  between operations  1.56 us (2%)
    all_to_all x1, blocking collectives, body(): lax.all_to_all(sums, both, 0, 0, axis_index_groups=parity, tiled=True)  21 us
    all_to_all x1, blocking collectives, body(): halves = lax.all_to_all(halves, both, 0, 0, tiled=True)  17.3 us
    pallas_call x1, Pallas kernels, forward(): pl.pallas_call(forward_kernel, out_shape=(pltpu.VMEM((devices // 2, 4, co...  9.06 us
    ppermute x6, starting transfers between devices, along(): lax.ppermute(array, 'tm', [(i, (i + 2 * steps) % n_tm) for i in range(n_t...  7.68 us
    ppermute x1, starting transfers between devices, body(): twin = lax.ppermute(mix(True, *held), 'tm', swap)  4.82 us
    ppermute x1, starting transfers between devices, body(): received = lax.ppermute(payload, both, moves)  4.3 us
    pallas_call x1, Pallas kernels, adjoint_of(): pl.pallas_call(adjoint_kernel, out_shape=(jax.ShapeDtypeStruct((time_dev...  3.3 us
    pallas_call x1, Pallas kernels, diffuse(): pl.pallas_call(diffuse_kernel, out_shape=jax.ShapeDtypeStruct(shape, f32)...  2.45 us
  transfers between devices with their start and end apart: 10, of which 5 were waited for; matrix products, arithmetic and copies ran while one was open for 0% of the time, Pallas kernels for 1%

profile of v8, /device:TPU:3, one launch (start us, length us, event | category | flops | bytes accessed | tf_op | source)
XLA Modules:
  0.0 81.0 jit_solution(16600193500798296792)
XLA Ops:
  0.6 0.0 copy-start.3
  1.4 9.1 %forward.1 = (f32[64,4,384]{2,1,0:T(4,128)S(1)}, f32[64,4,384]{2,1,0:T(4,128)S(1)}, bf16[512,128,128]{2,1,0:T(8,128)(2,1)S(1)}) custom-call(s32[1]{0:T(128)} %bitcast.tm_ref, s32[1]{0:T(128)S(6)} %copy.10.count_ref, s32[3,512]{1,0:T(4,128)} %coords_ref.1, bf16[4,64,512]{2,1,0:T(8,128)(2,1)} %flux_hbm.1, bf16[512,128,128]{2,1,0:T(8,128)(2,1)} %foot_ref.1), custom_call_target="tpu_custom_call" | custom-call | tf_op jit(solution)/shard_map/forward/pallas_call | solution.py:148
  10.4 0.8 collective-permute-start
  11.2 1.3 %collective-permute-done = f32[64,4,384]{2,1,0:T(4,128)S(1)} collective-permute-done((f32[64,4,384]{2,1,0:T(4,128)S(1)}, f32[64,4,384]{2,1,0:T(4,128)S(1)}, u32[]{:S(2)}, u32[]{:S(2)}) %collective-permute-start) | collective-permute-done | bytes 393248 | tf_op jit(solution)/shard_map/ppermute | solution.py:489
  12.5 0.1 add.3
  12.6 21.0 %all_to_all.10.sums_ref = f32[64,4,384]{2,1,0:T(4,128)S(1)} all-to-all(f32[64,4,384]{2,1,0:T(4,128)S(1)} %add.3), channel_id=1, replica_groups={{0,2,4,6,8,10,12,14,16,18,20,22,24,26,28,30,32,34,36,38,40,42,44,46,48,..., dimensions={0} | all-to-all | bytes 786432 | tf_op jit(solution)/shard_map/all_to_all | solution.py:490
  33.7 0.7 misfit.1
  34.4 17.3 %all_to_all.11.misfit_ref = bf16[128,4,384]{2,1,0:T(4,128)(2,1)S(1)} all-to-all(bf16[128,4,384]{2,1,0:T(4,128)(2,1)S(1)} %get-tuple-element.19), channel_id=1, replica_groups=mesh['space'=16,'tm'=8] {'space','tm'}, dimensions={0} | all-to-all | bytes 786432 | tf_op jit(solution)/shard_map/all_to_all | solution.py:492
  51.7 0.0 copy-done.3
  51.7 3.3 %adjoint.1 = (bf16[256,512]{1,0:T(8,128)(2,1)S(1)}, bf16[48,512]{1,0:T(8,128)(2,1)S(1)}, bf16[16,512]{1,0:T(8,128)(2,1)S(1)}) custom-call(s32[1]{0:T(128)} %bitcast.tm_ref, s32[1]{0:T(128)S(6)} %copy.10.count_ref, s32[3,512]{1,0:T(4,128)S(1)} %copy-done.3, bf16[128,4,384]{2,1,0:T(4,128)(2,1)S(1)} %all_to_all.11.misfit_ref, ...), custom_call_target="tpu_custom_call" | custom-call | tf_op jit(solution)/shard_map/adjoint/pallas_call | solution.py:297
  55.0 1.0 %collective-permute-start.4 = (bf16[256,512]{1,0:T(8,128)(2,1)S(1)}, bf16[256,512]{1,0:T(8,128)(2,1)S(1)}, u32[]{:S(2)}, u32[]{:S(2)}) collective-permute-start(bf16[256,512]{1,0:T(8,128)(2,1)S(1)} %get-tuple-element.26.refs_0_), channel_id=1, source_target_pairs={{0,4},{1,5},{2,6},{3,7},{4,0},{5,1},{6,2},{7,3},{8,12},{9,13},{10,... | collective-permute-start | bytes 786440 | tf_op jit(solution)/shard_map/ppermute | solution.py:498
  56.0 1.2 %collective-permute-start.5 = (bf16[256,512]{1,0:T(8,128)(2,1)S(1)}, bf16[256,512]{1,0:T(8,128)(2,1)S(1)}, u32[]{:S(2)}, u32[]{:S(2)}) collective-permute-start(bf16[256,512]{1,0:T(8,128)(2,1)S(1)} %get-tuple-element.26.refs_0_), channel_id=1, source_target_pairs={{0,6},{1,7},{2,0},{3,1},{4,2},{5,3},{6,4},{7,5},{8,14},{9,15},{10,... | collective-permute-start | bytes 786440 | tf_op jit(solution)/shard_map/ppermute | solution.py:498
  57.2 0.3 collective-permute-start.2
  57.5 1.2 %collective-permute-start.1 = (bf16[16,512]{1,0:T(8,128)(2,1)S(1)}, bf16[16,512]{1,0:T(8,128)(2,1)S(1)}, u32[]{:S(2)}, u32[]{:S(2)}) collective-permute-start(bf16[16,512]{1,0:T(8,128)(2,1)S(1)} %get-tuple-element.21), channel_id=1, source_target_pairs={{0,1},{1,0},{2,3},{3,2},{4,5},{5,4},{6,7},{7,6},{8,9},{9,8},{10,11... | collective-permute-start | bytes 49160 | tf_op jit(solution)/shard_map/ppermute | solution.py:500
  58.7 0.8 %collective-permute-done.1 = bf16[16,512]{1,0:T(8,128)(2,1)S(1)} collective-permute-done((bf16[16,512]{1,0:T(8,128)(2,1)S(1)}, bf16[16,512]{1,0:T(8,128)(2,1)S(1)}, u32[]{:S(2)}, u32[]{:S(2)}) %collective-permute-start.1) | collective-permute-done | bytes 16416 | tf_op jit(solution)/shard_map/ppermute | solution.py:500
  59.5 4.3 %collective-permute-start.3 = (bf16[64,512]{1,0:T(8,128)(2,1)S(1)}, bf16[64,512]{1,0:T(8,128)(2,1)S(1)}, u32[]{:S(2)}, u32[]{:S(2)}) collective-permute-start(bf16[64,512]{1,0:T(8,128)(2,1)S(1)} %pad_maximum_fusion), channel_id=1, source_target_pairs={{0,8},{9,1},{2,10},{11,3},{4,12},{13,5},{6,14},{15,7},{8,16},{17,9... | collective-permute-start | bytes 196616 | tf_op jit(solution)/shard_map/ppermute | solution.py:508
  63.8 1.3 %collective-permute-done.3.refs_8_ = bf16[64,512]{1,0:T(8,128)(2,1)S(1)} collective-permute-done((bf16[64,512]{1,0:T(8,128)(2,1)S(1)}, bf16[64,512]{1,0:T(8,128)(2,1)S(1)}, u32[]{:S(2)}, u32[]{:S(2)}) %collective-permute-start.3) | collective-permute-done | bytes 65568 | tf_op jit(solution)/shard_map/ppermute | solution.py:508
  65.1 2.5 %collective-permute-start.7 = (bf16[32,512]{1,0:T(8,128)(2,1)S(1)}, bf16[32,512]{1,0:T(8,128)(2,1)S(1)}, u32[]{:S(2)}, u32[]{:S(2)}) collective-permute-start(bf16[32,512]{1,0:T(8,128)(2,1)S(1)} %slice.4.refs_4_), channel_id=1, source_target_pairs={{0,4},{1,5},{2,6},{3,7},{4,0},{5,1},{6,2},{7,3},{8,12},{9,13},{10,... | collective-permute-start | bytes 98312 | tf_op jit(solution)/shard_map/ppermute | solution.py:498
  67.7 0.5 collective-permute-start.6
  68.2 0.0 collective-permute-done.4.refs_2_
  68.2 2.2 %collective-permute-start.8 = (bf16[32,512]{1,0:T(8,128)(2,1)S(1)}, bf16[32,512]{1,0:T(8,128)(2,1)S(1)}, u32[]{:S(2)}, u32[]{:S(2)}) collective-permute-start(bf16[32,512]{1,0:T(8,128)(2,1)S(1)} %slice.4.refs_4_), channel_id=1, source_target_pairs={{0,6},{1,7},{2,0},{3,1},{4,2},{5,3},{6,4},{7,5},{8,14},{9,15},{10,... | collective-permute-start | bytes 98312 | tf_op jit(solution)/shard_map/ppermute | solution.py:498
  70.4 0.4 weights.1
  70.8 0.0 collective-permute-done.7.refs_6_
  70.8 0.9 %collective-permute-done.6.refs_5_ = bf16[32,512]{1,0:T(8,128)(2,1)S(1)} collective-permute-done((bf16[32,512]{1,0:T(8,128)(2,1)S(1)}, bf16[32,512]{1,0:T(8,128)(2,1)S(1)}, u32[]{:S(2)}, u32[]{:S(2)}) %collective-permute-start.6) | collective-permute-done | bytes 32800 | tf_op jit(solution)/shard_map/ppermute | solution.py:498
  71.7 0.0 collective-permute-done.5.refs_3_
  71.7 0.0 collective-permute-done.2.refs_1_
  71.7 0.0 collective-permute-done.8.refs_7_
  71.7 0.3 mix_twin.1
  72.0 4.8 %collective-permute-start.9 = (f32[4,72,512]{2,1,0:T(8,128)S(1)}, f32[4,72,512]{2,1,0:T(8,128)S(1)}, u32[]{:S(2)}, u32[]{:S(2)}) collective-permute-start(f32[4,72,512]{2,1,0:T(8,128)S(1)} %mix_twin.1), channel_id=1, source_target_pairs={{0,1},{1,0},{2,3},{3,2},{4,5},{5,4},{6,7},{7,6},{8,9},{9,8},{10,11... | collective-permute-start | bytes 1769480 | tf_op jit(solution)/shard_map/ppermute | solution.py:514
  76.8 0.3 mix_own.1.own_ref
  77.1 1.3 %collective-permute-done.9.twin_ref = f32[4,72,512]{2,1,0:T(8,128)S(1)} collective-permute-done((f32[4,72,512]{2,1,0:T(8,128)S(1)}, f32[4,72,512]{2,1,0:T(8,128)S(1)}, u32[]{:S(2)}, u32[]{:S(2)}) %collective-permute-start.9) | collective-permute-done | bytes 589856 | tf_op jit(solution)/shard_map/ppermute | solution.py:514
  78.4 2.5 %diffuse.1 = f32[4,64,512]{2,1,0:T(8,128)} custom-call(s32[1]{0:T(128)} %bitcast.tm_ref, f32[4,72,512]{2,1,0:T(8,128)S(1)} %mix_own.1.own_ref, f32[4,72,512]{2,1,0:T(8,128)S(1)} %collective-permute-done.9.twin_ref, f32[64,512]{1,0:T(8,128)S(1)} %copy-done), custom_call_target="tpu_custom_call" | custom-call | tf_op jit(solution)/shard_map/diffuse/pallas_call | solution.py:463
  (10 shorter events, 0.0 us)
Async XLA Ops:
  0.6 51.1 %copy-start.3 = (s32[3,512]{1,0:T(4,128)S(1)}, s32[3,512]{1,0:T(4,128)}, u32[]{:S(2)}) copy-start(s32[3,512]{1,0:T(4,128)} %coords_ref.1) | copy-start | bytes 18436
  0.6 33.0 %copy-start.1 = (f32[12288]{0:T(1024)S(1)}, f32[12288]{0:T(1024)}, u32[]{:S(2)}) copy-start(f32[12288]{0:T(1024)} %param.13) | copy-start | bytes 147460
  0.7 33.0 %copy-start.2 = (f32[12288]{0:T(1024)S(1)}, f32[12288]{0:T(1024)}, u32[]{:S(2)}) copy-start(f32[12288]{0:T(1024)} %param.12) | copy-start | bytes 147460
  0.7 51.0 %copy-start = (f32[64,512]{1,0:T(8,128)S(1)}, f32[64,512]{1,0:T(8,128)}, u32[]{:S(2)}) copy-start(f32[64,512]{1,0:T(8,128)} %diff_ref.3) | copy-start | bytes 393220
  1.4 69.0 %copy-start.4 = (f32[32,32]{1,0:T(8,128)S(1)}, f32[32,32]{1,0:T(8,128)}, u32[]{:S(2)}) copy-start(f32[32,32]{1,0:T(8,128)} %cov_ref) | copy-start | bytes 12292
  10.4 2.1 %collective-permute-start = (f32[64,4,384]{2,1,0:T(4,128)S(1)}, f32[64,4,384]{2,1,0:T(4,128)S(1)}, u32[]{:S(2)}, u32[]{:S(2)}) collective-permute-start(f32[64,4,384]{2,1,0:T(4,128)S(1)} %get-tuple-element.17), channel_id=1, source_target_pairs={{0,1},{1,0},{2,3},{3,2},{4,5},{5,4},{6,7},{7,6},{8,9},{9,8},{10,11... | collective-permute-start | bytes 1179656 | tf_op jit(solution)/shard_map/ppermute | solution.py:489
  55.0 13.2 %collective-permute-start.4 = (bf16[256,512]{1,0:T(8,128)(2,1)S(1)}, bf16[256,512]{1,0:T(8,128)(2,1)S(1)}, u32[]{:S(2)}, u32[]{:S(2)}) collective-permute-start(bf16[256,512]{1,0:T(8,128)(2,1)S(1)} %get-tuple-element.26.refs_0_), channel_id=1, source_target_pairs={{0,4},{1,5},{2,6},{3,7},{4,0},{5,1},{6,2},{7,3},{8,12},{9,13},{10,... | collective-permute-start | bytes 786440 | tf_op jit(solution)/shard_map/ppermute | solution.py:498
  56.0 15.7 %collective-permute-start.5 = (bf16[256,512]{1,0:T(8,128)(2,1)S(1)}, bf16[256,512]{1,0:T(8,128)(2,1)S(1)}, u32[]{:S(2)}, u32[]{:S(2)}) collective-permute-start(bf16[256,512]{1,0:T(8,128)(2,1)S(1)} %get-tuple-element.26.refs_0_), channel_id=1, source_target_pairs={{0,6},{1,7},{2,0},{3,1},{4,2},{5,3},{6,4},{7,5},{8,14},{9,15},{10,... | collective-permute-start | bytes 786440 | tf_op jit(solution)/shard_map/ppermute | solution.py:498
  57.2 14.5 %collective-permute-start.2 = (bf16[256,512]{1,0:T(8,128)(2,1)S(1)}, bf16[256,512]{1,0:T(8,128)(2,1)S(1)}, u32[]{:S(2)}, u32[]{:S(2)}) collective-permute-start(bf16[256,512]{1,0:T(8,128)(2,1)S(1)} %get-tuple-element.26.refs_0_), channel_id=1, source_target_pairs={{0,2},{1,3},{2,4},{3,5},{4,6},{5,7},{6,0},{7,1},{8,10},{9,11},{10,... | collective-permute-start | bytes 786440 | tf_op jit(solution)/shard_map/ppermute | solution.py:498
  57.5 2.0 %collective-permute-start.1 = (bf16[16,512]{1,0:T(8,128)(2,1)S(1)}, bf16[16,512]{1,0:T(8,128)(2,1)S(1)}, u32[]{:S(2)}, u32[]{:S(2)}) collective-permute-start(bf16[16,512]{1,0:T(8,128)(2,1)S(1)} %get-tuple-element.21), channel_id=1, source_target_pairs={{0,1},{1,0},{2,3},{3,2},{4,5},{5,4},{6,7},{7,6},{8,9},{9,8},{10,11... | collective-permute-start | bytes 49160 | tf_op jit(solution)/shard_map/ppermute | solution.py:500
  59.5 5.6 %collective-permute-start.3 = (bf16[64,512]{1,0:T(8,128)(2,1)S(1)}, bf16[64,512]{1,0:T(8,128)(2,1)S(1)}, u32[]{:S(2)}, u32[]{:S(2)}) collective-permute-start(bf16[64,512]{1,0:T(8,128)(2,1)S(1)} %pad_maximum_fusion), channel_id=1, source_target_pairs={{0,8},{9,1},{2,10},{11,3},{4,12},{13,5},{6,14},{15,7},{8,16},{17,9... | collective-permute-start | bytes 196616 | tf_op jit(solution)/shard_map/ppermute | solution.py:508
  65.1 5.7 %collective-permute-start.7 = (bf16[32,512]{1,0:T(8,128)(2,1)S(1)}, bf16[32,512]{1,0:T(8,128)(2,1)S(1)}, u32[]{:S(2)}, u32[]{:S(2)}) collective-permute-start(bf16[32,512]{1,0:T(8,128)(2,1)S(1)} %slice.4.refs_4_), channel_id=1, source_target_pairs={{0,4},{1,5},{2,6},{3,7},{4,0},{5,1},{6,2},{7,3},{8,12},{9,13},{10,... | collective-permute-start | bytes 98312 | tf_op jit(solution)/shard_map/ppermute | solution.py:498
  67.7 4.0 %collective-permute-start.6 = (bf16[32,512]{1,0:T(8,128)(2,1)S(1)}, bf16[32,512]{1,0:T(8,128)(2,1)S(1)}, u32[]{:S(2)}, u32[]{:S(2)}) collective-permute-start(bf16[32,512]{1,0:T(8,128)(2,1)S(1)} %slice.4.refs_4_), channel_id=1, source_target_pairs={{0,2},{1,3},{2,4},{3,5},{4,6},{5,7},{6,0},{7,1},{8,10},{9,11},{10,... | collective-permute-start | bytes 98312 | tf_op jit(solution)/shard_map/ppermute | solution.py:498
  68.2 3.5 %collective-permute-start.8 = (bf16[32,512]{1,0:T(8,128)(2,1)S(1)}, bf16[32,512]{1,0:T(8,128)(2,1)S(1)}, u32[]{:S(2)}, u32[]{:S(2)}) collective-permute-start(bf16[32,512]{1,0:T(8,128)(2,1)S(1)} %slice.4.refs_4_), channel_id=1, source_target_pairs={{0,6},{1,7},{2,0},{3,1},{4,2},{5,3},{6,4},{7,5},{8,14},{9,15},{10,... | collective-permute-start | bytes 98312 | tf_op jit(solution)/shard_map/ppermute | solution.py:498
  72.0 6.4 %collective-permute-start.9 = (f32[4,72,512]{2,1,0:T(8,128)S(1)}, f32[4,72,512]{2,1,0:T(8,128)S(1)}, u32[]{:S(2)}, u32[]{:S(2)}) collective-permute-start(f32[4,72,512]{2,1,0:T(8,128)S(1)} %mix_twin.1), channel_id=1, source_target_pairs={{0,1},{1,0},{2,3},{3,2},{4,5},{5,4},{6,7},{7,6},{8,9},{9,8},{10,11... | collective-permute-start | bytes 1769480 | tf_op jit(solution)/shard_map/ppermute | solution.py:514
